TPU v7x, 32 devices: a whole 2x2x4 slice. The times are simulated.
32 devices in a mesh: lat: 8 (over z, x), lon: 4 (over y, core).
Axes of the slice: x: 2, y: 2, z: 4, core: 2. Of those that a mesh axis runs over, the one named last changes fastest.
Arguments:
- field_in: bfloat16 [80, 384, 512], P('lat', 'lon'), may hold values from -6 to 6
- kernel_taps: bfloat16 [3, 80, 3, 33], P(None, 'lat'), may hold values from -0.8984375 to 0.8984375
- row_reach: int32 [80], P('lat'), may hold values from 1 to 16, as said below
- mix_weight: bfloat16 [3, 512, 512], replicated, may hold values from -0.15625 to 0.15625
- up_weight: bfloat16 [512, 1024], replicated, may hold values from -0.25 to 0.25
- down_weight: bfloat16 [1024, 512], replicated, may hold values from -0.1875 to 0.1875
- cotangent: bfloat16 [80, 384, 512], P('lat', 'lon'), may hold values from -6 to 6
Outputs:
- block_out: bfloat16 [80, 384, 512], P('lat', 'lon')
- grad_field: bfloat16 [80, 384, 512], P('lat', 'lon')
- grad_mix: bfloat16 [3, 512, 512], replicated
- grad_up: bfloat16 [512, 1024], replicated
- grad_down: bfloat16 [1024, 512], replicated
Inputs may be any that keep to these rules, and one draw needn't show every extreme that they name: `row_reach`: how many longitude cells each latitude row's kernel reaches on either side.
All inputs are finite; a program needn't handle non-finite values.
Results may differ from a plain program's by a relative error of at most 0.0068.
Values may be sent and summed in bfloat16 or wider, within the bound.
No kernel may reach another device: no remote copies, remote signals or barrier semaphores. Data moves between devices by JAX's collectives and lax.ppermute only.
A program may use at most 128 MiB of HBM per device.

v0:
```python
import functools
import math

import jax
import jax.numpy as jnp
from jax import lax
from jax.experimental import pallas as pl
from jax.experimental.pallas import tpu as pltpu
from jax.sharding import PartitionSpec as P

inv_root_two = 0.7071067811865476
inv_root_tau = 0.3989422804014327
AXES = ("lat", "lon")


class Place:
    def __init__(self):
        self.lats = lax.axis_size("lat")
        self.lons = lax.axis_size("lon")
        self.count = self.lats * self.lons
        self.lat = lax.axis_index("lat")
        self.lon = lax.axis_index("lon")
        self.flat = self.lat * self.lons + self.lon
        lats, lons = self.lats, self.lons
        self.east = [(i, (i + 1) % lons) for i in range(lons)]
        self.west = [(j, i) for i, j in self.east]
        self.pairs = [
            (r * lons + c, (r ^ 1) * lons + c) for r in range(lats) for c in range(lons)
        ]
        self.bridges = []
        for r in range(lats):
            other = r - 1 if r % 2 == 0 else r + 1
            for c in range(lons):
                if 0 <= other < lats:
                    self.bridges.append((r * lons + c, other * lons + c))
                else:
                    self.bridges.append((r * lons + c, r * lons + (c + lons // 2) % lons))
        self.even = self.lat % 2 == 0


def route(place, mask_of):
    return [(i, i ^ mask_of(i)) for i in range(place.count)]


def send_along(place, block, mask_of):
    return lax.ppermute(block, AXES, route(place, mask_of))


def first_mask(i):
    return 2 if i % 2 == 0 else 4


def second_mask(i):
    return 4 if i % 2 == 0 else 2


def after(value, *others):
    return lax.optimization_barrier((value, *others))[0] if others else value


def near_mask(i):
    return 8


def pick(array, index):
    return lax.dynamic_index_in_dim(array, index, 0, keepdims=False)


def joined(bit, own, other):
    return jnp.concatenate([jnp.where(bit == 0, own, other), jnp.where(bit == 0, other, own)])


class Ring:
    def __init__(self, place):
        self.place = place
        self.core = place.flat % 2
        side_y, side_x = (place.flat // 2) % 2, (place.flat // 4) % 2
        self.first = jnp.where(self.core == 0, side_y, side_x)
        self.second = jnp.where(self.core == 0, side_x, side_y)
        self.near = (place.flat // 8) % 2

    def to_core(self, keep, send):
        got = send_along(self.place, send, lambda i: 1)
        return keep.astype(jnp.float32) + got.astype(jnp.float32)

    def leaving(self, buf, bit):
        return pick(buf, 1 - bit).astype(jnp.bfloat16)

    def step(self, buf, out, mask_of, bit, *ties):
        got = after(send_along(self.place, out, mask_of), *ties)
        return pick(buf, bit) + got.astype(jnp.float32)

    def far_step(self, own, scale, *ties):
        far = after(send_along(self.place, own, lambda i: 16), *ties)
        return ((own.astype(jnp.float32) + far.astype(jnp.float32)) * scale).astype(own.dtype)

    def gather_near(self, piece, *ties):
        piece = piece[None]
        return joined(self.near, piece, after(send_along(self.place, piece, near_mask), *ties))

    def gather_second(self, buf, *ties):
        return joined(self.second, buf, after(send_along(self.place, buf, second_mask), *ties))

    def gather_first(self, buf, *ties):
        return joined(self.first, buf, after(send_along(self.place, buf, first_mask), *ties))

    def gather_core(self, buf, *ties):
        return after(send_along(self.place, buf, lambda i: 1), *ties)


def halves(core, own, other, axis):
    size = own.shape[axis]
    shape = own.shape[:axis] + (2 * size,) + own.shape[axis + 1 :]
    out = jnp.zeros(shape, own.dtype)
    out = lax.dynamic_update_slice_in_dim(out, own, core * size, axis)
    return lax.dynamic_update_slice_in_dim(out, other, (1 - core) * size, axis)


OVER_ROWS = (((0,), (0,)), ((), ()))
OVER_LANES = (((1,), (1,)), ((), ()))
VMEM_LIMIT = 56 * 1024 * 1024


def dot(left, right, dims=(((1,), (0,)), ((), ()))):
    return lax.dot_general(left, right, dims, preferred_element_type=jnp.float32)


def tiles(count, size, body):
    def step(i, carry):
        body(pl.ds(pl.multiple_of(i * size, size), size))
        return carry

    lax.fori_loop(0, count // size, step, 0)


def band_kernel(reach_ref, taps, bands, lines, *, cols):
    basis, rows, _, count = taps.shape
    width = lines.shape[2]
    away = jnp.abs(lax.broadcasted_iota(jnp.int32, (3, count), 1) - (count - 1) // 2)
    lines[...] = jnp.zeros(lines.shape, lines.dtype)

    def one_row(r, carry):
        inside = away <= reach_ref[r]
        for k in range(basis):
            lines[k, :, :count] = jnp.where(inside, taps[k, r].astype(jnp.float32), 0.0)
            for d in range(3):
                line = jnp.broadcast_to(lines[k, pl.ds(d, 1)], (cols, width))
                band = pltpu.roll(line, 0, 1, stride=1, stride_axis=0)
                bands[r, k * cols : (k + 1) * cols, d * width : (d + 1) * width] = band.astype(
                    bands.dtype
                )
        return carry

    lax.fori_loop(0, rows, one_row, 0)


def started(pairs, sems, first=0):
    copies = [pltpu.make_async_copy(a, b, sems.at[first + i]) for i, (a, b) in enumerate(pairs)]
    for copy in copies:
        copy.start()
    return copies


def finish(copies):
    for copy in copies:
        copy.wait()


def main_kernel(
    core_ref, field, north, south, west, east, corners_west, corners_east, bands_in, mix_in,
    up_in, down_in, cot_in,
    block_out, hg_out, mlp_send_out, mlp_keep_out, mix_send_out, mix_keep_out,
    ext, bands, mix, up, down, cot, feats, hidden, act, pre_grad, hg, block, turned, pre_a,
    pre_b, ag_a, ag_b, mlp_send, mlp_keep, mix_send, mix_keep, sems
):
    core = core_ref[0]
    rows, cols, channels = field.shape
    reach = west.shape[1]
    basis = mix.shape[0]
    points = rows * cols
    half_units, half_channels = up.shape[1] // 2, channels // 2
    body, inner = pl.ds(1, rows), pl.ds(reach, cols)
    begin, end = pl.ds(0, reach), pl.ds(reach + cols, reach)
    loads = started(
        [
            (field, ext.at[body, inner]),
            (west, ext.at[body, begin]),
            (east, ext.at[body, end]),
            (north, ext.at[0, inner]),
            (south, ext.at[rows + 1, inner]),
            (corners_west.at[0], ext.at[0, begin]),
            (corners_west.at[1], ext.at[rows + 1, begin]),
            (corners_east.at[0], ext.at[0, end]),
            (corners_east.at[1], ext.at[rows + 1, end]),
        ],
        sems,
    )
    band_loads = started([(bands_in.at[r], bands.at[r]) for r in range(rows)], sems, 9)
    late = 9 + rows
    weights = started([(mix_in, mix), (up_in, up), (down_in, down), (cot_in, cot)], sems, late)
    finish(loads)

    for r in range(rows):
        finish(band_loads[r : r + 1])
        window = ext[r : r + 3].reshape(3 * ext.shape[1], channels)
        out = dot(bands[r], window).astype(feats.dtype)
        at = pl.ds(r * cols, cols)
        for k in range(basis):
            feats[k, at, :] = out[k * cols : (k + 1) * cols]
        hidden[at, :] = ext[r + 1, inner, :]
    finish(weights[:1])

    for i in range(3):
        at = pl.ds(i * (points // 3), points // 3)
        total = hidden[at, :].astype(jnp.float32)
        for k in range(basis):
            total = total + dot(feats[k, at, :], mix[k])
        hidden[at, :] = total.astype(hidden.dtype)
    finish(weights[1:])
    size = pre_a.shape[0]
    slots = ((pre_a, ag_a), (pre_b, ag_b))

    def products(i):
        at = pl.ds(i * size, size)
        pre, ag = slots[i % 2]
        pre[...] = dot(hidden[at, :], up[...])
        ag[...] = dot(cot[at, :], down[...], OVER_LANES)

    def activation(i):
        at = pl.ds(i * size, size)
        pre, ag = slots[i % 2]
        value = pre[...]
        phi = 0.5 * (1.0 + lax.erf(value * inv_root_two))
        act[at, :] = (value * phi).astype(act.dtype)
        slope = phi + value * jnp.exp(-0.5 * value * value) * inv_root_tau
        pre_grad[at, :] = (ag[...] * slope).astype(pre_grad.dtype)

    products(0)
    for i in range(points // size):
        if (i + 1) * size < points:
            products(i + 1)
        activation(i)
    turned[...] = hidden[...].T

    def mlp_sums(half, out):
        at = pl.ds(pl.multiple_of(half * half_units, half_units), half_units)
        out[:half_units] = dot(act[:, at], cot[...], OVER_ROWS).astype(out.dtype)
        out[half_units:] = dot(turned[...], pre_grad[:, at]).astype(out.dtype)

    mlp_sums(1 - core, mlp_send)
    stores = started([(mlp_send, mlp_send_out)], sems, late + 4)
    mlp_sums(core, mlp_keep)
    stores += started([(mlp_keep, mlp_keep_out)], sems, late + 5)

    parts = [pl.ds(i * (points // 3), points // 3) for i in range(3)]
    for at in parts:
        total = cot[at, :].astype(jnp.float32) + dot(pre_grad[at, :], up[...], OVER_LANES)
        hg[at, :] = total.astype(hg.dtype)
    stores += started([(hg, hg_out)], sems, late + 6)

    def mix_sums(half, out):
        at = pl.ds(pl.multiple_of(half * half_channels, half_channels), half_channels)
        for k in range(basis):
            out[k] = dot(feats[k, :, at], hg[...], OVER_ROWS).astype(out.dtype)

    mix_sums(1 - core, mix_send)
    stores += started([(mix_send, mix_send_out)], sems, late + 7)
    mix_sums(core, mix_keep)
    stores += started([(mix_keep, mix_keep_out)], sems, late + 8)

    for i, at in enumerate(parts):
        total = hidden[at, :].astype(jnp.float32) + dot(act[at, :], down[...])
        block[at, :] = total.astype(block.dtype)
        stores += started([(block.at[at], block_out.at[at])], sems, late + 9 + i)
    finish(stores)


def adjoint_kernel(
    hg_in, mix_in, bands_in, inner_out, rim_out, west_out, east_out,
    hg, mix, bands, grads, pulled, inner, sems, *, cols
):
    basis, channels = mix.shape[0], mix.shape[1]
    rows, width = pulled.shape[0] - 2, pulled.shape[1]
    reach = (width - cols) // 2
    loads = started([(hg_in, hg)], sems)
    loads += started([(mix_in.at[k], mix.at[k]) for k in range(basis)], sems, 1)
    late = 1 + basis
    band_loads = started([(bands_in.at[r], bands.at[r]) for r in range(rows)], sems, late)
    pulled[...] = jnp.zeros(pulled.shape, pulled.dtype)
    group = 5 if rows % 5 == 0 else 1
    finish(loads[:1])
    for k in range(basis):
        finish(loads[1 + k : 2 + k])
        for r in range(0, rows, group):
            part = dot(hg[r * cols : (r + group) * cols, :], mix[k], OVER_LANES)
            grads[r : r + group, k * cols : (k + 1) * cols] = part.astype(grads.dtype).reshape(
                group, cols, channels
            )
    stores = []

    def give(row):
        own = hg[(row - 1) * cols : row * cols, :].astype(jnp.float32)
        inner[row - 1] = (pulled[row, reach : reach + cols] + own).astype(inner.dtype)
        copies = [(inner.at[row - 1], inner_out.at[row - 1])]
        stores.extend(started(copies, sems, late + rows + row - 1))

    for r in range(rows):
        finish(band_loads[r : r + 1])
        part = dot(bands[r], grads[r], OVER_ROWS)
        pulled[r : r + 3] += part.reshape(3, width, channels)
        if r:
            give(r)
    give(rows)
    west_out[...] = pulled[:, :reach].astype(west_out.dtype)
    east_out[...] = pulled[:, reach + cols :].astype(east_out.dtype)
    for n, r in enumerate((0, rows + 1)):
        rim_out[n] = pulled[r, reach : reach + cols]
    finish(stores)


def call(kernel, operands, kinds, shapes, out_kinds, scratch, flops, nbytes):
    return pl.pallas_call(
        kernel,
        out_shape=[jax.ShapeDtypeStruct(shape, kind) for shape, kind in shapes],
        in_specs=[pl.BlockSpec(memory_space=kind) for kind in kinds],
        out_specs=[pl.BlockSpec(memory_space=kind) for kind in out_kinds],
        scratch_shapes=scratch,
        compiler_params=pltpu.CompilerParams(vmem_limit_bytes=VMEM_LIMIT),
        cost_estimate=pl.CostEstimate(flops=flops, bytes_accessed=nbytes, transcendentals=0),
    )(*operands)


def local(field_in, kernel_taps, row_reach, mix_weight, up_weight, down_weight, cotangent):
    lat_rows, lon_cols, channels = field_in.shape
    basis_count = kernel_taps.shape[0]
    tap_count = kernel_taps.shape[3]
    reach = (tap_count - 1) // 2
    hidden_units = up_weight.shape[1]
    place = Place()

    top, bottom = field_in[0], field_in[lat_rows - 1]
    inner = lax.ppermute(jnp.where(place.even, bottom, top), AXES, place.pairs)
    outer = lax.ppermute(jnp.where(place.even, top, bottom), AXES, place.bridges)
    west = lax.ppermute(field_in[:, lon_cols - reach :], "lon", place.east)
    east = lax.ppermute(field_in[:, :reach], "lon", place.west)
    north = jnp.where(place.even, outer, inner)
    south = jnp.where(place.even, inner, outer)
    corners = jnp.stack([north[lon_cols - reach :], south[lon_cols - reach :]])
    corners_west = lax.ppermute(corners, "lon", place.east)
    corners = jnp.stack([north[:reach], south[:reach]])
    corners_east = lax.ppermute(corners, "lon", place.west)

    low, full = jnp.bfloat16, jnp.float32
    points = lat_rows * lon_cols
    width = lon_cols + 2 * reach
    vmem, anywhere, smem = pltpu.VMEM, pl.ANY, pltpu.SMEM
    cot = cotangent.reshape(points, channels)
    band_shape = (lat_rows, basis_count * lon_cols, 3 * width)
    gemm = 2 * points * channels * hidden_units
    mix_gemm = 2 * points * channels * channels * basis_count
    band_gemm = 2 * lat_rows * basis_count * lon_cols * 3 * width * channels
    (bands,) = call(
        functools.partial(band_kernel, cols=lon_cols),
        (row_reach, kernel_taps),
        [smem, vmem],
        [(band_shape, low)],
        [vmem],
        [pltpu.VMEM((basis_count, 3, width), full)],
        0,
        2 * points * hidden_units * 4,
    )

    half_units, half_channels = hidden_units // 2, channels // 2
    mlp_half = (half_units + channels, channels)
    mix_half = (basis_count, half_channels, channels)
    big, wide, many = (points, channels), (points, hidden_units), (basis_count, points, channels)
    core = place.flat % 2
    core_op = core[None].astype(jnp.int32)
    sized = (points // 5, hidden_units)
    block_out, hidden_grad, mlp_send, mlp_keep, mix_send, mix_keep = call(
        main_kernel,
        (
            core_op, field_in, north, south, west, east, corners_west, corners_east, bands,
            mix_weight, up_weight, down_weight, cot,
        ),
        [smem] + [anywhere] * 12,
        [(big, low), (big, low), (mlp_half, low), (mlp_half, low), (mix_half, low), (mix_half, low)],
        [anywhere] * 6,
        [
            pltpu.VMEM((lat_rows + 2, width, channels), low),
            pltpu.VMEM(band_shape, low),
            pltpu.VMEM(mix_weight.shape, low),
            pltpu.VMEM(up_weight.shape, low),
            pltpu.VMEM(down_weight.shape, low),
            pltpu.VMEM(big, low),
            pltpu.VMEM(many, low),
            pltpu.VMEM(big, low),
            pltpu.VMEM(wide, low),
            pltpu.VMEM(wide, low),
            pltpu.VMEM(big, low),
            pltpu.VMEM(big, low),
            pltpu.VMEM((channels, points), low),
            pltpu.VMEM(sized, full),
            pltpu.VMEM(sized, full),
            pltpu.VMEM(sized, full),
            pltpu.VMEM(sized, full),
            pltpu.VMEM(mlp_half, low),
            pltpu.VMEM(mlp_half, low),
            pltpu.VMEM(mix_half, low),
            pltpu.VMEM(mix_half, low),
            pltpu.SemaphoreType.DMA((21 + lat_rows,)),
        ],
        band_gemm + 2 * mix_gemm + 6 * gemm,
        7 * points * hidden_units * 2,
    )

    def adjoint_of(hidden_grad, *start):
        side = (lat_rows + 2, reach, channels)
        return call(
            functools.partial(adjoint_kernel, cols=lon_cols),
            (after(hidden_grad, *start), mix_weight, bands),
            [anywhere] * 3,
            [
                (field_in.shape, low), ((2, lon_cols, channels), full), (side, low), (side, low),
            ],
            [anywhere] + [vmem] * 3,
            [
                pltpu.VMEM(big, low),
                pltpu.VMEM(mix_weight.shape, low),
                pltpu.VMEM(band_shape, low),
                pltpu.VMEM((lat_rows, basis_count * lon_cols, channels), low),
                pltpu.VMEM((lat_rows + 2, width, channels), full),
                pltpu.VMEM(field_in.shape, low),
                pltpu.SemaphoreType.DMA((1 + basis_count + 2 * lat_rows,)),
            ],
            band_gemm + mix_gemm,
            3 * points * hidden_units * 4,
        )

    grad_scale = 1.0 / math.sqrt(points * place.count)
    if place.count == 32:
        ring = Ring(place)
        block_shape = (2, 2, 2, mlp_half[0] // 8, channels)
        mlp = ring.to_core(mlp_keep.reshape(block_shape), mlp_send.reshape(block_shape))
        mlp_out = ring.leaving(mlp, ring.first)
        block_shape = (2, 2, 2, basis_count * half_channels // 8, channels)
        mix = ring.to_core(mix_keep.reshape(block_shape), mix_send.reshape(block_shape))
        mix_out = ring.leaving(mix, ring.first)
        inner, rims, to_west, to_east = adjoint_of(hidden_grad, mlp_out, mix_out)
        from_east = lax.ppermute(to_west, "lon", place.west)
        from_west = lax.ppermute(to_east, "lon", place.east)
        mlp = ring.step(mlp, mlp_out, first_mask, ring.first, to_west)
        mlp_out = ring.leaving(mlp, ring.second)
        mix = ring.step(mix, mix_out, first_mask, ring.first, mlp_out)
        mix_out = ring.leaving(mix, ring.second)
        mlp = ring.step(mlp, mlp_out, second_mask, ring.second, mix_out)
        mlp_out = ring.leaving(mlp, ring.near)
        mix = ring.step(mix, mix_out, second_mask, ring.second, mlp_out)
        mix_out = ring.leaving(mix, ring.near)
        mlp = ring.step(mlp, mlp_out, near_mask, ring.near, mix_out).astype(low)
        mix = ring.step(mix, mix_out, near_mask, ring.near, mlp).astype(low)
        mlp_piece = ring.far_step(mlp, grad_scale, mix)
        mix_piece = ring.far_step(mix, grad_scale, mlp_piece)
        mlp = ring.gather_near(mlp_piece)
        mix = ring.gather_near(mix_piece, mlp)
        mlp = ring.gather_second(mlp, mix)
        from_east, from_west, _ = lax.optimization_barrier((from_east, from_west, mlp))
        mix = ring.gather_second(mix, mlp)
        mlp = ring.gather_first(mlp, mix)
        mix = ring.gather_first(mix, mlp)
        last_block = mix
        mlp_other = ring.gather_core(mlp, mix).reshape(mlp_half)
        mlp = mlp.reshape(mlp_half)
        down_out = halves(core, mlp[:half_units], mlp_other[:half_units], 0)
        up_out = halves(core, mlp[half_units:], mlp_other[half_units:], 1)
        mix_other, down_out, up_out = lax.optimization_barrier(
            (ring.gather_core(mix).reshape(mix_half), down_out, up_out)
        )
        mix_out = halves(core, mix.reshape(mix_half), mix_other, 1)
    else:
        last_block = mix_keep
        inner, rims, to_west, to_east = adjoint_of(hidden_grad)
        from_east = lax.ppermute(to_west, "lon", place.west)
        from_west = lax.ppermute(to_east, "lon", place.east)

        def whole(keep, send):
            keep, send = keep.astype(full)[None], send.astype(full)[None]
            both = jnp.where(core == 0, jnp.concatenate([keep, send]), jnp.concatenate([send, keep]))
            return lax.psum(both, AXES) * grad_scale

        mlp_sum = whole(mlp_keep, mlp_send).astype(low)
        mix_sum = whole(mix_keep, mix_send).astype(low)
        down_out = mlp_sum[:, :half_units].reshape(down_weight.shape)
        up_out = jnp.concatenate([mlp_sum[0, half_units:], mlp_sum[1, half_units:]], axis=1)
        mix_out = mix_sum.swapaxes(0, 1).reshape(mix_weight.shape)

    corner_east = jnp.stack([from_east[0], from_east[lat_rows + 1]]).astype(full)
    corner_west = jnp.stack([from_west[0], from_west[lat_rows + 1]]).astype(full)
    rims = rims.at[:, lon_cols - reach :].add(corner_east)
    rims = rims.at[:, :reach].add(corner_west).astype(low)
    near = lax.ppermute(jnp.where(place.even, rims[1], rims[0]), AXES, place.pairs)
    far = lax.ppermute(jnp.where(place.even, rims[0], rims[1]), AXES, place.bridges)
    near, far, _ = lax.optimization_barrier((near, far, last_block))
    middle = lon_cols - 2 * reach
    beyond = jnp.stack(
        [jnp.where(place.even, far, near), jnp.where(place.even, near, far)]
    ).astype(full)
    sides = jnp.concatenate(
        [
            from_west[1 : lat_rows + 1].astype(full),
            jnp.zeros((lat_rows, middle, channels), full),
            from_east[1 : lat_rows + 1].astype(full),
        ],
        axis=1,
    )
    nothing = jnp.zeros((lat_rows - 2, lon_cols, channels), full)
    ends = jnp.concatenate([beyond[:1], nothing, beyond[1:]])
    grad_field = (inner.astype(full) + sides + ends).astype(low)
    return (block_out.reshape(field_in.shape), grad_field, mix_out, up_out, down_out)


def solution(mesh):
    placed = (
        P("lat", "lon", None),
        P(None, "lat", None, None),
        P("lat"),
        P(),
        P(),
        P(),
        P("lat", "lon", None),
    )
    return jax.shard_map(
        local,
        mesh=mesh,
        in_specs=placed,
        out_specs=(P("lat", "lon", None), P("lat", "lon", None), P(), P(), P()),
        check_vma=False,
    )
```

profile of v0, /device:TPU:0, one launch (start us, length us, event | category | flops | bytes accessed | tf_op | source)
XLA Modules:
  0.0 105.8 jit_solution(1708411688419787425)
XLA Ops:
  1.6 3.0 %collective-permute-start.1 = (bf16[96,512]{1,0:T(8,128)(2,1)S(1)}, bf16[96,512]{1,0:T(8,128)(2,1)S(1)}, u32[]{:S(2)}, u32[]{:S(2)}) collective-permute-start(bf16[96,512]{1,0:T(8,128)(2,1)S(1)} %get-tuple-element.99), channel_id=1, source_target_pairs={{0,4},{1,5},{2,6},{3,7},{4,0},{5,1},{6,2},{7,3},{8,12},{9,13},{10,... | collective-permute-start | bytes 294920 | tf_op jit(solution)/shard_map/ppermute | solution.py:342
  4.6 1.5 %collective-permute-start = (bf16[96,512]{1,0:T(8,128)(2,1)S(1)}, bf16[96,512]{1,0:T(8,128)(2,1)S(1)}, u32[]{:S(2)}, u32[]{:S(2)}) collective-permute-start(bf16[96,512]{1,0:T(8,128)(2,1)S(1)} %get-tuple-element.100), channel_id=1, source_target_pairs={{0,2},{1,3},{2,0},{3,1},{4,8},{5,9},{6,10},{7,11},{8,4},{9,5},{10,... | collective-permute-start | bytes 294920 | tf_op jit(solution)/shard_map/ppermute | solution.py:343
  7.2 1.7 %collective-permute-start.3 = (bf16[10,16,512]{2,1,0:T(8,128)(2,1)S(1)}, bf16[10,16,512]{2,1,0:T(8,128)(2,1)S(1)}, u32[]{:S(2)}, u32[]{:S(2)}) collective-permute-start(bf16[10,16,512]{2,1,0:T(8,128)(2,1)S(1)} %get-tuple-element.97), channel_id=1, source_target_pairs={{1,0},{2,1},{3,2},{0,3},{5,4},{6,5},{7,6},{4,7},{9,8},{10,9},{11,1... | collective-permute-start | bytes 491528 | tf_op jit(solution)/shard_map/ppermute | solution.py:345
  9.4 1.7 %collective-permute-start.5 = (bf16[2,16,512]{2,1,0:T(8,128)(2,1)S(1)}, bf16[2,16,512]{2,1,0:T(8,128)(2,1)S(1)}, u32[]{:S(2)}, u32[]{:S(2)}) collective-permute-start(bf16[2,16,512]{2,1,0:T(8,128)(2,1)S(1)} %pad_maximum_fusion.7), channel_id=1, source_target_pairs={{1,0},{2,1},{3,2},{0,3},{5,4},{6,5},{7,6},{4,7},{9,8},{10,9},{11,1... | collective-permute-start | bytes 98312 | tf_op jit(solution)/shard_map/ppermute | solution.py:351
  11.1 3.5 %shard_map.110.bands_in = bf16[10,288,384]{2,1,0:T(8,128)(2,1)} custom-call(s32[10]{0:T(128)} %reach_ref.1, bf16[3,10,3,33]{3,2,1,0:T(4,128)(2,1)} %taps.1), custom_call_target="tpu_custom_call" | custom-call | bytes 7864320 | tf_op jit(solution)/shard_map/pallas_call | solution.py:322
  15.4 16.6 %shard_map.111 = (bf16[960,512]{1,0:T(8,128)(2,1)}, bf16[960,512]{1,0:T(8,128)(2,1)}, bf16[1024,512]{1,0:T(8,128)(2,1)}, bf16[1024,512]{1,0:T(8,128)(2,1)}, bf16...) custom-call(s32[1]{0:T(128)} %bitcast.core_ref, bf16[10,96,512]{2,1,0:T(8,128)(2,1)} %field.1, ...), custom_call_target="tpu_custom_call" | custom-call | flops 10192158720 | bytes 13762560 | tf_op jit(solution)/shard_map/pallas_call | solution.py:322
  32.7 2.2 %collective-permute-done.6 = bf16[2,2,2,128,512]{4,3,2,1,0:T(8,128)(2,1)S(1)} collective-permute-done((bf16[2,2,2,128,512]{4,3,2,1,0:T(8,128)(2,1)}, bf16[2,2,2,128,512]{4,3,2,1,0:T(8,128)(2,1)S(1)}, u32[]{:S(2)}, u32[]{:S(2)}) %collective-permute-start.6) | collective-permute-done | bytes 1048608 | tf_op jit(solution)/shard_map/ppermute | solution.py:46
  34.9 1.6 %convert_add_fusion = f32[2,2,2,128,512]{4,3,2,1,0:T(8,128)S(1)} fusion(bf16[2,2,2,128,512]{4,3,2,1,0:T(8,128)(2,1)} %bitcast.73, bf16[2,2,2,128,512]{4,3,2,1,0:T(8,128)(2,1)S(1)} %collective-permute-done.6), kind=kLoop, calls=%fused_computation | loop fusion | flops 1572864 | bytes 4194304 | tf_op jit(solution)/shard_map/add | solution.py:84
  36.6 1.6 %collective-permute-start.10 = (bf16[2,2,128,512]{3,2,1,0:T(8,128)(2,1)S(1)}, bf16[2,2,128,512]{3,2,1,0:T(8,128)(2,1)S(1)}, u32[]{:S(2)}, u32[]{:S(2)}) collective-permute-start(bf16[2,2,128,512]{3,2,1,0:T(8,128)(2,1)S(1)} %fusion.2), channel_id=1, source_target_pairs={{0,2},{1,5},{2,0},{3,7},{4,6},{5,1},{6,4},{7,3},{8,10},{9,13},{10,... | collective-permute-start | bytes 1572872 | tf_op jit(solution)/shard_map/ppermute | solution.py:46
  39.1 8.7 %shard_map.112 = (bf16[10,96,512]{2,1,0:T(8,128)(2,1)}, f32[2,96,512]{2,1,0:T(8,128)}, bf16[12,16,512]{2,1,0:T(8,128)(2,1)}, bf16[12,16,512]{2,1,0:T(8,128)(2,1)}) custom-call(bf16[960,512]{1,0:T(8,128)(2,1)} %get-tuple-element.67.hg_in, bf16[3,512,512]{2,1,0:T(8,128)(2,1)} %mix_in.3, bf16[10,288,384]{2,1,0:T(8,128)(2,1)} %shard_map.110.bands_in), custom_call_target="tpu_custom_call" | custom-call | flops 2642411520 | bytes 11796480 | tf_op jit(solution)/shard_map/pallas_call | solution.py:322
  47.8 1.1 %collective-permute-start.8 = (bf16[12,16,512]{2,1,0:T(8,128)(2,1)}, bf16[12,16,512]{2,1,0:T(8,128)(2,1)S(1)}, u32[]{:S(2)}, u32[]{:S(2)}) collective-permute-start(bf16[12,16,512]{2,1,0:T(8,128)(2,1)} %get-tuple-element.69), channel_id=1, source_target_pairs={{1,0},{2,1},{3,2},{0,3},{5,4},{6,5},{7,6},{4,7},{9,8},{10,9},{11,1... | collective-permute-start | bytes 589832 | tf_op jit(solution)/shard_map/ppermute | solution.py:450
  49.2 1.8 %collective-permute-start.11 = (bf16[2,128,512]{2,1,0:T(8,128)(2,1)S(1)}, bf16[2,128,512]{2,1,0:T(8,128)(2,1)S(1)}, u32[]{:S(2)}, u32[]{:S(2)}) collective-permute-start(bf16[2,128,512]{2,1,0:T(8,128)(2,1)S(1)} %fusion.4), channel_id=1, source_target_pairs={{0,4},{1,3},{2,6},{3,1},{4,0},{5,7},{6,2},{7,5},{8,12},{9,11},{10,... | collective-permute-start | bytes 786440 | tf_op jit(solution)/shard_map/ppermute | solution.py:46
  51.1 1.2 %collective-permute-start.14 = (bf16[2,96,512]{2,1,0:T(8,128)(2,1)S(1)}, bf16[2,96,512]{2,1,0:T(8,128)(2,1)S(1)}, u32[]{:S(2)}, u32[]{:S(2)}) collective-permute-start(bf16[2,96,512]{2,1,0:T(8,128)(2,1)S(1)} %fusion.6), channel_id=1, source_target_pairs={{0,4},{1,3},{2,6},{3,1},{4,0},{5,7},{6,2},{7,5},{8,12},{9,11},{10,... | collective-permute-start | bytes 589832 | tf_op jit(solution)/shard_map/ppermute | solution.py:46
  52.3 3.3 %collective-permute-done.11 = bf16[2,128,512]{2,1,0:T(8,128)(2,1)S(1)} collective-permute-done((bf16[2,128,512]{2,1,0:T(8,128)(2,1)S(1)}, bf16[2,128,512]{2,1,0:T(8,128)(2,1)S(1)}, u32[]{:S(2)}, u32[]{:S(2)}) %collective-permute-start.11) | collective-permute-done | bytes 262176 | tf_op jit(solution)/shard_map/ppermute | solution.py:46
  55.7 2.1 %collective-permute-start.13 = (bf16[128,512]{1,0:T(8,128)(2,1)S(1)}, bf16[128,512]{1,0:T(8,128)(2,1)S(1)}, u32[]{:S(2)}, u32[]{:S(2)}) collective-permute-start(bf16[128,512]{1,0:T(8,128)(2,1)S(1)} %fusion.8), channel_id=1, source_target_pairs={{0,8},{1,9},{2,10},{3,11},{4,12},{5,13},{6,14},{7,15},{8,0},{9,1},... | collective-permute-start | bytes 393224 | tf_op jit(solution)/shard_map/ppermute | solution.py:46
  57.9 2.0 %collective-permute-start.16 = (bf16[96,512]{1,0:T(8,128)(2,1)S(1)}, bf16[96,512]{1,0:T(8,128)(2,1)S(1)}, u32[]{:S(2)}, u32[]{:S(2)}) collective-permute-start(bf16[96,512]{1,0:T(8,128)(2,1)S(1)} %fusion.9), channel_id=1, source_target_pairs={{0,8},{1,9},{2,10},{3,11},{4,12},{5,13},{6,14},{7,15},{8,0},{9,1},... | collective-permute-start | bytes 294920 | tf_op jit(solution)/shard_map/ppermute | solution.py:46
  60.8 3.1 %collective-permute-start.15 = (bf16[128,512]{1,0:T(8,128)(2,1)S(1)}, bf16[128,512]{1,0:T(8,128)(2,1)S(1)}, u32[]{:S(2)}, u32[]{:S(2)}) collective-permute-start(bf16[128,512]{1,0:T(8,128)(2,1)S(1)} %fusion.5), channel_id=1, source_target_pairs={{0,16},{1,17},{2,18},{3,19},{4,20},{5,21},{6,22},{7,23},{8,24},{9,... | collective-permute-start | bytes 393224 | tf_op jit(solution)/shard_map/ppermute | solution.py:46
  64.0 2.7 %collective-permute-start.19 = (bf16[96,512]{1,0:T(8,128)(2,1)S(1)}, bf16[96,512]{1,0:T(8,128)(2,1)S(1)}, u32[]{:S(2)}, u32[]{:S(2)}) collective-permute-start(bf16[96,512]{1,0:T(8,128)(2,1)S(1)} %fusion.7), channel_id=1, source_target_pairs={{0,16},{1,17},{2,18},{3,19},{4,20},{5,21},{6,22},{7,23},{8,24},{9,... | collective-permute-start | bytes 294920 | tf_op jit(solution)/shard_map/ppermute | solution.py:46
  66.9 6.8 %collective-permute-start.17 = (bf16[1,128,512]{2,1,0:T(8,128)(2,1)S(1)}, bf16[1,128,512]{2,1,0:T(8,128)(2,1)S(1)}, u32[]{:S(2)}, u32[]{:S(2)}) collective-permute-start(bf16[1,128,512]{2,1,0:T(8,128)(2,1)S(1)} %bitcast.76), channel_id=1, source_target_pairs={{0,8},{1,9},{2,10},{3,11},{4,12},{5,13},{6,14},{7,15},{8,0},{9,1},... | collective-permute-start | bytes 393224 | tf_op jit(solution)/shard_map/ppermute | solution.py:46
  74.3 1.6 %collective-permute-start.20 = (bf16[1,96,512]{2,1,0:T(8,128)(2,1)S(1)}, bf16[1,96,512]{2,1,0:T(8,128)(2,1)S(1)}, u32[]{:S(2)}, u32[]{:S(2)}) collective-permute-start(bf16[1,96,512]{2,1,0:T(8,128)(2,1)S(1)} %fusion.10), channel_id=1, source_target_pairs={{0,8},{1,9},{2,10},{3,11},{4,12},{5,13},{6,14},{7,15},{8,0},{9,1},... | collective-permute-start | bytes 294920 | tf_op jit(solution)/shard_map/ppermute | solution.py:46
  75.8 1.5 %collective-permute-done.17 = bf16[1,128,512]{2,1,0:T(8,128)(2,1)S(1)} collective-permute-done((bf16[1,128,512]{2,1,0:T(8,128)(2,1)S(1)}, bf16[1,128,512]{2,1,0:T(8,128)(2,1)S(1)}, u32[]{:S(2)}, u32[]{:S(2)}) %collective-permute-start.17) | collective-permute-done | bytes 131104 | tf_op jit(solution)/shard_map/ppermute | solution.py:46
  77.4 1.0 collective-permute-start.18
  78.4 1.6 %collective-permute-done.20 = bf16[1,96,512]{2,1,0:T(8,128)(2,1)S(1)} collective-permute-done((bf16[1,96,512]{2,1,0:T(8,128)(2,1)S(1)}, bf16[1,96,512]{2,1,0:T(8,128)(2,1)S(1)}, u32[]{:S(2)}, u32[]{:S(2)}) %collective-permute-start.20) | collective-permute-done | bytes 98336 | tf_op jit(solution)/shard_map/ppermute | solution.py:46
  80.0 1.3 %collective-permute-start.23 = (bf16[2,96,512]{2,1,0:T(8,128)(2,1)S(1)}, bf16[2,96,512]{2,1,0:T(8,128)(2,1)S(1)}, u32[]{:S(2)}, u32[]{:S(2)}) collective-permute-start(bf16[2,96,512]{2,1,0:T(8,128)(2,1)S(1)} %pad_maximum_fusion.5), channel_id=1, source_target_pairs={{0,4},{1,3},{2,6},{3,1},{4,0},{5,7},{6,2},{7,5},{8,12},{9,11},{10,... | collective-permute-start | bytes 589832 | tf_op jit(solution)/shard_map/ppermute | solution.py:46
  81.4 2.5 %collective-permute-done.18 = bf16[2,128,512]{2,1,0:T(8,128)(2,1)S(1)} collective-permute-done((bf16[2,128,512]{2,1,0:T(8,128)(2,1)S(1)}, bf16[2,128,512]{2,1,0:T(8,128)(2,1)S(1)}, u32[]{:S(2)}, u32[]{:S(2)}) %collective-permute-start.18) | collective-permute-done | bytes 262176 | tf_op jit(solution)/shard_map/ppermute | solution.py:46
  83.9 1.8 %collective-permute-start.25 = (bf16[4,128,512]{2,1,0:T(8,128)(2,1)S(1)}, bf16[4,128,512]{2,1,0:T(8,128)(2,1)S(1)}, u32[]{:S(2)}, u32[]{:S(2)}) collective-permute-start(bf16[4,128,512]{2,1,0:T(8,128)(2,1)S(1)} %pad_maximum_fusion.2), channel_id=1, source_target_pairs={{0,2},{1,5},{2,0},{3,7},{4,6},{5,1},{6,4},{7,3},{8,10},{9,13},{10,... | collective-permute-start | bytes 1572872 | tf_op jit(solution)/shard_map/ppermute | solution.py:46
  87.2 1.7 %collective-permute-start.24 = (bf16[4,96,512]{2,1,0:T(8,128)(2,1)S(1)}, bf16[4,96,512]{2,1,0:T(8,128)(2,1)S(1)}, u32[]{:S(2)}, u32[]{:S(2)}) collective-permute-start(bf16[4,96,512]{2,1,0:T(8,128)(2,1)S(1)} %pad_maximum_fusion.3), channel_id=1, source_target_pairs={{0,2},{1,5},{2,0},{3,7},{4,6},{5,1},{6,4},{7,3},{8,10},{9,13},{10,... | collective-permute-start | bytes 1179656 | tf_op jit(solution)/shard_map/ppermute | solution.py:46
  89.1 5.2 %collective-permute-done.25 = bf16[4,128,512]{2,1,0:T(8,128)(2,1)S(1)} collective-permute-done((bf16[4,128,512]{2,1,0:T(8,128)(2,1)S(1)}, bf16[4,128,512]{2,1,0:T(8,128)(2,1)S(1)}, u32[]{:S(2)}, u32[]{:S(2)}) %collective-permute-start.25) | collective-permute-done | bytes 524320 | tf_op jit(solution)/shard_map/ppermute | solution.py:46
  94.4 1.3 %collective-permute-start.27 = (bf16[8,128,512]{2,1,0:T(8,128)(2,1)S(1)}, bf16[8,128,512]{2,1,0:T(8,128)(2,1)S(1)}, u32[]{:S(2)}, u32[]{:S(2)}) collective-permute-start(bf16[8,128,512]{2,1,0:T(8,128)(2,1)S(1)} %pad_maximum_fusion), channel_id=1, source_target_pairs={{0,1},{1,0},{2,3},{3,2},{4,5},{5,4},{6,7},{7,6},{8,9},{9,8},{10,11... | collective-permute-start | bytes 3145736 | tf_op jit(solution)/shard_map/ppermute | solution.py:46
  95.6 3.8 %collective-permute-done.24 = bf16[4,96,512]{2,1,0:T(8,128)(2,1)S(1)} collective-permute-done((bf16[4,96,512]{2,1,0:T(8,128)(2,1)S(1)}, bf16[4,96,512]{2,1,0:T(8,128)(2,1)S(1)}, u32[]{:S(2)}, u32[]{:S(2)}) %collective-permute-start.24) | collective-permute-done | bytes 393248 | tf_op jit(solution)/shard_map/ppermute | solution.py:46
  99.6 1.3 %collective-permute-start.26 = (bf16[8,96,512]{2,1,0:T(8,128)(2,1)S(1)}, bf16[8,96,512]{2,1,0:T(8,128)(2,1)S(1)}, u32[]{:S(2)}, u32[]{:S(2)}) collective-permute-start(bf16[8,96,512]{2,1,0:T(8,128)(2,1)S(1)} %pad_maximum_fusion.1), channel_id=1, source_target_pairs={{0,1},{1,0},{2,3},{3,2},{4,5},{5,4},{6,7},{7,6},{8,9},{9,8},{10,11... | collective-permute-start | bytes 2359304 | tf_op jit(solution)/shard_map/ppermute | solution.py:46
  102.5 1.3 %fusion.1 = bf16[10,96,512]{2,1,0:T(8,128)(2,1)} fusion(f32[10,16,512]{2,1,0:T(8,128)S(1)} %slice_convert_fusion, f32[10,16,512]{2,1,0:T(8,128)S(1)} %slice_convert_fusion.1, f32[1,96,512]{2,1,0:T(8,128)S(1)} %get-tuple-element.106, f32[1,96,512]{2,1,0:T(8,128)S(1)} %get-tuple-element.105, bf16[10,96,512]{2,1,0:T(8,128)(2,1)S(1)} %copy-done.3, ...), kind=kLoop, calls=%fused_computation.3 | loop fusion | flops 3932160 | bytes 3015080 | tf_op jit(solution)/shard_map/convert_element_type | solution.py:518
  (111 shorter events, 12.4 us)
Async XLA Ops:
  1.6 7.3 %collective-permute-start.1 = (bf16[96,512]{1,0:T(8,128)(2,1)S(1)}, bf16[96,512]{1,0:T(8,128)(2,1)S(1)}, u32[]{:S(2)}, u32[]{:S(2)}) collective-permute-start(bf16[96,512]{1,0:T(8,128)(2,1)S(1)} %get-tuple-element.99), channel_id=1, source_target_pairs={{0,4},{1,5},{2,6},{3,7},{4,0},{5,1},{6,2},{7,3},{8,12},{9,13},{10,... | collective-permute-start | bytes 294920 | tf_op jit(solution)/shard_map/ppermute | solution.py:342
  4.6 4.6 %collective-permute-start = (bf16[96,512]{1,0:T(8,128)(2,1)S(1)}, bf16[96,512]{1,0:T(8,128)(2,1)S(1)}, u32[]{:S(2)}, u32[]{:S(2)}) collective-permute-start(bf16[96,512]{1,0:T(8,128)(2,1)S(1)} %get-tuple-element.100), channel_id=1, source_target_pairs={{0,2},{1,3},{2,0},{3,1},{4,8},{5,9},{6,10},{7,11},{8,4},{9,5},{10,... | collective-permute-start | bytes 294920 | tf_op jit(solution)/shard_map/ppermute | solution.py:343
  7.2 7.5 %collective-permute-start.2 = (bf16[10,16,512]{2,1,0:T(8,128)(2,1)S(1)}, bf16[10,16,512]{2,1,0:T(8,128)(2,1)S(1)}, u32[]{:S(2)}, u32[]{:S(2)}) collective-permute-start(bf16[10,16,512]{2,1,0:T(8,128)(2,1)S(1)} %get-tuple-element.98), channel_id=1, source_target_pairs={{0,1},{1,2},{2,3},{3,0},{4,5},{5,6},{6,7},{7,4},{8,9},{9,10},{10,1... | collective-permute-start | bytes 491528 | tf_op jit(solution)/shard_map/ppermute | solution.py:344
  7.2 7.5 %collective-permute-start.3 = (bf16[10,16,512]{2,1,0:T(8,128)(2,1)S(1)}, bf16[10,16,512]{2,1,0:T(8,128)(2,1)S(1)}, u32[]{:S(2)}, u32[]{:S(2)}) collective-permute-start(bf16[10,16,512]{2,1,0:T(8,128)(2,1)S(1)} %get-tuple-element.97), channel_id=1, source_target_pairs={{1,0},{2,1},{3,2},{0,3},{5,4},{6,5},{7,6},{4,7},{9,8},{10,9},{11,1... | collective-permute-start | bytes 491528 | tf_op jit(solution)/shard_map/ppermute | solution.py:345
  9.3 5.5 %copy-start.6 = (bf16[96,512]{1,0:T(8,128)(2,1)}, bf16[96,512]{1,0:T(8,128)(2,1)S(1)}, u32[]{:S(2)}) copy-start(bf16[96,512]{1,0:T(8,128)(2,1)S(1)} %get-tuple-element.121.south) | copy-start | bytes 294916
  9.3 5.5 %copy-start.7 = (bf16[96,512]{1,0:T(8,128)(2,1)}, bf16[96,512]{1,0:T(8,128)(2,1)S(1)}, u32[]{:S(2)}) copy-start(bf16[96,512]{1,0:T(8,128)(2,1)S(1)} %get-tuple-element.122.north) | copy-start | bytes 294916
  9.3 5.4 %collective-permute-start.4 = (bf16[2,16,512]{2,1,0:T(8,128)(2,1)S(1)}, bf16[2,16,512]{2,1,0:T(8,128)(2,1)S(1)}, u32[]{:S(2)}, u32[]{:S(2)}) collective-permute-start(bf16[2,16,512]{2,1,0:T(8,128)(2,1)S(1)} %pad_maximum_fusion.6), channel_id=1, source_target_pairs={{0,1},{1,2},{2,3},{3,0},{4,5},{5,6},{6,7},{7,4},{8,9},{9,10},{10,1... | collective-permute-start | bytes 98312 | tf_op jit(solution)/shard_map/ppermute | solution.py:349
  9.4 5.3 %collective-permute-start.5 = (bf16[2,16,512]{2,1,0:T(8,128)(2,1)S(1)}, bf16[2,16,512]{2,1,0:T(8,128)(2,1)S(1)}, u32[]{:S(2)}, u32[]{:S(2)}) collective-permute-start(bf16[2,16,512]{2,1,0:T(8,128)(2,1)S(1)} %pad_maximum_fusion.7), channel_id=1, source_target_pairs={{1,0},{2,1},{3,2},{0,3},{5,4},{6,5},{7,6},{4,7},{9,8},{10,9},{11,1... | collective-permute-start | bytes 98312 | tf_op jit(solution)/shard_map/ppermute | solution.py:351
  32.0 2.9 %collective-permute-start.6 = (bf16[2,2,2,128,512]{4,3,2,1,0:T(8,128)(2,1)}, bf16[2,2,2,128,512]{4,3,2,1,0:T(8,128)(2,1)S(1)}, u32[]{:S(2)}, u32[]{:S(2)}) collective-permute-start(bf16[2,2,2,128,512]{4,3,2,1,0:T(8,128)(2,1)} %bitcast.77), channel_id=1, source_target_pairs={{0,1},{1,0},{2,3},{3,2},{4,5},{5,4},{6,7},{7,6},{8,9},{9,8},{10,11... | collective-permute-start | bytes 3145736 | tf_op jit(solution)/shard_map/ppermute | solution.py:46
  32.1 6.1 %collective-permute-start.7 = (bf16[2,2,2,96,512]{4,3,2,1,0:T(8,128)(2,1)}, bf16[2,2,2,96,512]{4,3,2,1,0:T(8,128)(2,1)S(1)}, u32[]{:S(2)}, u32[]{:S(2)}) collective-permute-start(bf16[2,2,2,96,512]{4,3,2,1,0:T(8,128)(2,1)} %bitcast.79), channel_id=1, source_target_pairs={{0,1},{1,0},{2,3},{3,2},{4,5},{5,4},{6,7},{7,6},{8,9},{9,8},{10,11... | collective-permute-start | bytes 2359304 | tf_op jit(solution)/shard_map/ppermute | solution.py:46
  34.9 3.3 %copy-start.4 = (bf16[3,256,512]{2,1,0:T(8,128)(2,1)S(1)}, bf16[3,256,512]{2,1,0:T(8,128)(2,1)}, u32[]{:S(2)}) copy-start(bf16[3,256,512]{2,1,0:T(8,128)(2,1)} %get-tuple-element.65) | copy-start | bytes 2359300
  36.6 12.3 %collective-permute-start.10 = (bf16[2,2,128,512]{3,2,1,0:T(8,128)(2,1)S(1)}, bf16[2,2,128,512]{3,2,1,0:T(8,128)(2,1)S(1)}, u32[]{:S(2)}, u32[]{:S(2)}) collective-permute-start(bf16[2,2,128,512]{3,2,1,0:T(8,128)(2,1)S(1)} %fusion.2), channel_id=1, source_target_pairs={{0,2},{1,5},{2,0},{3,7},{4,6},{5,1},{6,4},{7,3},{8,10},{9,13},{10,... | collective-permute-start | bytes 1572872 | tf_op jit(solution)/shard_map/ppermute | solution.py:46
  38.5 12.4 %collective-permute-start.12 = (bf16[2,2,96,512]{3,2,1,0:T(8,128)(2,1)S(1)}, bf16[2,2,96,512]{3,2,1,0:T(8,128)(2,1)S(1)}, u32[]{:S(2)}, u32[]{:S(2)}) collective-permute-start(bf16[2,2,96,512]{3,2,1,0:T(8,128)(2,1)S(1)} %fusion.3), channel_id=1, source_target_pairs={{0,2},{1,5},{2,0},{3,7},{4,6},{5,1},{6,4},{7,3},{8,10},{9,13},{10,... | collective-permute-start | bytes 1179656 | tf_op jit(solution)/shard_map/ppermute | solution.py:46
  47.8 38.0 %collective-permute-start.8 = (bf16[12,16,512]{2,1,0:T(8,128)(2,1)}, bf16[12,16,512]{2,1,0:T(8,128)(2,1)S(1)}, u32[]{:S(2)}, u32[]{:S(2)}) collective-permute-start(bf16[12,16,512]{2,1,0:T(8,128)(2,1)} %get-tuple-element.69), channel_id=1, source_target_pairs={{1,0},{2,1},{3,2},{0,3},{5,4},{6,5},{7,6},{4,7},{9,8},{10,9},{11,1... | collective-permute-start | bytes 589832 | tf_op jit(solution)/shard_map/ppermute | solution.py:450
  48.9 36.8 %collective-permute-start.9 = (bf16[12,16,512]{2,1,0:T(8,128)(2,1)}, bf16[12,16,512]{2,1,0:T(8,128)(2,1)S(1)}, u32[]{:S(2)}, u32[]{:S(2)}) collective-permute-start(bf16[12,16,512]{2,1,0:T(8,128)(2,1)} %get-tuple-element.70), channel_id=1, source_target_pairs={{0,1},{1,2},{2,3},{3,0},{4,5},{5,6},{6,7},{7,4},{8,9},{9,10},{10,1... | collective-permute-start | bytes 589832 | tf_op jit(solution)/shard_map/ppermute | solution.py:451
  49.2 6.4 %collective-permute-start.11 = (bf16[2,128,512]{2,1,0:T(8,128)(2,1)S(1)}, bf16[2,128,512]{2,1,0:T(8,128)(2,1)S(1)}, u32[]{:S(2)}, u32[]{:S(2)}) collective-permute-start(bf16[2,128,512]{2,1,0:T(8,128)(2,1)S(1)} %fusion.4), channel_id=1, source_target_pairs={{0,4},{1,3},{2,6},{3,1},{4,0},{5,7},{6,2},{7,5},{8,12},{9,11},{10,... | collective-permute-start | bytes 786440 | tf_op jit(solution)/shard_map/ppermute | solution.py:46
  51.1 6.7 %collective-permute-start.14 = (bf16[2,96,512]{2,1,0:T(8,128)(2,1)S(1)}, bf16[2,96,512]{2,1,0:T(8,128)(2,1)S(1)}, u32[]{:S(2)}, u32[]{:S(2)}) collective-permute-start(bf16[2,96,512]{2,1,0:T(8,128)(2,1)S(1)} %fusion.6), channel_id=1, source_target_pairs={{0,4},{1,3},{2,6},{3,1},{4,0},{5,7},{6,2},{7,5},{8,12},{9,11},{10,... | collective-permute-start | bytes 589832 | tf_op jit(solution)/shard_map/ppermute | solution.py:46
  55.7 5.1 %collective-permute-start.13 = (bf16[128,512]{1,0:T(8,128)(2,1)S(1)}, bf16[128,512]{1,0:T(8,128)(2,1)S(1)}, u32[]{:S(2)}, u32[]{:S(2)}) collective-permute-start(bf16[128,512]{1,0:T(8,128)(2,1)S(1)} %fusion.8), channel_id=1, source_target_pairs={{0,8},{1,9},{2,10},{3,11},{4,12},{5,13},{6,14},{7,15},{8,0},{9,1},... | collective-permute-start | bytes 393224 | tf_op jit(solution)/shard_map/ppermute | solution.py:46
  57.9 6.0 %collective-permute-start.16 = (bf16[96,512]{1,0:T(8,128)(2,1)S(1)}, bf16[96,512]{1,0:T(8,128)(2,1)S(1)}, u32[]{:S(2)}, u32[]{:S(2)}) collective-permute-start(bf16[96,512]{1,0:T(8,128)(2,1)S(1)} %fusion.9), channel_id=1, source_target_pairs={{0,8},{1,9},{2,10},{3,11},{4,12},{5,13},{6,14},{7,15},{8,0},{9,1},... | collective-permute-start | bytes 294920 | tf_op jit(solution)/shard_map/ppermute | solution.py:46
  60.8 6.1 %collective-permute-start.15 = (bf16[128,512]{1,0:T(8,128)(2,1)S(1)}, bf16[128,512]{1,0:T(8,128)(2,1)S(1)}, u32[]{:S(2)}, u32[]{:S(2)}) collective-permute-start(bf16[128,512]{1,0:T(8,128)(2,1)S(1)} %fusion.5), channel_id=1, source_target_pairs={{0,16},{1,17},{2,18},{3,19},{4,20},{5,21},{6,22},{7,23},{8,24},{9,... | collective-permute-start | bytes 393224 | tf_op jit(solution)/shard_map/ppermute | solution.py:46
  64.0 10.3 %collective-permute-start.19 = (bf16[96,512]{1,0:T(8,128)(2,1)S(1)}, bf16[96,512]{1,0:T(8,128)(2,1)S(1)}, u32[]{:S(2)}, u32[]{:S(2)}) collective-permute-start(bf16[96,512]{1,0:T(8,128)(2,1)S(1)} %fusion.7), channel_id=1, source_target_pairs={{0,16},{1,17},{2,18},{3,19},{4,20},{5,21},{6,22},{7,23},{8,24},{9,... | collective-permute-start | bytes 294920 | tf_op jit(solution)/shard_map/ppermute | solution.py:46
  66.9 10.4 %collective-permute-start.17 = (bf16[1,128,512]{2,1,0:T(8,128)(2,1)S(1)}, bf16[1,128,512]{2,1,0:T(8,128)(2,1)S(1)}, u32[]{:S(2)}, u32[]{:S(2)}) collective-permute-start(bf16[1,128,512]{2,1,0:T(8,128)(2,1)S(1)} %bitcast.76), channel_id=1, source_target_pairs={{0,8},{1,9},{2,10},{3,11},{4,12},{5,13},{6,14},{7,15},{8,0},{9,1},... | collective-permute-start | bytes 393224 | tf_op jit(solution)/shard_map/ppermute | solution.py:46
  74.3 11.5 %copy-start.5 = (f32[2,96,512]{2,1,0:T(8,128)S(1)}, f32[2,96,512]{2,1,0:T(8,128)}, u32[]{:S(2)}) copy-start(f32[2,96,512]{2,1,0:T(8,128)} %get-tuple-element.83) | copy-start | bytes 1179652
  74.3 5.7 %collective-permute-start.20 = (bf16[1,96,512]{2,1,0:T(8,128)(2,1)S(1)}, bf16[1,96,512]{2,1,0:T(8,128)(2,1)S(1)}, u32[]{:S(2)}, u32[]{:S(2)}) collective-permute-start(bf16[1,96,512]{2,1,0:T(8,128)(2,1)S(1)} %fusion.10), channel_id=1, source_target_pairs={{0,8},{1,9},{2,10},{3,11},{4,12},{5,13},{6,14},{7,15},{8,0},{9,1},... | collective-permute-start | bytes 294920 | tf_op jit(solution)/shard_map/ppermute | solution.py:46
  77.4 6.4 %collective-permute-start.18 = (bf16[2,128,512]{2,1,0:T(8,128)(2,1)S(1)}, bf16[2,128,512]{2,1,0:T(8,128)(2,1)S(1)}, u32[]{:S(2)}, u32[]{:S(2)}) collective-permute-start(bf16[2,128,512]{2,1,0:T(8,128)(2,1)S(1)} %pad_maximum_fusion.4), channel_id=1, source_target_pairs={{0,4},{1,3},{2,6},{3,1},{4,0},{5,7},{6,2},{7,5},{8,12},{9,11},{10,... | collective-permute-start | bytes 786440 | tf_op jit(solution)/shard_map/ppermute | solution.py:46
  80.0 7.1 %collective-permute-start.23 = (bf16[2,96,512]{2,1,0:T(8,128)(2,1)S(1)}, bf16[2,96,512]{2,1,0:T(8,128)(2,1)S(1)}, u32[]{:S(2)}, u32[]{:S(2)}) collective-permute-start(bf16[2,96,512]{2,1,0:T(8,128)(2,1)S(1)} %pad_maximum_fusion.5), channel_id=1, source_target_pairs={{0,4},{1,3},{2,6},{3,1},{4,0},{5,7},{6,2},{7,5},{8,12},{9,11},{10,... | collective-permute-start | bytes 589832 | tf_op jit(solution)/shard_map/ppermute | solution.py:46
  83.9 10.3 %collective-permute-start.25 = (bf16[4,128,512]{2,1,0:T(8,128)(2,1)S(1)}, bf16[4,128,512]{2,1,0:T(8,128)(2,1)S(1)}, u32[]{:S(2)}, u32[]{:S(2)}) collective-permute-start(bf16[4,128,512]{2,1,0:T(8,128)(2,1)S(1)} %pad_maximum_fusion.2), channel_id=1, source_target_pairs={{0,2},{1,5},{2,0},{3,7},{4,6},{5,1},{6,4},{7,3},{8,10},{9,13},{10,... | collective-permute-start | bytes 1572872 | tf_op jit(solution)/shard_map/ppermute | solution.py:46
  85.9 15.0 %collective-permute-start.21 = (bf16[96,512]{1,0:T(8,128)(2,1)S(1)}, bf16[96,512]{1,0:T(8,128)(2,1)S(1)}, u32[]{:S(2)}, u32[]{:S(2)}) collective-permute-start(bf16[96,512]{1,0:T(8,128)(2,1)S(1)} %get-tuple-element.114), channel_id=1, source_target_pairs={{0,4},{1,5},{2,6},{3,7},{4,0},{5,1},{6,2},{7,3},{8,12},{9,13},{10,... | collective-permute-start | bytes 294920 | tf_op jit(solution)/shard_map/ppermute | solution.py:501
  86.8 14.1 %collective-permute-start.22 = (bf16[96,512]{1,0:T(8,128)(2,1)S(1)}, bf16[96,512]{1,0:T(8,128)(2,1)S(1)}, u32[]{:S(2)}, u32[]{:S(2)}) collective-permute-start(bf16[96,512]{1,0:T(8,128)(2,1)S(1)} %get-tuple-element.113), channel_id=1, source_target_pairs={{0,2},{1,3},{2,0},{3,1},{4,8},{5,9},{6,10},{7,11},{8,4},{9,5},{10,... | collective-permute-start | bytes 294920 | tf_op jit(solution)/shard_map/ppermute | solution.py:502
  87.2 12.2 %collective-permute-start.24 = (bf16[4,96,512]{2,1,0:T(8,128)(2,1)S(1)}, bf16[4,96,512]{2,1,0:T(8,128)(2,1)S(1)}, u32[]{:S(2)}, u32[]{:S(2)}) collective-permute-start(bf16[4,96,512]{2,1,0:T(8,128)(2,1)S(1)} %pad_maximum_fusion.3), channel_id=1, source_target_pairs={{0,2},{1,5},{2,0},{3,7},{4,6},{5,1},{6,4},{7,3},{8,10},{9,13},{10,... | collective-permute-start | bytes 1179656 | tf_op jit(solution)/shard_map/ppermute | solution.py:46
  94.4 9.4 %collective-permute-start.27 = (bf16[8,128,512]{2,1,0:T(8,128)(2,1)S(1)}, bf16[8,128,512]{2,1,0:T(8,128)(2,1)S(1)}, u32[]{:S(2)}, u32[]{:S(2)}) collective-permute-start(bf16[8,128,512]{2,1,0:T(8,128)(2,1)S(1)} %pad_maximum_fusion), channel_id=1, source_target_pairs={{0,1},{1,0},{2,3},{3,2},{4,5},{5,4},{6,7},{7,6},{8,9},{9,8},{10,11... | collective-permute-start | bytes 3145736 | tf_op jit(solution)/shard_map/ppermute | solution.py:46
  99.6 4.4 %collective-permute-start.26 = (bf16[8,96,512]{2,1,0:T(8,128)(2,1)S(1)}, bf16[8,96,512]{2,1,0:T(8,128)(2,1)S(1)}, u32[]{:S(2)}, u32[]{:S(2)}) collective-permute-start(bf16[8,96,512]{2,1,0:T(8,128)(2,1)S(1)} %pad_maximum_fusion.1), channel_id=1, source_target_pairs={{0,1},{1,0},{2,3},{3,2},{4,5},{5,4},{6,7},{7,6},{8,9},{9,8},{10,11... | collective-permute-start | bytes 2359304 | tf_op jit(solution)/shard_map/ppermute | solution.py:46
  (8 other events, 7.7 us)
where the time goes:
time: 106 us
  starting transfers between devices  43 us (41%)
  Pallas kernels  28.9 us (27%)
  waiting for transfers between devices  21.8 us (21%)
  local copies, waits for them, and re-layouts  5.54 us (5%)
  other arithmetic  5.37 us (5%)
  between operations  1.21 us (1%)
    ppermute x18, starting transfers between devices, send_along(): return lax.ppermute(block, AXES, route(place, mask_of))  32.5 us
    pallas_call x3, Pallas kernels, call(): pl.pallas_call(kernel, out_shape=[jax.ShapeDtypeStruct(shape, kind) for s...  28.9 us
    ppermute x18, waiting for transfers between devices, send_along(): return lax.ppermute(block, AXES, route(place, mask_of))  21.6 us
    unnamed x24, local copies, waits for them, and re-layouts  3.31 us
    ppermute x1, starting transfers between devices, local(): inner = lax.ppermute(jnp.where(place.even, bottom, top), AXES, place.pairs)  3 us
  transfers between devices with their start and end apart: 28, of which 11 were waited for; matrix products, arithmetic and copies ran while one was open for 6% of the time, Pallas kernels for 12%

commit v1 on v0

--- a/solution.py
+++ b/solution.py
@@ -108,12 +108,14 @@
         return after(send_along(self.place, buf, lambda i: 1), *ties)
 
 
-def halves(core, own, other, axis):
+def first_half(core, own, axis):
     size = own.shape[axis]
-    shape = own.shape[:axis] + (2 * size,) + own.shape[axis + 1 :]
-    out = jnp.zeros(shape, own.dtype)
-    out = lax.dynamic_update_slice_in_dim(out, own, core * size, axis)
-    return lax.dynamic_update_slice_in_dim(out, other, (1 - core) * size, axis)
+    out = jnp.zeros(own.shape[:axis] + (2 * size,) + own.shape[axis + 1 :], own.dtype)
+    return lax.dynamic_update_slice_in_dim(out, own, core * size, axis)
+
+
+def second_half(core, out, other, axis):
+    return lax.dynamic_update_slice_in_dim(out, other, (1 - core) * other.shape[axis], axis)
 
 
 OVER_ROWS = (((0,), (0,)), ((), ()))
@@ -131,27 +133,6 @@
         return carry
 
     lax.fori_loop(0, count // size, step, 0)
-
-
-def band_kernel(reach_ref, taps, bands, lines, *, cols):
-    basis, rows, _, count = taps.shape
-    width = lines.shape[2]
-    away = jnp.abs(lax.broadcasted_iota(jnp.int32, (3, count), 1) - (count - 1) // 2)
-    lines[...] = jnp.zeros(lines.shape, lines.dtype)
-
-    def one_row(r, carry):
-        inside = away <= reach_ref[r]
-        for k in range(basis):
-            lines[k, :, :count] = jnp.where(inside, taps[k, r].astype(jnp.float32), 0.0)
-            for d in range(3):
-                line = jnp.broadcast_to(lines[k, pl.ds(d, 1)], (cols, width))
-                band = pltpu.roll(line, 0, 1, stride=1, stride_axis=0)
-                bands[r, k * cols : (k + 1) * cols, d * width : (d + 1) * width] = band.astype(
-                    bands.dtype
-                )
-        return carry
-
-    lax.fori_loop(0, rows, one_row, 0)
 
 
 def started(pairs, sems, first=0):
@@ -167,10 +148,10 @@
 
 
 def main_kernel(
-    core_ref, field, north, south, west, east, corners_west, corners_east, bands_in, mix_in,
-    up_in, down_in, cot_in,
-    block_out, hg_out, mlp_send_out, mlp_keep_out, mix_send_out, mix_keep_out,
-    ext, bands, mix, up, down, cot, feats, hidden, act, pre_grad, hg, block, turned, pre_a,
+    core_ref, reach_ref, field, north, south, west, east, corners_west, corners_east, taps_in,
+    mix_in, up_in, down_in, cot_in,
+    block_out, hg_out, bands_out, mlp_send_out, mlp_keep_out, mix_send_out, mix_keep_out,
+    ext, taps, lines, bands, mix, up, down, cot, feats, hidden, act, pre_grad, hg, block, turned, pre_a,
     pre_b, ag_a, ag_b, mlp_send, mlp_keep, mix_send, mix_keep, sems
 ):
     core = core_ref[0]
@@ -181,6 +162,7 @@
     half_units, half_channels = up.shape[1] // 2, channels // 2
     body, inner = pl.ds(1, rows), pl.ds(reach, cols)
     begin, end = pl.ds(0, reach), pl.ds(reach + cols, reach)
+    tap_load = started([(taps_in, taps)], sems, 9)
     loads = started(
         [
             (field, ext.at[body, inner]),
@@ -195,13 +177,27 @@
         ],
         sems,
     )
-    band_loads = started([(bands_in.at[r], bands.at[r]) for r in range(rows)], sems, 9)
-    late = 9 + rows
+    late = 10
     weights = started([(mix_in, mix), (up_in, up), (down_in, down), (cot_in, cot)], sems, late)
+    finish(tap_load)
+
+    count, width = taps.shape[3], lines.shape[3]
+    away = jnp.abs(lax.broadcasted_iota(jnp.int32, (3, count), 1) - (count - 1) // 2)
+    lines[...] = jnp.zeros(lines.shape, lines.dtype)
+    for r in range(rows):
+        inside = away <= reach_ref[r]
+        for k in range(basis):
+            lines[r, k, :, :count] = jnp.where(inside, taps[k, r].astype(jnp.float32), 0.0)
+            for d in range(3):
+                line = jnp.broadcast_to(lines[r, k, d : d + 1], (cols, width))
+                band = pltpu.roll(line, 0, 1, stride=1, stride_axis=0)
+                bands[r, k * cols : (k + 1) * cols, d * width : (d + 1) * width] = band.astype(
+                    bands.dtype
+                )
+    stores = started([(bands, bands_out)], sems, late + 12)
     finish(loads)
 
     for r in range(rows):
-        finish(band_loads[r : r + 1])
         window = ext[r : r + 3].reshape(3 * ext.shape[1], channels)
         out = dot(bands[r], window).astype(feats.dtype)
         at = pl.ds(r * cols, cols)
@@ -248,7 +244,7 @@
         out[half_units:] = dot(turned[...], pre_grad[:, at]).astype(out.dtype)
 
     mlp_sums(1 - core, mlp_send)
-    stores = started([(mlp_send, mlp_send_out)], sems, late + 4)
+    stores += started([(mlp_send, mlp_send_out)], sems, late + 4)
     mlp_sums(core, mlp_keep)
     stores += started([(mlp_keep, mlp_keep_out)], sems, late + 5)
 
@@ -359,17 +355,6 @@
     gemm = 2 * points * channels * hidden_units
     mix_gemm = 2 * points * channels * channels * basis_count
     band_gemm = 2 * lat_rows * basis_count * lon_cols * 3 * width * channels
-    (bands,) = call(
-        functools.partial(band_kernel, cols=lon_cols),
-        (row_reach, kernel_taps),
-        [smem, vmem],
-        [(band_shape, low)],
-        [vmem],
-        [pltpu.VMEM((basis_count, 3, width), full)],
-        0,
-        2 * points * hidden_units * 4,
-    )
-
     half_units, half_channels = hidden_units // 2, channels // 2
     mlp_half = (half_units + channels, channels)
     mix_half = (basis_count, half_channels, channels)
@@ -377,17 +362,19 @@
     core = place.flat % 2
     core_op = core[None].astype(jnp.int32)
     sized = (points // 5, hidden_units)
-    block_out, hidden_grad, mlp_send, mlp_keep, mix_send, mix_keep = call(
+    block_out, hidden_grad, bands, mlp_send, mlp_keep, mix_send, mix_keep = call(
         main_kernel,
         (
-            core_op, field_in, north, south, west, east, corners_west, corners_east, bands,
-            mix_weight, up_weight, down_weight, cot,
+            core_op, row_reach, field_in, north, south, west, east, corners_west, corners_east,
+            kernel_taps, mix_weight, up_weight, down_weight, cot,
         ),
-        [smem] + [anywhere] * 12,
-        [(big, low), (big, low), (mlp_half, low), (mlp_half, low), (mix_half, low), (mix_half, low)],
-        [anywhere] * 6,
+        [smem] * 2 + [anywhere] * 12,
+        [(big, low), (big, low), (band_shape, low), (mlp_half, low), (mlp_half, low), (mix_half, low), (mix_half, low)],
+        [anywhere] * 7,
         [
             pltpu.VMEM((lat_rows + 2, width, channels), low),
+            pltpu.VMEM(kernel_taps.shape, low),
+            pltpu.VMEM((lat_rows, basis_count, 3, width), full),
             pltpu.VMEM(band_shape, low),
             pltpu.VMEM(mix_weight.shape, low),
             pltpu.VMEM(up_weight.shape, low),
@@ -408,7 +395,7 @@
             pltpu.VMEM(mlp_half, low),
             pltpu.VMEM(mix_half, low),
             pltpu.VMEM(mix_half, low),
-            pltpu.SemaphoreType.DMA((21 + lat_rows,)),
+            pltpu.SemaphoreType.DMA((23,)),
         ],
         band_gemm + 2 * mix_gemm + 6 * gemm,
         7 * points * hidden_units * 2,
@@ -437,6 +424,34 @@
             3 * points * hidden_units * 4,
         )
 
+    def rim_blocks(rims, from_east, from_west):
+        corner_east = jnp.stack([from_east[0], from_east[lat_rows + 1]]).astype(full)
+        corner_west = jnp.stack([from_west[0], from_west[lat_rows + 1]]).astype(full)
+        rims = rims.at[:, lon_cols - reach :].add(corner_east)
+        rims = rims.at[:, :reach].add(corner_west).astype(low)
+        return jnp.where(place.even, rims[1], rims[0]), jnp.where(place.even, rims[0], rims[1])
+
+    def beyond(near, far):
+        near = lax.ppermute(near, AXES, place.pairs)
+        far = lax.ppermute(far, AXES, place.bridges)
+        return near, far
+
+    def whole_field(inner, from_east, from_west, near, far):
+        middle = lon_cols - 2 * reach
+        ends = jnp.stack([jnp.where(place.even, far, near), jnp.where(place.even, near, far)])
+        ends = ends.astype(full)
+        sides = jnp.concatenate(
+            [
+                from_west[1 : lat_rows + 1].astype(full),
+                jnp.zeros((lat_rows, middle, channels), full),
+                from_east[1 : lat_rows + 1].astype(full),
+            ],
+            axis=1,
+        )
+        nothing = jnp.zeros((lat_rows - 2, lon_cols, channels), full)
+        ends = jnp.concatenate([ends[:1], nothing, ends[1:]])
+        return (inner.astype(full) + sides + ends).astype(low)
+
     grad_scale = 1.0 / math.sqrt(points * place.count)
     if place.count == 32:
         ring = Ring(place)
@@ -459,29 +474,42 @@
         mix_out = ring.leaving(mix, ring.near)
         mlp = ring.step(mlp, mlp_out, near_mask, ring.near, mix_out).astype(low)
         mix = ring.step(mix, mix_out, near_mask, ring.near, mlp).astype(low)
-        mlp_piece = ring.far_step(mlp, grad_scale, mix)
-        mix_piece = ring.far_step(mix, grad_scale, mlp_piece)
-        mlp = ring.gather_near(mlp_piece)
-        mix = ring.gather_near(mix_piece, mlp)
-        mlp = ring.gather_second(mlp, mix)
-        from_east, from_west, _ = lax.optimization_barrier((from_east, from_west, mlp))
+        from_east, from_west, _ = lax.optimization_barrier((from_east, from_west, mix))
+        top_rim, bottom_rim = rim_blocks(rims, from_east, from_west)
+        mlp = ring.far_step(mlp, grad_scale, mix)
+        mix = ring.far_step(mix, grad_scale, mlp, top_rim, bottom_rim)
+        from_north, from_south = beyond(top_rim, bottom_rim)
+        mlp = ring.gather_near(mlp)
+        mix = ring.gather_near(mix, mlp)
+        from_north, from_south, _ = lax.optimization_barrier((from_north, from_south, mlp))
+        mlp = ring.gather_second(mlp, mix, from_north, from_south)
         mix = ring.gather_second(mix, mlp)
         mlp = ring.gather_first(mlp, mix)
-        mix = ring.gather_first(mix, mlp)
-        last_block = mix
-        mlp_other = ring.gather_core(mlp, mix).reshape(mlp_half)
-        mlp = mlp.reshape(mlp_half)
-        down_out = halves(core, mlp[:half_units], mlp_other[:half_units], 0)
-        up_out = halves(core, mlp[half_units:], mlp_other[half_units:], 1)
-        mix_other, down_out, up_out = lax.optimization_barrier(
-            (ring.gather_core(mix).reshape(mix_half), down_out, up_out)
+        mlp_other = ring.gather_core(mlp)
+        grad_field = whole_field(inner, from_east, from_west, from_north, from_south)
+        own = mlp.reshape(mlp_half)
+        down_out = first_half(core, own[:half_units], 0)
+        up_out = first_half(core, own[half_units:], 1)
+        got = send_along(place, mix, first_mask)
+        got, grad_field, down_out, up_out, _ = lax.optimization_barrier(
+            (got, grad_field, down_out, up_out, mlp)
         )
-        mix_out = halves(core, mix.reshape(mix_half), mix_other, 1)
+        mix = joined(ring.first, mix, got)
+        mix_other = ring.gather_core(mix)
+        mix_out = first_half(core, mix.reshape(mix_half), 1)
+        mlp_other, mix_out, _ = lax.optimization_barrier((mlp_other, mix_out, mix))
+        mlp_other = mlp_other.reshape(mlp_half)
+        down_out = second_half(core, down_out, mlp_other[:half_units], 0)
+        up_out = second_half(core, up_out, mlp_other[half_units:], 1)
+        mix_other, down_out, up_out = lax.optimization_barrier((mix_other, down_out, up_out))
+        mix_out = second_half(core, mix_out, mix_other.reshape(mix_half), 1)
     else:
-        last_block = mix_keep
         inner, rims, to_west, to_east = adjoint_of(hidden_grad)
         from_east = lax.ppermute(to_west, "lon", place.west)
         from_west = lax.ppermute(to_east, "lon", place.east)
+
+        rim_pair = rim_blocks(rims, from_east, from_west)
+        grad_field = whole_field(inner, from_east, from_west, *beyond(*rim_pair))
 
         def whole(keep, send):
             keep, send = keep.astype(full)[None], send.astype(full)[None]
@@ -494,28 +522,6 @@
         up_out = jnp.concatenate([mlp_sum[0, half_units:], mlp_sum[1, half_units:]], axis=1)
         mix_out = mix_sum.swapaxes(0, 1).reshape(mix_weight.shape)
 
-    corner_east = jnp.stack([from_east[0], from_east[lat_rows + 1]]).astype(full)
-    corner_west = jnp.stack([from_west[0], from_west[lat_rows + 1]]).astype(full)
-    rims = rims.at[:, lon_cols - reach :].add(corner_east)
-    rims = rims.at[:, :reach].add(corner_west).astype(low)
-    near = lax.ppermute(jnp.where(place.even, rims[1], rims[0]), AXES, place.pairs)
-    far = lax.ppermute(jnp.where(place.even, rims[0], rims[1]), AXES, place.bridges)
-    near, far, _ = lax.optimization_barrier((near, far, last_block))
-    middle = lon_cols - 2 * reach
-    beyond = jnp.stack(
-        [jnp.where(place.even, far, near), jnp.where(place.even, near, far)]
-    ).astype(full)
-    sides = jnp.concatenate(
-        [
-            from_west[1 : lat_rows + 1].astype(full),
-            jnp.zeros((lat_rows, middle, channels), full),
-            from_east[1 : lat_rows + 1].astype(full),
-        ],
-        axis=1,
-    )
-    nothing = jnp.zeros((lat_rows - 2, lon_cols, channels), full)
-    ends = jnp.concatenate([beyond[:1], nothing, beyond[1:]])
-    grad_field = (inner.astype(full) + sides + ends).astype(low)
     return (block_out.reshape(field_in.shape), grad_field, mix_out, up_out, down_out)
 
 

time: 106 us -> 103 us (0.972)
  starting transfers between devices: 43 us -> 35.6 us
  waiting for transfers between devices: 21.8 us -> 28.6 us
  Pallas kernels: 28.9 us -> 24.4 us
  local copies, waits for them, and re-layouts: 5.54 us -> 7.45 us
    ppermute x18, starting transfers between devices: 32.5 us -> 25.1 us  [send_along(): return lax.ppermute(block, AXES, route(place, mask_of))]
    pallas_call x3 -> x2, Pallas kernels: 28.9 us -> 24.4 us  [call(): pl.pallas_call(kernel, out_shape=[jax.ShapeDtypeStruct(shape, kind) for s...]
    ppermute x18, waiting for transfers between devices: 21.6 us -> 24.4 us  [send_along(): return lax.ppermute(block, AXES, route(place, mask_of))]
    ppermute x1, waiting for transfers between devices: 0.01 us -> 2.54 us  [local(): corners_east = lax.ppermute(corners, 'lon', place.west)]
    ppermute x1, starting transfers between devices: 1.52 us -> 3.03 us  [local(): lax.ppermute(jnp.where(place.even, top, bottom), AXES, place.bridges)]
    ppermute x1, starting transfers between devices: 3 us -> 1.52 us  [local(): inner = lax.ppermute(jnp.where(place.even, bottom, top), AXES, place.pairs)]
    dynamic_update_slice x6, local copies, waits for them, and re-layouts: 0.35 us -> 1.48 us  [the longest x3 1.3 us: second_half(): lax.dynamic_update_slice_in_dim(out, other, (1 - core) * other.shape[axis...]
    ppermute x2, starting transfers between devices: 1.27 us -> 2.36 us  [the longest x1 1.57 us: beyond(): near = lax.ppermute(near, AXES, place.pairs)]
  transfers between devices with their start and end apart: 28 -> 28, of which waited for: 11 -> 14; matrix products, arithmetic and copies ran while one was open for 6% -> 6% of each run, Pallas kernels for 12% -> 8%
where the time goes in v1:
time: 103 us
  starting transfers between devices  35.6 us (35%)
  waiting for transfers between devices  28.6 us (28%)
  Pallas kernels  24.4 us (24%)
  local copies, waits for them, and re-layouts  7.45 us (7%)
  other arithmetic  5.37 us (5%)
  between operations  1.29 us (1%)
    ppermute x18, starting transfers between devices, send_along(): return lax.ppermute(block, AXES, route(place, mask_of))  25.1 us
    pallas_call x2, Pallas kernels, call(): pl.pallas_call(kernel, out_shape=[jax.ShapeDtypeStruct(shape, kind) for s...  24.4 us
    ppermute x18, waiting for transfers between devices, send_along(): return lax.ppermute(block, AXES, route(place, mask_of))  24.4 us
    unnamed x32, local copies, waits for them, and re-layouts  4.13 us
    ppermute x1, starting transfers between devices, local(): lax.ppermute(jnp.where(place.even, top, bottom), AXES, place.bridges)  3.03 us
    ppermute x1, waiting for transfers between devices, local(): corners_east = lax.ppermute(corners, 'lon', place.west)  2.54 us
  transfers between devices with their start and end apart: 28, of which 14 were waited for; matrix products, arithmetic and copies ran while one was open for 6% of the time, Pallas kernels for 8%

profile of v1, /device:TPU:0, one launch (start us, length us, event | category | flops | bytes accessed | tf_op | source)
XLA Modules:
  0.0 102.7 jit_solution(17693722502746061867)
XLA Ops:
  1.6 3.0 %collective-permute-start = (bf16[96,512]{1,0:T(8,128)(2,1)S(1)}, bf16[96,512]{1,0:T(8,128)(2,1)S(1)}, u32[]{:S(2)}, u32[]{:S(2)}) collective-permute-start(bf16[96,512]{1,0:T(8,128)(2,1)S(1)} %get-tuple-element.110), channel_id=1, source_target_pairs={{0,2},{1,3},{2,0},{3,1},{4,8},{5,9},{6,10},{7,11},{8,4},{9,5},{10,... | collective-permute-start | bytes 294920 | tf_op jit(solution)/shard_map/ppermute | solution.py:339
  4.6 1.5 %collective-permute-start.1 = (bf16[96,512]{1,0:T(8,128)(2,1)S(1)}, bf16[96,512]{1,0:T(8,128)(2,1)S(1)}, u32[]{:S(2)}, u32[]{:S(2)}) collective-permute-start(bf16[96,512]{1,0:T(8,128)(2,1)S(1)} %get-tuple-element.109), channel_id=1, source_target_pairs={{0,4},{1,5},{2,6},{3,7},{4,0},{5,1},{6,2},{7,3},{8,12},{9,13},{10,... | collective-permute-start | bytes 294920 | tf_op jit(solution)/shard_map/ppermute | solution.py:338
  6.2 1.0 fusion.13
  7.2 1.7 %collective-permute-start.3 = (bf16[10,16,512]{2,1,0:T(8,128)(2,1)S(1)}, bf16[10,16,512]{2,1,0:T(8,128)(2,1)S(1)}, u32[]{:S(2)}, u32[]{:S(2)}) collective-permute-start(bf16[10,16,512]{2,1,0:T(8,128)(2,1)S(1)} %get-tuple-element.107), channel_id=1, source_target_pairs={{1,0},{2,1},{3,2},{0,3},{5,4},{6,5},{7,6},{4,7},{9,8},{10,9},{11,1... | collective-permute-start | bytes 491528 | tf_op jit(solution)/shard_map/ppermute | solution.py:341
  9.7 1.2 %collective-permute-start.5 = (bf16[2,16,512]{2,1,0:T(8,128)(2,1)S(1)}, bf16[2,16,512]{2,1,0:T(8,128)(2,1)S(1)}, u32[]{:S(2)}, u32[]{:S(2)}) collective-permute-start(bf16[2,16,512]{2,1,0:T(8,128)(2,1)S(1)} %pad_maximum_fusion.7), channel_id=1, source_target_pairs={{1,0},{2,1},{3,2},{0,3},{5,4},{6,5},{7,6},{4,7},{9,8},{10,9},{11,1... | collective-permute-start | bytes 98312 | tf_op jit(solution)/shard_map/ppermute | solution.py:347
  10.9 2.5 %collective-permute-done.5.corners_east = bf16[2,16,512]{2,1,0:T(8,128)(2,1)S(1)} collective-permute-done((bf16[2,16,512]{2,1,0:T(8,128)(2,1)S(1)}, bf16[2,16,512]{2,1,0:T(8,128)(2,1)S(1)}, u32[]{:S(2)}, u32[]{:S(2)}) %collective-permute-start.5) | collective-permute-done | bytes 32800 | tf_op jit(solution)/shard_map/ppermute | solution.py:347
  13.5 1.0 collective-permute-done.4.corners_west
  15.2 15.7 %shard_map.110 = (bf16[960,512]{1,0:T(8,128)(2,1)}, bf16[960,512]{1,0:T(8,128)(2,1)}, bf16[10,288,384]{2,1,0:T(8,128)(2,1)}, bf16[1024,512]{1,0:T(8,128)(2,1)}, ...) custom-call(s32[1]{0:T(128)} %bitcast.core_ref, s32[10]{0:T(128)} %reach_ref.1, ...), custom_call_target="tpu_custom_call" | custom-call | flops 10192158720 | bytes 13762560 | tf_op jit(solution)/shard_map/pallas_call | solution.py:318
  31.7 2.2 %collective-permute-done.8 = bf16[2,2,2,128,512]{4,3,2,1,0:T(8,128)(2,1)S(1)} collective-permute-done((bf16[2,2,2,128,512]{4,3,2,1,0:T(8,128)(2,1)}, bf16[2,2,2,128,512]{4,3,2,1,0:T(8,128)(2,1)S(1)}, u32[]{:S(2)}, u32[]{:S(2)}) %collective-permute-start.8) | collective-permute-done | bytes 1048608 | tf_op jit(solution)/shard_map/ppermute | solution.py:46
  33.9 1.6 %convert_add_fusion = f32[2,2,2,128,512]{4,3,2,1,0:T(8,128)S(1)} fusion(bf16[2,2,2,128,512]{4,3,2,1,0:T(8,128)(2,1)} %bitcast.73, bf16[2,2,2,128,512]{4,3,2,1,0:T(8,128)(2,1)S(1)} %collective-permute-done.8), kind=kLoop, calls=%fused_computation | loop fusion | flops 1572864 | bytes 4194304 | tf_op jit(solution)/shard_map/add | solution.py:84
  36.9 1.2 %collective-permute-start.7 = (bf16[2,2,96,512]{3,2,1,0:T(8,128)(2,1)S(1)}, bf16[2,2,96,512]{3,2,1,0:T(8,128)(2,1)S(1)}, u32[]{:S(2)}, u32[]{:S(2)}) collective-permute-start(bf16[2,2,96,512]{3,2,1,0:T(8,128)(2,1)S(1)} %fusion.3), channel_id=1, source_target_pairs={{0,2},{1,5},{2,0},{3,7},{4,6},{5,1},{6,4},{7,3},{8,10},{9,13},{10,... | collective-permute-start | bytes 1179656 | tf_op jit(solution)/shard_map/ppermute | solution.py:46
  38.0 8.7 %shard_map.111 = (bf16[10,96,512]{2,1,0:T(8,128)(2,1)}, f32[2,96,512]{2,1,0:T(8,128)}, bf16[12,16,512]{2,1,0:T(8,128)(2,1)}, bf16[12,16,512]{2,1,0:T(8,128)(2,1)}) custom-call(bf16[960,512]{1,0:T(8,128)(2,1)} %get-tuple-element.72.hg_in, bf16[3,512,512]{2,1,0:T(8,128)(2,1)} %mix_in.3, bf16[10,288,384]{2,1,0:T(8,128)(2,1)} %get-tuple-element.73.bands_in), custom_call_target="tpu_custom_call" | custom-call | flops 2642411520 | bytes 11796480 | tf_op jit(solution)/shard_map/pallas_call | solution.py:318
  47.6 2.3 %collective-permute-start.11 = (bf16[2,128,512]{2,1,0:T(8,128)(2,1)S(1)}, bf16[2,128,512]{2,1,0:T(8,128)(2,1)S(1)}, u32[]{:S(2)}, u32[]{:S(2)}) collective-permute-start(bf16[2,128,512]{2,1,0:T(8,128)(2,1)S(1)} %fusion.4), channel_id=1, source_target_pairs={{0,4},{1,3},{2,6},{3,1},{4,0},{5,7},{6,2},{7,5},{8,12},{9,11},{10,... | collective-permute-start | bytes 786440 | tf_op jit(solution)/shard_map/ppermute | solution.py:46
  50.0 1.5 %collective-permute-start.10 = (bf16[2,96,512]{2,1,0:T(8,128)(2,1)S(1)}, bf16[2,96,512]{2,1,0:T(8,128)(2,1)S(1)}, u32[]{:S(2)}, u32[]{:S(2)}) collective-permute-start(bf16[2,96,512]{2,1,0:T(8,128)(2,1)S(1)} %fusion.6), channel_id=1, source_target_pairs={{0,4},{1,3},{2,6},{3,1},{4,0},{5,7},{6,2},{7,5},{8,12},{9,11},{10,... | collective-permute-start | bytes 589832 | tf_op jit(solution)/shard_map/ppermute | solution.py:46
  51.5 2.7 %collective-permute-done.11 = bf16[2,128,512]{2,1,0:T(8,128)(2,1)S(1)} collective-permute-done((bf16[2,128,512]{2,1,0:T(8,128)(2,1)S(1)}, bf16[2,128,512]{2,1,0:T(8,128)(2,1)S(1)}, u32[]{:S(2)}, u32[]{:S(2)}) %collective-permute-start.11) | collective-permute-done | bytes 262176 | tf_op jit(solution)/shard_map/ppermute | solution.py:46
  54.3 2.2 %collective-permute-start.13 = (bf16[128,512]{1,0:T(8,128)(2,1)S(1)}, bf16[128,512]{1,0:T(8,128)(2,1)S(1)}, u32[]{:S(2)}, u32[]{:S(2)}) collective-permute-start(bf16[128,512]{1,0:T(8,128)(2,1)S(1)} %fusion.8), channel_id=1, source_target_pairs={{0,8},{1,9},{2,10},{3,11},{4,12},{5,13},{6,14},{7,15},{8,0},{9,1},... | collective-permute-start | bytes 393224 | tf_op jit(solution)/shard_map/ppermute | solution.py:46
  56.6 2.0 %collective-permute-start.12 = (bf16[96,512]{1,0:T(8,128)(2,1)S(1)}, bf16[96,512]{1,0:T(8,128)(2,1)S(1)}, u32[]{:S(2)}, u32[]{:S(2)}) collective-permute-start(bf16[96,512]{1,0:T(8,128)(2,1)S(1)} %fusion.9), channel_id=1, source_target_pairs={{0,8},{1,9},{2,10},{3,11},{4,12},{5,13},{6,14},{7,15},{8,0},{9,1},... | collective-permute-start | bytes 294920 | tf_op jit(solution)/shard_map/ppermute | solution.py:46
  59.5 3.1 %collective-permute-start.15 = (bf16[128,512]{1,0:T(8,128)(2,1)S(1)}, bf16[128,512]{1,0:T(8,128)(2,1)S(1)}, u32[]{:S(2)}, u32[]{:S(2)}) collective-permute-start(bf16[128,512]{1,0:T(8,128)(2,1)S(1)} %fusion.5), channel_id=1, source_target_pairs={{0,16},{1,17},{2,18},{3,19},{4,20},{5,21},{6,22},{7,23},{8,24},{9,... | collective-permute-start | bytes 393224 | tf_op jit(solution)/shard_map/ppermute | solution.py:46
  62.6 2.7 %collective-permute-start.14 = (bf16[96,512]{1,0:T(8,128)(2,1)S(1)}, bf16[96,512]{1,0:T(8,128)(2,1)S(1)}, u32[]{:S(2)}, u32[]{:S(2)}) collective-permute-start(bf16[96,512]{1,0:T(8,128)(2,1)S(1)} %fusion.7), channel_id=1, source_target_pairs={{0,16},{1,17},{2,18},{3,19},{4,20},{5,21},{6,22},{7,23},{8,24},{9,... | collective-permute-start | bytes 294920 | tf_op jit(solution)/shard_map/ppermute | solution.py:46
  65.4 1.6 %collective-permute-start.22 = (bf16[96,512]{1,0:T(8,128)(2,1)S(1)}, bf16[96,512]{1,0:T(8,128)(2,1)S(1)}, u32[]{:S(2)}, u32[]{:S(2)}) collective-permute-start(bf16[96,512]{1,0:T(8,128)(2,1)S(1)} %get-tuple-element.126), channel_id=1, source_target_pairs={{0,4},{1,5},{2,6},{3,7},{4,0},{5,1},{6,2},{7,3},{8,12},{9,13},{10,... | collective-permute-start | bytes 294920 | tf_op jit(solution)/shard_map/ppermute | solution.py:435
  67.9 4.6 %collective-permute-start.19 = (bf16[1,128,512]{2,1,0:T(8,128)(2,1)S(1)}, bf16[1,128,512]{2,1,0:T(8,128)(2,1)S(1)}, u32[]{:S(2)}, u32[]{:S(2)}) collective-permute-start(bf16[1,128,512]{2,1,0:T(8,128)(2,1)S(1)} %bitcast.75), channel_id=1, source_target_pairs={{0,8},{1,9},{2,10},{3,11},{4,12},{5,13},{6,14},{7,15},{8,0},{9,1},... | collective-permute-start | bytes 393224 | tf_op jit(solution)/shard_map/ppermute | solution.py:46
  72.8 1.8 %collective-permute-start.18 = (bf16[1,96,512]{2,1,0:T(8,128)(2,1)S(1)}, bf16[1,96,512]{2,1,0:T(8,128)(2,1)S(1)}, u32[]{:S(2)}, u32[]{:S(2)}) collective-permute-start(bf16[1,96,512]{2,1,0:T(8,128)(2,1)S(1)} %fusion.10), channel_id=1, source_target_pairs={{0,8},{1,9},{2,10},{3,11},{4,12},{5,13},{6,14},{7,15},{8,0},{9,1},... | collective-permute-start | bytes 294920 | tf_op jit(solution)/shard_map/ppermute | solution.py:46
  74.6 3.1 %collective-permute-done.19 = bf16[1,128,512]{2,1,0:T(8,128)(2,1)S(1)} collective-permute-done((bf16[1,128,512]{2,1,0:T(8,128)(2,1)S(1)}, bf16[1,128,512]{2,1,0:T(8,128)(2,1)S(1)}, u32[]{:S(2)}, u32[]{:S(2)}) %collective-permute-start.19) | collective-permute-done | bytes 131104 | tf_op jit(solution)/shard_map/ppermute | solution.py:46
  77.9 1.9 %collective-permute-done.18 = bf16[1,96,512]{2,1,0:T(8,128)(2,1)S(1)} collective-permute-done((bf16[1,96,512]{2,1,0:T(8,128)(2,1)S(1)}, bf16[1,96,512]{2,1,0:T(8,128)(2,1)S(1)}, u32[]{:S(2)}, u32[]{:S(2)}) %collective-permute-start.18) | collective-permute-done | bytes 98336 | tf_op jit(solution)/shard_map/ppermute | solution.py:46
  80.3 3.9 %collective-permute-done.21 = bf16[2,128,512]{2,1,0:T(8,128)(2,1)S(1)} collective-permute-done((bf16[2,128,512]{2,1,0:T(8,128)(2,1)S(1)}, bf16[2,128,512]{2,1,0:T(8,128)(2,1)S(1)}, u32[]{:S(2)}, u32[]{:S(2)}) %collective-permute-start.21) | collective-permute-done | bytes 262176 | tf_op jit(solution)/shard_map/ppermute | solution.py:46
  85.2 1.1 %collective-permute-done.20 = bf16[2,96,512]{2,1,0:T(8,128)(2,1)S(1)} collective-permute-done((bf16[2,96,512]{2,1,0:T(8,128)(2,1)S(1)}, bf16[2,96,512]{2,1,0:T(8,128)(2,1)S(1)}, u32[]{:S(2)}, u32[]{:S(2)}) %collective-permute-start.20) | collective-permute-done | bytes 196640 | tf_op jit(solution)/shard_map/ppermute | solution.py:46
  87.2 6.3 %collective-permute-done.25 = bf16[4,128,512]{2,1,0:T(8,128)(2,1)S(1)} collective-permute-done((bf16[4,128,512]{2,1,0:T(8,128)(2,1)S(1)}, bf16[4,128,512]{2,1,0:T(8,128)(2,1)S(1)}, u32[]{:S(2)}, u32[]{:S(2)}) %collective-permute-start.25) | collective-permute-done | bytes 524320 | tf_op jit(solution)/shard_map/ppermute | solution.py:46
  93.8 1.3 %fusion.1 = bf16[10,96,512]{2,1,0:T(8,128)(2,1)} fusion(f32[10,16,512]{2,1,0:T(8,128)S(1)} %slice_convert_fusion, f32[10,16,512]{2,1,0:T(8,128)S(1)} %slice_convert_fusion.1, f32[1,96,512]{2,1,0:T(8,128)S(1)} %get-tuple-element.116, f32[1,96,512]{2,1,0:T(8,128)S(1)} %get-tuple-element.115, bf16[10,96,512]{2,1,0:T(8,128)(2,1)S(1)} %copy-done.7, ...), kind=kLoop, calls=%fused_computation.3 | loop fusion | flops 3932160 | bytes 3015080 | tf_op jit(solution)/shard_map/convert_element_type | solution.py:453
  96.4 1.3 %collective-permute-done.24 = bf16[4,96,512]{2,1,0:T(8,128)(2,1)S(1)} collective-permute-done((bf16[4,96,512]{2,1,0:T(8,128)(2,1)S(1)}, bf16[4,96,512]{2,1,0:T(8,128)(2,1)S(1)}, u32[]{:S(2)}, u32[]{:S(2)}) %collective-permute-start.24) | collective-permute-done | bytes 393248 | tf_op jit(solution)/shard_map/ppermute | solution.py:46
  98.3 1.0 %copy-done.5 = bf16[512,1024]{1,0:T(8,128)(2,1)S(1)} copy-done((bf16[512,1024]{1,0:T(8,128)(2,1)S(1)}, bf16[512,1024]{1,0:T(8,128)(2,1)}, u32[]{:S(2)}) %copy-start.5) | copy-done | bytes 1048600
  100.4 1.2 %constant_dynamic-update-slice_fusion = bf16[3,512,512]{2,1,0:T(8,128)(2,1)S(1)} fusion(bf16[3,512,512]{2,1,0:T(8,128)(2,1)S(1)} %constant_dynamic-update-slice_fusion.3, bf16[3,256,512]{2,1,0:T(8,128)(2,1)} %bitcast.36, s32[]{:T(128)S(6)} %select_n.258), kind=kLoop, calls=%fused_computation.66 | loop fusion | bytes 1572868 | tf_op jit(solution)/shard_map/dynamic_update_slice | solution.py:118
  101.6 1.1 %copy-done = bf16[3,512,512]{2,1,0:T(8,128)(2,1)} copy-done((bf16[3,512,512]{2,1,0:T(8,128)(2,1)}, bf16[3,512,512]{2,1,0:T(8,128)(2,1)S(1)}, u32[]{:S(2)}) %copy-start) | copy-done | bytes 1572888
  (118 shorter events, 13.3 us)
Async XLA Ops:
  1.6 7.4 %collective-permute-start = (bf16[96,512]{1,0:T(8,128)(2,1)S(1)}, bf16[96,512]{1,0:T(8,128)(2,1)S(1)}, u32[]{:S(2)}, u32[]{:S(2)}) collective-permute-start(bf16[96,512]{1,0:T(8,128)(2,1)S(1)} %get-tuple-element.110), channel_id=1, source_target_pairs={{0,2},{1,3},{2,0},{3,1},{4,8},{5,9},{6,10},{7,11},{8,4},{9,5},{10,... | collective-permute-start | bytes 294920 | tf_op jit(solution)/shard_map/ppermute | solution.py:339
  4.6 5.0 %collective-permute-start.1 = (bf16[96,512]{1,0:T(8,128)(2,1)S(1)}, bf16[96,512]{1,0:T(8,128)(2,1)S(1)}, u32[]{:S(2)}, u32[]{:S(2)}) collective-permute-start(bf16[96,512]{1,0:T(8,128)(2,1)S(1)} %get-tuple-element.109), channel_id=1, source_target_pairs={{0,4},{1,5},{2,6},{3,7},{4,0},{5,1},{6,2},{7,3},{8,12},{9,13},{10,... | collective-permute-start | bytes 294920 | tf_op jit(solution)/shard_map/ppermute | solution.py:338
  7.2 7.3 %collective-permute-start.2 = (bf16[10,16,512]{2,1,0:T(8,128)(2,1)S(1)}, bf16[10,16,512]{2,1,0:T(8,128)(2,1)S(1)}, u32[]{:S(2)}, u32[]{:S(2)}) collective-permute-start(bf16[10,16,512]{2,1,0:T(8,128)(2,1)S(1)} %get-tuple-element.108), channel_id=1, source_target_pairs={{0,1},{1,2},{2,3},{3,0},{4,5},{5,6},{6,7},{7,4},{8,9},{9,10},{10,1... | collective-permute-start | bytes 491528 | tf_op jit(solution)/shard_map/ppermute | solution.py:340
  7.2 7.3 %collective-permute-start.3 = (bf16[10,16,512]{2,1,0:T(8,128)(2,1)S(1)}, bf16[10,16,512]{2,1,0:T(8,128)(2,1)S(1)}, u32[]{:S(2)}, u32[]{:S(2)}) collective-permute-start(bf16[10,16,512]{2,1,0:T(8,128)(2,1)S(1)} %get-tuple-element.107), channel_id=1, source_target_pairs={{1,0},{2,1},{3,2},{0,3},{5,4},{6,5},{7,6},{4,7},{9,8},{10,9},{11,1... | collective-permute-start | bytes 491528 | tf_op jit(solution)/shard_map/ppermute | solution.py:341
  9.7 4.8 %copy-start.10 = (bf16[96,512]{1,0:T(8,128)(2,1)}, bf16[96,512]{1,0:T(8,128)(2,1)S(1)}, u32[]{:S(2)}) copy-start(bf16[96,512]{1,0:T(8,128)(2,1)S(1)} %get-tuple-element.131.south) | copy-start | bytes 294916
  9.7 4.8 %copy-start.11 = (bf16[96,512]{1,0:T(8,128)(2,1)}, bf16[96,512]{1,0:T(8,128)(2,1)S(1)}, u32[]{:S(2)}) copy-start(bf16[96,512]{1,0:T(8,128)(2,1)S(1)} %get-tuple-element.132.north) | copy-start | bytes 294916
  9.7 3.7 %collective-permute-start.5 = (bf16[2,16,512]{2,1,0:T(8,128)(2,1)S(1)}, bf16[2,16,512]{2,1,0:T(8,128)(2,1)S(1)}, u32[]{:S(2)}, u32[]{:S(2)}) collective-permute-start(bf16[2,16,512]{2,1,0:T(8,128)(2,1)S(1)} %pad_maximum_fusion.7), channel_id=1, source_target_pairs={{1,0},{2,1},{3,2},{0,3},{5,4},{6,5},{7,6},{4,7},{9,8},{10,9},{11,1... | collective-permute-start | bytes 98312 | tf_op jit(solution)/shard_map/ppermute | solution.py:347
  10.9 3.6 %collective-permute-start.4 = (bf16[2,16,512]{2,1,0:T(8,128)(2,1)S(1)}, bf16[2,16,512]{2,1,0:T(8,128)(2,1)S(1)}, u32[]{:S(2)}, u32[]{:S(2)}) collective-permute-start(bf16[2,16,512]{2,1,0:T(8,128)(2,1)S(1)} %pad_maximum_fusion.6), channel_id=1, source_target_pairs={{0,1},{1,2},{2,3},{3,0},{4,5},{5,6},{6,7},{7,4},{8,9},{9,10},{10,1... | collective-permute-start | bytes 98312 | tf_op jit(solution)/shard_map/ppermute | solution.py:345
  31.0 2.9 %collective-permute-start.8 = (bf16[2,2,2,128,512]{4,3,2,1,0:T(8,128)(2,1)}, bf16[2,2,2,128,512]{4,3,2,1,0:T(8,128)(2,1)S(1)}, u32[]{:S(2)}, u32[]{:S(2)}) collective-permute-start(bf16[2,2,2,128,512]{4,3,2,1,0:T(8,128)(2,1)} %bitcast.76), channel_id=1, source_target_pairs={{0,1},{1,0},{2,3},{3,2},{4,5},{5,4},{6,7},{7,6},{8,9},{9,8},{10,11... | collective-permute-start | bytes 3145736 | tf_op jit(solution)/shard_map/ppermute | solution.py:46
  31.1 5.5 %collective-permute-start.6 = (bf16[2,2,2,96,512]{4,3,2,1,0:T(8,128)(2,1)}, bf16[2,2,2,96,512]{4,3,2,1,0:T(8,128)(2,1)S(1)}, u32[]{:S(2)}, u32[]{:S(2)}) collective-permute-start(bf16[2,2,2,96,512]{4,3,2,1,0:T(8,128)(2,1)} %bitcast.78), channel_id=1, source_target_pairs={{0,1},{1,0},{2,3},{3,2},{4,5},{5,4},{6,7},{7,6},{8,9},{9,8},{10,11... | collective-permute-start | bytes 2359304 | tf_op jit(solution)/shard_map/ppermute | solution.py:46
  35.6 11.7 %collective-permute-start.9 = (bf16[2,2,128,512]{3,2,1,0:T(8,128)(2,1)S(1)}, bf16[2,2,128,512]{3,2,1,0:T(8,128)(2,1)S(1)}, u32[]{:S(2)}, u32[]{:S(2)}) collective-permute-start(bf16[2,2,128,512]{3,2,1,0:T(8,128)(2,1)S(1)} %fusion.2), channel_id=1, source_target_pairs={{0,2},{1,5},{2,0},{3,7},{4,6},{5,1},{6,4},{7,3},{8,10},{9,13},{10,... | collective-permute-start | bytes 1572872 | tf_op jit(solution)/shard_map/ppermute | solution.py:46
  36.9 13.0 %collective-permute-start.7 = (bf16[2,2,96,512]{3,2,1,0:T(8,128)(2,1)S(1)}, bf16[2,2,96,512]{3,2,1,0:T(8,128)(2,1)S(1)}, u32[]{:S(2)}, u32[]{:S(2)}) collective-permute-start(bf16[2,2,96,512]{3,2,1,0:T(8,128)(2,1)S(1)} %fusion.3), channel_id=1, source_target_pairs={{0,2},{1,5},{2,0},{3,7},{4,6},{5,1},{6,4},{7,3},{8,10},{9,13},{10,... | collective-permute-start | bytes 1179656 | tf_op jit(solution)/shard_map/ppermute | solution.py:46
  46.7 18.5 %collective-permute-start.16 = (bf16[12,16,512]{2,1,0:T(8,128)(2,1)}, bf16[12,16,512]{2,1,0:T(8,128)(2,1)S(1)}, u32[]{:S(2)}, u32[]{:S(2)}) collective-permute-start(bf16[12,16,512]{2,1,0:T(8,128)(2,1)} %get-tuple-element.74), channel_id=1, source_target_pairs={{1,0},{2,1},{3,2},{0,3},{5,4},{6,5},{7,6},{4,7},{9,8},{10,9},{11,1... | collective-permute-start | bytes 589832 | tf_op jit(solution)/shard_map/ppermute | solution.py:465
  47.3 18.0 %collective-permute-start.17 = (bf16[12,16,512]{2,1,0:T(8,128)(2,1)}, bf16[12,16,512]{2,1,0:T(8,128)(2,1)S(1)}, u32[]{:S(2)}, u32[]{:S(2)}) collective-permute-start(bf16[12,16,512]{2,1,0:T(8,128)(2,1)} %get-tuple-element.83), channel_id=1, source_target_pairs={{0,1},{1,2},{2,3},{3,0},{4,5},{5,6},{6,7},{7,4},{8,9},{9,10},{10,1... | collective-permute-start | bytes 589832 | tf_op jit(solution)/shard_map/ppermute | solution.py:466
  47.6 6.7 %collective-permute-start.11 = (bf16[2,128,512]{2,1,0:T(8,128)(2,1)S(1)}, bf16[2,128,512]{2,1,0:T(8,128)(2,1)S(1)}, u32[]{:S(2)}, u32[]{:S(2)}) collective-permute-start(bf16[2,128,512]{2,1,0:T(8,128)(2,1)S(1)} %fusion.4), channel_id=1, source_target_pairs={{0,4},{1,3},{2,6},{3,1},{4,0},{5,7},{6,2},{7,5},{8,12},{9,11},{10,... | collective-permute-start | bytes 786440 | tf_op jit(solution)/shard_map/ppermute | solution.py:46
  50.0 15.3 %copy-start.9 = (f32[2,96,512]{2,1,0:T(8,128)S(1)}, f32[2,96,512]{2,1,0:T(8,128)}, u32[]{:S(2)}) copy-start(f32[2,96,512]{2,1,0:T(8,128)} %get-tuple-element.82) | copy-start | bytes 1179652
  50.0 6.5 %collective-permute-start.10 = (bf16[2,96,512]{2,1,0:T(8,128)(2,1)S(1)}, bf16[2,96,512]{2,1,0:T(8,128)(2,1)S(1)}, u32[]{:S(2)}, u32[]{:S(2)}) collective-permute-start(bf16[2,96,512]{2,1,0:T(8,128)(2,1)S(1)} %fusion.6), channel_id=1, source_target_pairs={{0,4},{1,3},{2,6},{3,1},{4,0},{5,7},{6,2},{7,5},{8,12},{9,11},{10,... | collective-permute-start | bytes 589832 | tf_op jit(solution)/shard_map/ppermute | solution.py:46
  54.3 5.1 %collective-permute-start.13 = (bf16[128,512]{1,0:T(8,128)(2,1)S(1)}, bf16[128,512]{1,0:T(8,128)(2,1)S(1)}, u32[]{:S(2)}, u32[]{:S(2)}) collective-permute-start(bf16[128,512]{1,0:T(8,128)(2,1)S(1)} %fusion.8), channel_id=1, source_target_pairs={{0,8},{1,9},{2,10},{3,11},{4,12},{5,13},{6,14},{7,15},{8,0},{9,1},... | collective-permute-start | bytes 393224 | tf_op jit(solution)/shard_map/ppermute | solution.py:46
  56.6 6.0 %collective-permute-start.12 = (bf16[96,512]{1,0:T(8,128)(2,1)S(1)}, bf16[96,512]{1,0:T(8,128)(2,1)S(1)}, u32[]{:S(2)}, u32[]{:S(2)}) collective-permute-start(bf16[96,512]{1,0:T(8,128)(2,1)S(1)} %fusion.9), channel_id=1, source_target_pairs={{0,8},{1,9},{2,10},{3,11},{4,12},{5,13},{6,14},{7,15},{8,0},{9,1},... | collective-permute-start | bytes 294920 | tf_op jit(solution)/shard_map/ppermute | solution.py:46
  59.5 8.3 %collective-permute-start.15 = (bf16[128,512]{1,0:T(8,128)(2,1)S(1)}, bf16[128,512]{1,0:T(8,128)(2,1)S(1)}, u32[]{:S(2)}, u32[]{:S(2)}) collective-permute-start(bf16[128,512]{1,0:T(8,128)(2,1)S(1)} %fusion.5), channel_id=1, source_target_pairs={{0,16},{1,17},{2,18},{3,19},{4,20},{5,21},{6,22},{7,23},{8,24},{9,... | collective-permute-start | bytes 393224 | tf_op jit(solution)/shard_map/ppermute | solution.py:46
  62.6 10.1 %collective-permute-start.14 = (bf16[96,512]{1,0:T(8,128)(2,1)S(1)}, bf16[96,512]{1,0:T(8,128)(2,1)S(1)}, u32[]{:S(2)}, u32[]{:S(2)}) collective-permute-start(bf16[96,512]{1,0:T(8,128)(2,1)S(1)} %fusion.7), channel_id=1, source_target_pairs={{0,16},{1,17},{2,18},{3,19},{4,20},{5,21},{6,22},{7,23},{8,24},{9,... | collective-permute-start | bytes 294920 | tf_op jit(solution)/shard_map/ppermute | solution.py:46
  65.4 12.4 %collective-permute-start.22 = (bf16[96,512]{1,0:T(8,128)(2,1)S(1)}, bf16[96,512]{1,0:T(8,128)(2,1)S(1)}, u32[]{:S(2)}, u32[]{:S(2)}) collective-permute-start(bf16[96,512]{1,0:T(8,128)(2,1)S(1)} %get-tuple-element.126), channel_id=1, source_target_pairs={{0,4},{1,5},{2,6},{3,7},{4,0},{5,1},{6,2},{7,3},{8,12},{9,13},{10,... | collective-permute-start | bytes 294920 | tf_op jit(solution)/shard_map/ppermute | solution.py:435
  67.0 10.8 %collective-permute-start.23 = (bf16[96,512]{1,0:T(8,128)(2,1)S(1)}, bf16[96,512]{1,0:T(8,128)(2,1)S(1)}, u32[]{:S(2)}, u32[]{:S(2)}) collective-permute-start(bf16[96,512]{1,0:T(8,128)(2,1)S(1)} %get-tuple-element.125), channel_id=1, source_target_pairs={{0,2},{1,3},{2,0},{3,1},{4,8},{5,9},{6,10},{7,11},{8,4},{9,5},{10,... | collective-permute-start | bytes 294920 | tf_op jit(solution)/shard_map/ppermute | solution.py:436
  67.9 9.8 %collective-permute-start.19 = (bf16[1,128,512]{2,1,0:T(8,128)(2,1)S(1)}, bf16[1,128,512]{2,1,0:T(8,128)(2,1)S(1)}, u32[]{:S(2)}, u32[]{:S(2)}) collective-permute-start(bf16[1,128,512]{2,1,0:T(8,128)(2,1)S(1)} %bitcast.75), channel_id=1, source_target_pairs={{0,8},{1,9},{2,10},{3,11},{4,12},{5,13},{6,14},{7,15},{8,0},{9,1},... | collective-permute-start | bytes 393224 | tf_op jit(solution)/shard_map/ppermute | solution.py:46
  72.8 7.0 %collective-permute-start.18 = (bf16[1,96,512]{2,1,0:T(8,128)(2,1)S(1)}, bf16[1,96,512]{2,1,0:T(8,128)(2,1)S(1)}, u32[]{:S(2)}, u32[]{:S(2)}) collective-permute-start(bf16[1,96,512]{2,1,0:T(8,128)(2,1)S(1)} %fusion.10), channel_id=1, source_target_pairs={{0,8},{1,9},{2,10},{3,11},{4,12},{5,13},{6,14},{7,15},{8,0},{9,1},... | collective-permute-start | bytes 294920 | tf_op jit(solution)/shard_map/ppermute | solution.py:46
  77.8 6.4 %collective-permute-start.21 = (bf16[2,128,512]{2,1,0:T(8,128)(2,1)S(1)}, bf16[2,128,512]{2,1,0:T(8,128)(2,1)S(1)}, u32[]{:S(2)}, u32[]{:S(2)}) collective-permute-start(bf16[2,128,512]{2,1,0:T(8,128)(2,1)S(1)} %pad_maximum_fusion.4), channel_id=1, source_target_pairs={{0,4},{1,3},{2,6},{3,1},{4,0},{5,7},{6,2},{7,5},{8,12},{9,11},{10,... | collective-permute-start | bytes 786440 | tf_op jit(solution)/shard_map/ppermute | solution.py:46
  79.8 6.4 %collective-permute-start.20 = (bf16[2,96,512]{2,1,0:T(8,128)(2,1)S(1)}, bf16[2,96,512]{2,1,0:T(8,128)(2,1)S(1)}, u32[]{:S(2)}, u32[]{:S(2)}) collective-permute-start(bf16[2,96,512]{2,1,0:T(8,128)(2,1)S(1)} %pad_maximum_fusion.5), channel_id=1, source_target_pairs={{0,4},{1,3},{2,6},{3,1},{4,0},{5,7},{6,2},{7,5},{8,12},{9,11},{10,... | collective-permute-start | bytes 589832 | tf_op jit(solution)/shard_map/ppermute | solution.py:46
  84.3 9.2 %collective-permute-start.25 = (bf16[4,128,512]{2,1,0:T(8,128)(2,1)S(1)}, bf16[4,128,512]{2,1,0:T(8,128)(2,1)S(1)}, u32[]{:S(2)}, u32[]{:S(2)}) collective-permute-start(bf16[4,128,512]{2,1,0:T(8,128)(2,1)S(1)} %pad_maximum_fusion.2), channel_id=1, source_target_pairs={{0,2},{1,5},{2,0},{3,7},{4,6},{5,1},{6,4},{7,3},{8,10},{9,13},{10,... | collective-permute-start | bytes 1572872 | tf_op jit(solution)/shard_map/ppermute | solution.py:46
  86.4 7.4 %copy-start.7 = (bf16[10,96,512]{2,1,0:T(8,128)(2,1)S(1)}, bf16[10,96,512]{2,1,0:T(8,128)(2,1)}, u32[]{:S(2)}) copy-start(bf16[10,96,512]{2,1,0:T(8,128)(2,1)} %get-tuple-element.92) | copy-start | bytes 2949124
  86.4 11.4 %collective-permute-start.24 = (bf16[4,96,512]{2,1,0:T(8,128)(2,1)S(1)}, bf16[4,96,512]{2,1,0:T(8,128)(2,1)S(1)}, u32[]{:S(2)}, u32[]{:S(2)}) collective-permute-start(bf16[4,96,512]{2,1,0:T(8,128)(2,1)S(1)} %pad_maximum_fusion.3), channel_id=1, source_target_pairs={{0,2},{1,5},{2,0},{3,7},{4,6},{5,1},{6,4},{7,3},{8,10},{9,13},{10,... | collective-permute-start | bytes 1179656 | tf_op jit(solution)/shard_map/ppermute | solution.py:46
  93.7 4.5 %collective-permute-start.26 = (bf16[8,128,512]{2,1,0:T(8,128)(2,1)S(1)}, bf16[8,128,512]{2,1,0:T(8,128)(2,1)S(1)}, u32[]{:S(2)}, u32[]{:S(2)}) collective-permute-start(bf16[8,128,512]{2,1,0:T(8,128)(2,1)S(1)} %pad_maximum_fusion), channel_id=1, source_target_pairs={{0,1},{1,0},{2,3},{3,2},{4,5},{5,4},{6,7},{7,6},{8,9},{9,8},{10,11... | collective-permute-start | bytes 3145736 | tf_op jit(solution)/shard_map/ppermute | solution.py:46
  97.9 2.5 %collective-permute-start.27 = (bf16[8,96,512]{2,1,0:T(8,128)(2,1)S(1)}, bf16[8,96,512]{2,1,0:T(8,128)(2,1)}, u32[]{:S(2)}, u32[]{:S(2)}) collective-permute-start(bf16[8,96,512]{2,1,0:T(8,128)(2,1)S(1)} %pad_maximum_fusion.1), channel_id=1, source_target_pairs={{0,1},{1,0},{2,3},{3,2},{4,5},{5,4},{6,7},{7,6},{8,9},{9,8},{10,11... | collective-permute-start | bytes 2359304 | tf_op jit(solution)/shard_map/ppermute | solution.py:46
  (12 other events, 16.0 us)

commit v2 on v1

--- a/solution.py
+++ b/solution.py
@@ -80,11 +80,20 @@
         self.near = (place.flat // 8) % 2
 
     def to_core(self, keep, send):
-        got = send_along(self.place, send, lambda i: 1)
-        return keep.astype(jnp.float32) + got.astype(jnp.float32)
+        return keep, send_along(self.place, send, lambda i: 1)
+
+    def split(self, keep, got):
+        leaving, staying = [
+            pick(keep, at).astype(jnp.float32) + pick(got, at).astype(jnp.float32)
+            for at in (1 - self.first, self.first)
+        ]
+        return leaving.astype(jnp.bfloat16), staying
 
     def leaving(self, buf, bit):
         return pick(buf, 1 - bit).astype(jnp.bfloat16)
+
+    def first_step(self, staying, out, *ties):
+        return staying + after(send_along(self.place, out, first_mask), *ties).astype(jnp.float32)
 
     def step(self, buf, out, mask_of, bit, *ties):
         got = after(send_along(self.place, out, mask_of), *ties)
@@ -178,7 +187,6 @@
         sems,
     )
     late = 10
-    weights = started([(mix_in, mix), (up_in, up), (down_in, down), (cot_in, cot)], sems, late)
     finish(tap_load)
 
     count, width = taps.shape[3], lines.shape[3]
@@ -194,8 +202,8 @@
                 bands[r, k * cols : (k + 1) * cols, d * width : (d + 1) * width] = band.astype(
                     bands.dtype
                 )
-    stores = started([(bands, bands_out)], sems, late + 12)
     finish(loads)
+    weights = started([(mix_in, mix), (up_in, up), (down_in, down), (cot_in, cot)], sems, late)
 
     for r in range(rows):
         window = ext[r : r + 3].reshape(3 * ext.shape[1], channels)
@@ -244,15 +252,15 @@
         out[half_units:] = dot(turned[...], pre_grad[:, at]).astype(out.dtype)
 
     mlp_sums(1 - core, mlp_send)
-    stores += started([(mlp_send, mlp_send_out)], sems, late + 4)
+    stores = started([(mlp_send, mlp_send_out), (bands, bands_out)], sems, late + 4)
     mlp_sums(core, mlp_keep)
-    stores += started([(mlp_keep, mlp_keep_out)], sems, late + 5)
+    stores += started([(mlp_keep, mlp_keep_out)], sems, late + 6)
 
     parts = [pl.ds(i * (points // 3), points // 3) for i in range(3)]
     for at in parts:
         total = cot[at, :].astype(jnp.float32) + dot(pre_grad[at, :], up[...], OVER_LANES)
         hg[at, :] = total.astype(hg.dtype)
-    stores += started([(hg, hg_out)], sems, late + 6)
+    stores += started([(hg, hg_out)], sems, late + 7)
 
     def mix_sums(half, out):
         at = pl.ds(pl.multiple_of(half * half_channels, half_channels), half_channels)
@@ -260,14 +268,14 @@
             out[k] = dot(feats[k, :, at], hg[...], OVER_ROWS).astype(out.dtype)
 
     mix_sums(1 - core, mix_send)
-    stores += started([(mix_send, mix_send_out)], sems, late + 7)
+    stores += started([(mix_send, mix_send_out)], sems, late + 8)
     mix_sums(core, mix_keep)
-    stores += started([(mix_keep, mix_keep_out)], sems, late + 8)
+    stores += started([(mix_keep, mix_keep_out)], sems, late + 9)
 
     for i, at in enumerate(parts):
         total = hidden[at, :].astype(jnp.float32) + dot(act[at, :], down[...])
         block[at, :] = total.astype(block.dtype)
-        stores += started([(block.at[at], block_out.at[at])], sems, late + 9 + i)
+        stores += started([(block.at[at], block_out.at[at])], sems, late + 10 + i)
     finish(stores)
 
 
@@ -334,11 +342,12 @@
     hidden_units = up_weight.shape[1]
     place = Place()
 
+    west = lax.ppermute(field_in[:, lon_cols - reach :], "lon", place.east)
+    east = lax.ppermute(field_in[:, :reach], "lon", place.west)
     top, bottom = field_in[0], field_in[lat_rows - 1]
     inner = lax.ppermute(jnp.where(place.even, bottom, top), AXES, place.pairs)
     outer = lax.ppermute(jnp.where(place.even, top, bottom), AXES, place.bridges)
-    west = lax.ppermute(field_in[:, lon_cols - reach :], "lon", place.east)
-    east = lax.ppermute(field_in[:, :reach], "lon", place.west)
+    inner, outer, west, east = lax.optimization_barrier((inner, outer, west, east))
     north = jnp.where(place.even, outer, inner)
     south = jnp.where(place.even, inner, outer)
     corners = jnp.stack([north[lon_cols - reach :], south[lon_cols - reach :]])
@@ -457,16 +466,16 @@
         ring = Ring(place)
         block_shape = (2, 2, 2, mlp_half[0] // 8, channels)
         mlp = ring.to_core(mlp_keep.reshape(block_shape), mlp_send.reshape(block_shape))
-        mlp_out = ring.leaving(mlp, ring.first)
+        mlp_out, mlp = ring.split(*mlp)
         block_shape = (2, 2, 2, basis_count * half_channels // 8, channels)
         mix = ring.to_core(mix_keep.reshape(block_shape), mix_send.reshape(block_shape))
-        mix_out = ring.leaving(mix, ring.first)
+        mix_out, mix = ring.split(*mix)
         inner, rims, to_west, to_east = adjoint_of(hidden_grad, mlp_out, mix_out)
         from_east = lax.ppermute(to_west, "lon", place.west)
         from_west = lax.ppermute(to_east, "lon", place.east)
-        mlp = ring.step(mlp, mlp_out, first_mask, ring.first, to_west)
+        mlp = ring.first_step(mlp, mlp_out, to_west)
         mlp_out = ring.leaving(mlp, ring.second)
-        mix = ring.step(mix, mix_out, first_mask, ring.first, mlp_out)
+        mix = ring.first_step(mix, mix_out, mlp_out)
         mix_out = ring.leaving(mix, ring.second)
         mlp = ring.step(mlp, mlp_out, second_mask, ring.second, mix_out)
         mlp_out = ring.leaving(mlp, ring.near)

time: 103 us -> 108 us (1.049)
  waiting for transfers between devices: 28.6 us -> 31 us
  starting transfers between devices: 35.6 us -> 37 us
    ppermute x1, waiting for transfers between devices: 2.54 us -> 0.01 us  [local(): corners_east = lax.ppermute(corners, 'lon', place.west)]
    ppermute x1, waiting for transfers between devices: 0.69 us -> 2.72 us  [local(): inner = lax.ppermute(jnp.where(place.even, bottom, top), AXES, place.pairs)]
    ppermute x18, waiting for transfers between devices: 24.4 us -> 26.3 us  [send_along(): return lax.ppermute(block, AXES, route(place, mask_of))]
    ppermute x1, starting transfers between devices: 3.03 us -> 1.52 us  [local(): lax.ppermute(jnp.where(place.even, top, bottom), AXES, place.bridges)]
    ppermute x18, starting transfers between devices: 25.1 us -> 26.6 us  [send_along(): return lax.ppermute(block, AXES, route(place, mask_of))]
    convert_element_type x0 -> x2, other arithmetic: none -> 1.28 us  [split(): return (leaving.astype(jnp.bfloat16), staying)]
    unnamed x32 -> x34, local copies, waits for them, and re-layouts: 4.13 us -> 4.04 us
where the time goes in v2:
time: 108 us; the launch traced here: 107 us
  starting transfers between devices  37 us (34%)
  waiting for transfers between devices  31 us (29%)
  Pallas kernels  24.5 us (23%)
  local copies, waits for them, and re-layouts  7.24 us (7%)
  other arithmetic  5.93 us (5%)
  between operations  1.22 us (1%)
    ppermute x18, starting transfers between devices, send_along(): return lax.ppermute(block, AXES, route(place, mask_of))  26.6 us
    ppermute x18, waiting for transfers between devices, send_along(): return lax.ppermute(block, AXES, route(place, mask_of))  26.3 us
    pallas_call x2, Pallas kernels, call(): pl.pallas_call(kernel, out_shape=[jax.ShapeDtypeStruct(shape, kind) for s...  24.5 us
    unnamed x34, local copies, waits for them, and re-layouts  4.04 us
    ppermute x1, waiting for transfers between devices, local(): inner = lax.ppermute(jnp.where(place.even, bottom, top), AXES, place.pairs)  2.72 us
    ppermute x1, starting transfers between devices, local(): inner = lax.ppermute(jnp.where(place.even, bottom, top), AXES, place.pairs)  2.28 us
  transfers between devices with their start and end apart: 28, of which 14 were waited for; matrix products, arithmetic and copies ran while one was open for 6% of the time, Pallas kernels for 8%

profile of v2, /device:TPU:0, one launch (start us, length us, event | category | flops | bytes accessed | tf_op | source)
XLA Modules:
  0.0 106.9 jit_solution(11584982673535149098)
XLA Ops:
  2.2 2.0 %collective-permute-start.3 = (bf16[10,16,512]{2,1,0:T(8,128)(2,1)S(1)}, bf16[10,16,512]{2,1,0:T(8,128)(2,1)S(1)}, u32[]{:S(2)}, u32[]{:S(2)}) collective-permute-start(bf16[10,16,512]{2,1,0:T(8,128)(2,1)S(1)} %get-tuple-element.115), channel_id=1, source_target_pairs={{1,0},{2,1},{3,2},{0,3},{5,4},{6,5},{7,6},{4,7},{9,8},{10,9},{11,1... | collective-permute-start | bytes 491528 | tf_op jit(solution)/shard_map/ppermute | solution.py:346
  5.1 2.3 %collective-permute-start = (bf16[96,512]{1,0:T(8,128)(2,1)S(1)}, bf16[96,512]{1,0:T(8,128)(2,1)S(1)}, u32[]{:S(2)}, u32[]{:S(2)}) collective-permute-start(bf16[96,512]{1,0:T(8,128)(2,1)S(1)} %get-tuple-element.118), channel_id=1, source_target_pairs={{0,4},{1,5},{2,6},{3,7},{4,0},{5,1},{6,2},{7,3},{8,12},{9,13},{10,... | collective-permute-start | bytes 294920 | tf_op jit(solution)/shard_map/ppermute | solution.py:348
  7.4 1.5 %collective-permute-start.1 = (bf16[96,512]{1,0:T(8,128)(2,1)S(1)}, bf16[96,512]{1,0:T(8,128)(2,1)S(1)}, u32[]{:S(2)}, u32[]{:S(2)}) collective-permute-start(bf16[96,512]{1,0:T(8,128)(2,1)S(1)} %get-tuple-element.117), channel_id=1, source_target_pairs={{0,2},{1,3},{2,0},{3,1},{4,8},{5,9},{6,10},{7,11},{8,4},{9,5},{10,... | collective-permute-start | bytes 294920 | tf_op jit(solution)/shard_map/ppermute | solution.py:349
  8.9 2.7 %collective-permute-done = bf16[96,512]{1,0:T(8,128)(2,1)S(1)} collective-permute-done((bf16[96,512]{1,0:T(8,128)(2,1)S(1)}, bf16[96,512]{1,0:T(8,128)(2,1)S(1)}, u32[]{:S(2)}, u32[]{:S(2)}) %collective-permute-start) | collective-permute-done | bytes 98336 | tf_op jit(solution)/shard_map/ppermute | solution.py:348
  12.2 1.7 %collective-permute-start.5 = (bf16[2,16,512]{2,1,0:T(8,128)(2,1)S(1)}, bf16[2,16,512]{2,1,0:T(8,128)(2,1)S(1)}, u32[]{:S(2)}, u32[]{:S(2)}) collective-permute-start(bf16[2,16,512]{2,1,0:T(8,128)(2,1)S(1)} %pad_maximum_fusion.7), channel_id=1, source_target_pairs={{1,0},{2,1},{3,2},{0,3},{5,4},{6,5},{7,6},{4,7},{9,8},{10,9},{11,1... | collective-permute-start | bytes 98312 | tf_op jit(solution)/shard_map/ppermute | solution.py:356
  13.9 1.6 %collective-permute-done.4.corners_west = bf16[2,16,512]{2,1,0:T(8,128)(2,1)S(1)} collective-permute-done((bf16[2,16,512]{2,1,0:T(8,128)(2,1)S(1)}, bf16[2,16,512]{2,1,0:T(8,128)(2,1)S(1)}, u32[]{:S(2)}, u32[]{:S(2)}) %collective-permute-start.4) | collective-permute-done | bytes 32800 | tf_op jit(solution)/shard_map/ppermute | solution.py:354
  16.1 15.7 %shard_map.110 = (bf16[960,512]{1,0:T(8,128)(2,1)}, bf16[960,512]{1,0:T(8,128)(2,1)}, bf16[10,288,384]{2,1,0:T(8,128)(2,1)}, bf16[1024,512]{1,0:T(8,128)(2,1)}, ...) custom-call(s32[1]{0:T(128)} %bitcast.core_ref, s32[10]{0:T(128)} %reach_ref.1, ...), custom_call_target="tpu_custom_call" | custom-call | flops 10192158720 | bytes 13762560 | tf_op jit(solution)/shard_map/pallas_call | solution.py:326
  31.9 1.7 %collective-permute-start.8 = (bf16[2,2,2,128,512]{4,3,2,1,0:T(8,128)(2,1)}, bf16[2,2,2,128,512]{4,3,2,1,0:T(8,128)(2,1)S(1)}, u32[]{:S(2)}, u32[]{:S(2)}) collective-permute-start(bf16[2,2,2,128,512]{4,3,2,1,0:T(8,128)(2,1)} %bitcast.76), channel_id=1, source_target_pairs={{0,1},{1,0},{2,3},{3,2},{4,5},{5,4},{6,7},{7,6},{8,9},{9,8},{10,11... | collective-permute-start | bytes 3145736 | tf_op jit(solution)/shard_map/ppermute | solution.py:46
  33.7 2.4 %collective-permute-done.8 = bf16[2,2,2,128,512]{4,3,2,1,0:T(8,128)(2,1)S(1)} collective-permute-done((bf16[2,2,2,128,512]{4,3,2,1,0:T(8,128)(2,1)}, bf16[2,2,2,128,512]{4,3,2,1,0:T(8,128)(2,1)S(1)}, u32[]{:S(2)}, u32[]{:S(2)}) %collective-permute-start.8) | collective-permute-done | bytes 1048608 | tf_op jit(solution)/shard_map/ppermute | solution.py:46
  36.1 1.2 %fusion.2 = bf16[2,2,128,512]{3,2,1,0:T(8,128)(2,1)S(1)} fusion(bf16[2,2,2,128,512]{4,3,2,1,0:T(8,128)(2,1)S(1)} %collective-permute-done.8, s32[]{:T(128)S(6)} %select_n.232, bf16[2,2,2,128,512]{4,3,2,1,0:T(8,128)(2,1)} %bitcast.71), kind=kLoop, calls=%fused_computation.9 | loop fusion | flops 1048576 | bytes 1572868 | tf_op jit(solution)/shard_map/convert_element_type | solution.py:90
  38.1 1.6 %collective-permute-start.7 = (bf16[2,2,96,512]{3,2,1,0:T(8,128)(2,1)S(1)}, bf16[2,2,96,512]{3,2,1,0:T(8,128)(2,1)S(1)}, u32[]{:S(2)}, u32[]{:S(2)}) collective-permute-start(bf16[2,2,96,512]{3,2,1,0:T(8,128)(2,1)S(1)} %fusion.3), channel_id=1, source_target_pairs={{0,2},{1,5},{2,0},{3,7},{4,6},{5,1},{6,4},{7,3},{8,10},{9,13},{10,... | collective-permute-start | bytes 1179656 | tf_op jit(solution)/shard_map/ppermute | solution.py:46
  39.7 8.8 %shard_map.111 = (bf16[10,96,512]{2,1,0:T(8,128)(2,1)}, f32[2,96,512]{2,1,0:T(8,128)}, bf16[12,16,512]{2,1,0:T(8,128)(2,1)}, bf16[12,16,512]{2,1,0:T(8,128)(2,1)}) custom-call(bf16[960,512]{1,0:T(8,128)(2,1)} %get-tuple-element.80.hg_in, bf16[3,512,512]{2,1,0:T(8,128)(2,1)} %mix_in.3, bf16[10,288,384]{2,1,0:T(8,128)(2,1)} %get-tuple-element.81.bands_in), custom_call_target="tpu_custom_call" | custom-call | flops 2642411520 | bytes 11796480 | tf_op jit(solution)/shard_map/pallas_call | solution.py:326
  49.1 1.2 %bitcast_add_fusion = f32[2,2,128,512]{3,2,1,0:T(8,128)S(1)} fusion(bf16[2,2,128,512]{3,2,1,0:T(8,128)(2,1)} %collective-permute-done.9, bf16[2,2,2,128,512]{4,3,2,1,0:T(8,128)(2,1)S(1)} %collective-permute-done.8, s32[]{:T(128)S(6)} %select_n.231, bf16[2,2,2,128,512]{4,3,2,1,0:T(8,128)(2,1)S(1)} %bitcast.72), kind=kLoop, calls=%fused_computation.4 | loop fusion | flops 1310720 | bytes 2621444 | tf_op jit(solution)/shard_map/add | solution.py:96
  50.4 1.6 %collective-permute-start.11 = (bf16[2,128,512]{2,1,0:T(8,128)(2,1)S(1)}, bf16[2,128,512]{2,1,0:T(8,128)(2,1)S(1)}, u32[]{:S(2)}, u32[]{:S(2)}) collective-permute-start(bf16[2,128,512]{2,1,0:T(8,128)(2,1)S(1)} %fusion.4), channel_id=1, source_target_pairs={{0,4},{1,3},{2,6},{3,1},{4,0},{5,7},{6,2},{7,5},{8,12},{9,11},{10,... | collective-permute-start | bytes 786440 | tf_op jit(solution)/shard_map/ppermute | solution.py:46
  52.7 4.1 %collective-permute-done.11 = bf16[2,128,512]{2,1,0:T(8,128)(2,1)S(1)} collective-permute-done((bf16[2,128,512]{2,1,0:T(8,128)(2,1)S(1)}, bf16[2,128,512]{2,1,0:T(8,128)(2,1)S(1)}, u32[]{:S(2)}, u32[]{:S(2)}) %collective-permute-start.11) | collective-permute-done | bytes 262176 | tf_op jit(solution)/shard_map/ppermute | solution.py:46
  56.9 2.5 %collective-permute-start.13 = (bf16[128,512]{1,0:T(8,128)(2,1)S(1)}, bf16[128,512]{1,0:T(8,128)(2,1)S(1)}, u32[]{:S(2)}, u32[]{:S(2)}) collective-permute-start(bf16[128,512]{1,0:T(8,128)(2,1)S(1)} %fusion.8), channel_id=1, source_target_pairs={{0,8},{1,9},{2,10},{3,11},{4,12},{5,13},{6,14},{7,15},{8,0},{9,1},... | collective-permute-start | bytes 393224 | tf_op jit(solution)/shard_map/ppermute | solution.py:46
  59.5 2.0 %collective-permute-start.12 = (bf16[96,512]{1,0:T(8,128)(2,1)S(1)}, bf16[96,512]{1,0:T(8,128)(2,1)S(1)}, u32[]{:S(2)}, u32[]{:S(2)}) collective-permute-start(bf16[96,512]{1,0:T(8,128)(2,1)S(1)} %fusion.9), channel_id=1, source_target_pairs={{0,8},{1,9},{2,10},{3,11},{4,12},{5,13},{6,14},{7,15},{8,0},{9,1},... | collective-permute-start | bytes 294920 | tf_op jit(solution)/shard_map/ppermute | solution.py:46
  62.4 3.4 %collective-permute-start.15 = (bf16[128,512]{1,0:T(8,128)(2,1)S(1)}, bf16[128,512]{1,0:T(8,128)(2,1)S(1)}, u32[]{:S(2)}, u32[]{:S(2)}) collective-permute-start(bf16[128,512]{1,0:T(8,128)(2,1)S(1)} %fusion.5), channel_id=1, source_target_pairs={{0,16},{1,17},{2,18},{3,19},{4,20},{5,21},{6,22},{7,23},{8,24},{9,... | collective-permute-start | bytes 393224 | tf_op jit(solution)/shard_map/ppermute | solution.py:46
  65.8 2.5 %collective-permute-start.14 = (bf16[96,512]{1,0:T(8,128)(2,1)S(1)}, bf16[96,512]{1,0:T(8,128)(2,1)S(1)}, u32[]{:S(2)}, u32[]{:S(2)}) collective-permute-start(bf16[96,512]{1,0:T(8,128)(2,1)S(1)} %fusion.7), channel_id=1, source_target_pairs={{0,16},{1,17},{2,18},{3,19},{4,20},{5,21},{6,22},{7,23},{8,24},{9,... | collective-permute-start | bytes 294920 | tf_op jit(solution)/shard_map/ppermute | solution.py:46
  70.3 3.4 %collective-permute-done.15 = bf16[128,512]{1,0:T(8,128)(2,1)S(1)} collective-permute-done((bf16[128,512]{1,0:T(8,128)(2,1)S(1)}, bf16[128,512]{1,0:T(8,128)(2,1)S(1)}, u32[]{:S(2)}, u32[]{:S(2)}) %collective-permute-start.15) | collective-permute-done | bytes 131104 | tf_op jit(solution)/shard_map/ppermute | solution.py:46
  73.7 2.2 %collective-permute-done.14 = bf16[96,512]{1,0:T(8,128)(2,1)S(1)} collective-permute-done((bf16[96,512]{1,0:T(8,128)(2,1)S(1)}, bf16[96,512]{1,0:T(8,128)(2,1)S(1)}, u32[]{:S(2)}, u32[]{:S(2)}) %collective-permute-start.14) | collective-permute-done | bytes 98336 | tf_op jit(solution)/shard_map/ppermute | solution.py:46
  75.9 2.2 %collective-permute-start.19 = (bf16[1,128,512]{2,1,0:T(8,128)(2,1)S(1)}, bf16[1,128,512]{2,1,0:T(8,128)(2,1)S(1)}, u32[]{:S(2)}, u32[]{:S(2)}) collective-permute-start(bf16[1,128,512]{2,1,0:T(8,128)(2,1)S(1)} %bitcast.75), channel_id=1, source_target_pairs={{0,8},{1,9},{2,10},{3,11},{4,12},{5,13},{6,14},{7,15},{8,0},{9,1},... | collective-permute-start | bytes 393224 | tf_op jit(solution)/shard_map/ppermute | solution.py:46
  78.2 3.7 %collective-permute-done.19 = bf16[1,128,512]{2,1,0:T(8,128)(2,1)S(1)} collective-permute-done((bf16[1,128,512]{2,1,0:T(8,128)(2,1)S(1)}, bf16[1,128,512]{2,1,0:T(8,128)(2,1)S(1)}, u32[]{:S(2)}, u32[]{:S(2)}) %collective-permute-start.19) | collective-permute-done | bytes 131104 | tf_op jit(solution)/shard_map/ppermute | solution.py:46
  81.9 1.9 %collective-permute-start.21 = (bf16[2,128,512]{2,1,0:T(8,128)(2,1)S(1)}, bf16[2,128,512]{2,1,0:T(8,128)(2,1)S(1)}, u32[]{:S(2)}, u32[]{:S(2)}) collective-permute-start(bf16[2,128,512]{2,1,0:T(8,128)(2,1)S(1)} %pad_maximum_fusion.4), channel_id=1, source_target_pairs={{0,4},{1,3},{2,6},{3,1},{4,0},{5,7},{6,2},{7,5},{8,12},{9,11},{10,... | collective-permute-start | bytes 786440 | tf_op jit(solution)/shard_map/ppermute | solution.py:46
  83.9 2.0 %collective-permute-start.20 = (bf16[2,96,512]{2,1,0:T(8,128)(2,1)S(1)}, bf16[2,96,512]{2,1,0:T(8,128)(2,1)S(1)}, u32[]{:S(2)}, u32[]{:S(2)}) collective-permute-start(bf16[2,96,512]{2,1,0:T(8,128)(2,1)S(1)} %pad_maximum_fusion.5), channel_id=1, source_target_pairs={{0,4},{1,3},{2,6},{3,1},{4,0},{5,7},{6,2},{7,5},{8,12},{9,11},{10,... | collective-permute-start | bytes 589832 | tf_op jit(solution)/shard_map/ppermute | solution.py:46
  86.0 2.4 %collective-permute-done.21 = bf16[2,128,512]{2,1,0:T(8,128)(2,1)S(1)} collective-permute-done((bf16[2,128,512]{2,1,0:T(8,128)(2,1)S(1)}, bf16[2,128,512]{2,1,0:T(8,128)(2,1)S(1)}, u32[]{:S(2)}, u32[]{:S(2)}) %collective-permute-start.21) | collective-permute-done | bytes 262176 | tf_op jit(solution)/shard_map/ppermute | solution.py:46
  88.5 1.9 %collective-permute-start.25 = (bf16[4,128,512]{2,1,0:T(8,128)(2,1)S(1)}, bf16[4,128,512]{2,1,0:T(8,128)(2,1)S(1)}, u32[]{:S(2)}, u32[]{:S(2)}) collective-permute-start(bf16[4,128,512]{2,1,0:T(8,128)(2,1)S(1)} %pad_maximum_fusion.2), channel_id=1, source_target_pairs={{0,2},{1,5},{2,0},{3,7},{4,6},{5,1},{6,4},{7,3},{8,10},{9,13},{10,... | collective-permute-start | bytes 1572872 | tf_op jit(solution)/shard_map/ppermute | solution.py:46
  90.6 1.9 %collective-permute-start.24 = (bf16[4,96,512]{2,1,0:T(8,128)(2,1)S(1)}, bf16[4,96,512]{2,1,0:T(8,128)(2,1)S(1)}, u32[]{:S(2)}, u32[]{:S(2)}) collective-permute-start(bf16[4,96,512]{2,1,0:T(8,128)(2,1)S(1)} %pad_maximum_fusion.3), channel_id=1, source_target_pairs={{0,2},{1,5},{2,0},{3,7},{4,6},{5,1},{6,4},{7,3},{8,10},{9,13},{10,... | collective-permute-start | bytes 1179656 | tf_op jit(solution)/shard_map/ppermute | solution.py:46
  92.5 5.2 %collective-permute-done.25 = bf16[4,128,512]{2,1,0:T(8,128)(2,1)S(1)} collective-permute-done((bf16[4,128,512]{2,1,0:T(8,128)(2,1)S(1)}, bf16[4,128,512]{2,1,0:T(8,128)(2,1)S(1)}, u32[]{:S(2)}, u32[]{:S(2)}) %collective-permute-start.25) | collective-permute-done | bytes 524320 | tf_op jit(solution)/shard_map/ppermute | solution.py:46
  98.0 1.3 %fusion.1 = bf16[10,96,512]{2,1,0:T(8,128)(2,1)} fusion(f32[10,16,512]{2,1,0:T(8,128)S(1)} %slice_convert_fusion, f32[10,16,512]{2,1,0:T(8,128)S(1)} %slice_convert_fusion.1, f32[1,96,512]{2,1,0:T(8,128)S(1)} %get-tuple-element.124, f32[1,96,512]{2,1,0:T(8,128)S(1)} %get-tuple-element.123, bf16[10,96,512]{2,1,0:T(8,128)(2,1)S(1)} %copy-done.8, ...), kind=kLoop, calls=%fused_computation.2 | loop fusion | flops 3932160 | bytes 3015080 | tf_op jit(solution)/shard_map/convert_element_type | solution.py:462
  100.6 1.3 %collective-permute-done.24 = bf16[4,96,512]{2,1,0:T(8,128)(2,1)S(1)} collective-permute-done((bf16[4,96,512]{2,1,0:T(8,128)(2,1)S(1)}, bf16[4,96,512]{2,1,0:T(8,128)(2,1)S(1)}, u32[]{:S(2)}, u32[]{:S(2)}) %collective-permute-start.24) | collective-permute-done | bytes 393248 | tf_op jit(solution)/shard_map/ppermute | solution.py:46
  104.6 1.2 %constant_dynamic-update-slice_fusion.3 = bf16[3,512,512]{2,1,0:T(8,128)(2,1)S(1)} fusion(bf16[3,512,512]{2,1,0:T(8,128)(2,1)S(1)} %constant_dynamic-update-slice_fusion, bf16[3,256,512]{2,1,0:T(8,128)(2,1)} %bitcast.36, s32[]{:T(128)S(6)} %select_n.262), kind=kLoop, calls=%fused_computation.67 | loop fusion | bytes 1572868 | tf_op jit(solution)/shard_map/dynamic_update_slice | solution.py:127
  (118 shorter events, 14.6 us)
Async XLA Ops:
  1.7 10.4 %collective-permute-start.2 = (bf16[10,16,512]{2,1,0:T(8,128)(2,1)S(1)}, bf16[10,16,512]{2,1,0:T(8,128)(2,1)S(1)}, u32[]{:S(2)}, u32[]{:S(2)}) collective-permute-start(bf16[10,16,512]{2,1,0:T(8,128)(2,1)S(1)} %get-tuple-element.116), channel_id=1, source_target_pairs={{0,1},{1,2},{2,3},{3,0},{4,5},{5,6},{6,7},{7,4},{8,9},{9,10},{10,1... | collective-permute-start | bytes 491528 | tf_op jit(solution)/shard_map/ppermute | solution.py:345
  2.2 9.9 %collective-permute-start.3 = (bf16[10,16,512]{2,1,0:T(8,128)(2,1)S(1)}, bf16[10,16,512]{2,1,0:T(8,128)(2,1)S(1)}, u32[]{:S(2)}, u32[]{:S(2)}) collective-permute-start(bf16[10,16,512]{2,1,0:T(8,128)(2,1)S(1)} %get-tuple-element.115), channel_id=1, source_target_pairs={{1,0},{2,1},{3,2},{0,3},{5,4},{6,5},{7,6},{4,7},{9,8},{10,9},{11,1... | collective-permute-start | bytes 491528 | tf_op jit(solution)/shard_map/ppermute | solution.py:346
  5.1 6.5 %collective-permute-start = (bf16[96,512]{1,0:T(8,128)(2,1)S(1)}, bf16[96,512]{1,0:T(8,128)(2,1)S(1)}, u32[]{:S(2)}, u32[]{:S(2)}) collective-permute-start(bf16[96,512]{1,0:T(8,128)(2,1)S(1)} %get-tuple-element.118), channel_id=1, source_target_pairs={{0,4},{1,5},{2,6},{3,7},{4,0},{5,1},{6,2},{7,3},{8,12},{9,13},{10,... | collective-permute-start | bytes 294920 | tf_op jit(solution)/shard_map/ppermute | solution.py:348
  7.4 4.6 %collective-permute-start.1 = (bf16[96,512]{1,0:T(8,128)(2,1)S(1)}, bf16[96,512]{1,0:T(8,128)(2,1)S(1)}, u32[]{:S(2)}, u32[]{:S(2)}) collective-permute-start(bf16[96,512]{1,0:T(8,128)(2,1)S(1)} %get-tuple-element.117), channel_id=1, source_target_pairs={{0,2},{1,3},{2,0},{3,1},{4,8},{5,9},{6,10},{7,11},{8,4},{9,5},{10,... | collective-permute-start | bytes 294920 | tf_op jit(solution)/shard_map/ppermute | solution.py:349
  12.1 3.4 %collective-permute-start.4 = (bf16[2,16,512]{2,1,0:T(8,128)(2,1)S(1)}, bf16[2,16,512]{2,1,0:T(8,128)(2,1)S(1)}, u32[]{:S(2)}, u32[]{:S(2)}) collective-permute-start(bf16[2,16,512]{2,1,0:T(8,128)(2,1)S(1)} %pad_maximum_fusion.6), channel_id=1, source_target_pairs={{0,1},{1,2},{2,3},{3,0},{4,5},{5,6},{6,7},{7,4},{8,9},{9,10},{10,1... | collective-permute-start | bytes 98312 | tf_op jit(solution)/shard_map/ppermute | solution.py:354
  12.2 3.3 %collective-permute-start.5 = (bf16[2,16,512]{2,1,0:T(8,128)(2,1)S(1)}, bf16[2,16,512]{2,1,0:T(8,128)(2,1)S(1)}, u32[]{:S(2)}, u32[]{:S(2)}) collective-permute-start(bf16[2,16,512]{2,1,0:T(8,128)(2,1)S(1)} %pad_maximum_fusion.7), channel_id=1, source_target_pairs={{1,0},{2,1},{3,2},{0,3},{5,4},{6,5},{7,6},{4,7},{9,8},{10,9},{11,1... | collective-permute-start | bytes 98312 | tf_op jit(solution)/shard_map/ppermute | solution.py:356
  31.9 6.1 %copy-start.9 = (bf16[3,256,512]{2,1,0:T(8,128)(2,1)S(1)}, bf16[3,256,512]{2,1,0:T(8,128)(2,1)}, u32[]{:S(2)}) copy-start(bf16[3,256,512]{2,1,0:T(8,128)(2,1)} %get-tuple-element.75) | copy-start | bytes 2359300
  31.9 4.2 %collective-permute-start.8 = (bf16[2,2,2,128,512]{4,3,2,1,0:T(8,128)(2,1)}, bf16[2,2,2,128,512]{4,3,2,1,0:T(8,128)(2,1)S(1)}, u32[]{:S(2)}, u32[]{:S(2)}) collective-permute-start(bf16[2,2,2,128,512]{4,3,2,1,0:T(8,128)(2,1)} %bitcast.76), channel_id=1, source_target_pairs={{0,1},{1,0},{2,3},{3,2},{4,5},{5,4},{6,7},{7,6},{8,9},{9,8},{10,11... | collective-permute-start | bytes 3145736 | tf_op jit(solution)/shard_map/ppermute | solution.py:46
  33.6 4.4 %collective-permute-start.6 = (bf16[2,2,2,96,512]{4,3,2,1,0:T(8,128)(2,1)}, bf16[2,2,2,96,512]{4,3,2,1,0:T(8,128)(2,1)S(1)}, u32[]{:S(2)}, u32[]{:S(2)}) collective-permute-start(bf16[2,2,2,96,512]{4,3,2,1,0:T(8,128)(2,1)} %bitcast.78), channel_id=1, source_target_pairs={{0,1},{1,0},{2,3},{3,2},{4,5},{5,4},{6,7},{7,6},{8,9},{9,8},{10,11... | collective-permute-start | bytes 2359304 | tf_op jit(solution)/shard_map/ppermute | solution.py:46
  37.3 11.8 %collective-permute-start.9 = (bf16[2,2,128,512]{3,2,1,0:T(8,128)(2,1)S(1)}, bf16[2,2,128,512]{3,2,1,0:T(8,128)(2,1)}, u32[]{:S(2)}, u32[]{:S(2)}) collective-permute-start(bf16[2,2,128,512]{3,2,1,0:T(8,128)(2,1)S(1)} %fusion.2), channel_id=1, source_target_pairs={{0,2},{1,5},{2,0},{3,7},{4,6},{5,1},{6,4},{7,3},{8,10},{9,13},{10,... | collective-permute-start | bytes 1572872 | tf_op jit(solution)/shard_map/ppermute | solution.py:46
  38.1 13.8 %collective-permute-start.7 = (bf16[2,2,96,512]{3,2,1,0:T(8,128)(2,1)S(1)}, bf16[2,2,96,512]{3,2,1,0:T(8,128)(2,1)S(1)}, u32[]{:S(2)}, u32[]{:S(2)}) collective-permute-start(bf16[2,2,96,512]{3,2,1,0:T(8,128)(2,1)S(1)} %fusion.3), channel_id=1, source_target_pairs={{0,2},{1,5},{2,0},{3,7},{4,6},{5,1},{6,4},{7,3},{8,10},{9,13},{10,... | collective-permute-start | bytes 1179656 | tf_op jit(solution)/shard_map/ppermute | solution.py:46
  39.7 9.4 %copy-start.7 = (bf16[1024,512]{1,0:T(8,128)(2,1)S(1)}, bf16[1024,512]{1,0:T(8,128)(2,1)}, u32[]{:S(2)}) copy-start(bf16[1024,512]{1,0:T(8,128)(2,1)} %get-tuple-element.77) | copy-start | bytes 3145732
  48.5 19.8 %collective-permute-start.16 = (bf16[12,16,512]{2,1,0:T(8,128)(2,1)}, bf16[12,16,512]{2,1,0:T(8,128)(2,1)S(1)}, u32[]{:S(2)}, u32[]{:S(2)}) collective-permute-start(bf16[12,16,512]{2,1,0:T(8,128)(2,1)} %get-tuple-element.82), channel_id=1, source_target_pairs={{1,0},{2,1},{3,2},{0,3},{5,4},{6,5},{7,6},{4,7},{9,8},{10,9},{11,1... | collective-permute-start | bytes 589832 | tf_op jit(solution)/shard_map/ppermute | solution.py:474
  48.9 19.3 %collective-permute-start.17 = (bf16[12,16,512]{2,1,0:T(8,128)(2,1)}, bf16[12,16,512]{2,1,0:T(8,128)(2,1)S(1)}, u32[]{:S(2)}, u32[]{:S(2)}) collective-permute-start(bf16[12,16,512]{2,1,0:T(8,128)(2,1)} %get-tuple-element.91), channel_id=1, source_target_pairs={{0,1},{1,2},{2,3},{3,0},{4,5},{5,6},{6,7},{7,4},{8,9},{9,10},{10,1... | collective-permute-start | bytes 589832 | tf_op jit(solution)/shard_map/ppermute | solution.py:475
  50.4 6.4 %collective-permute-start.11 = (bf16[2,128,512]{2,1,0:T(8,128)(2,1)S(1)}, bf16[2,128,512]{2,1,0:T(8,128)(2,1)S(1)}, u32[]{:S(2)}, u32[]{:S(2)}) collective-permute-start(bf16[2,128,512]{2,1,0:T(8,128)(2,1)S(1)} %fusion.4), channel_id=1, source_target_pairs={{0,4},{1,3},{2,6},{3,1},{4,0},{5,7},{6,2},{7,5},{8,12},{9,11},{10,... | collective-permute-start | bytes 786440 | tf_op jit(solution)/shard_map/ppermute | solution.py:46
  52.2 16.2 %copy-start.10 = (f32[2,96,512]{2,1,0:T(8,128)S(1)}, f32[2,96,512]{2,1,0:T(8,128)}, u32[]{:S(2)}) copy-start(f32[2,96,512]{2,1,0:T(8,128)} %get-tuple-element.90) | copy-start | bytes 1179652
  52.2 7.3 %collective-permute-start.10 = (bf16[2,96,512]{2,1,0:T(8,128)(2,1)S(1)}, bf16[2,96,512]{2,1,0:T(8,128)(2,1)S(1)}, u32[]{:S(2)}, u32[]{:S(2)}) collective-permute-start(bf16[2,96,512]{2,1,0:T(8,128)(2,1)S(1)} %fusion.6), channel_id=1, source_target_pairs={{0,4},{1,3},{2,6},{3,1},{4,0},{5,7},{6,2},{7,5},{8,12},{9,11},{10,... | collective-permute-start | bytes 589832 | tf_op jit(solution)/shard_map/ppermute | solution.py:46
  56.9 5.5 %collective-permute-start.13 = (bf16[128,512]{1,0:T(8,128)(2,1)S(1)}, bf16[128,512]{1,0:T(8,128)(2,1)S(1)}, u32[]{:S(2)}, u32[]{:S(2)}) collective-permute-start(bf16[128,512]{1,0:T(8,128)(2,1)S(1)} %fusion.8), channel_id=1, source_target_pairs={{0,8},{1,9},{2,10},{3,11},{4,12},{5,13},{6,14},{7,15},{8,0},{9,1},... | collective-permute-start | bytes 393224 | tf_op jit(solution)/shard_map/ppermute | solution.py:46
  59.5 6.3 %collective-permute-start.12 = (bf16[96,512]{1,0:T(8,128)(2,1)S(1)}, bf16[96,512]{1,0:T(8,128)(2,1)S(1)}, u32[]{:S(2)}, u32[]{:S(2)}) collective-permute-start(bf16[96,512]{1,0:T(8,128)(2,1)S(1)} %fusion.9), channel_id=1, source_target_pairs={{0,8},{1,9},{2,10},{3,11},{4,12},{5,13},{6,14},{7,15},{8,0},{9,1},... | collective-permute-start | bytes 294920 | tf_op jit(solution)/shard_map/ppermute | solution.py:46
  62.4 11.3 %collective-permute-start.15 = (bf16[128,512]{1,0:T(8,128)(2,1)S(1)}, bf16[128,512]{1,0:T(8,128)(2,1)S(1)}, u32[]{:S(2)}, u32[]{:S(2)}) collective-permute-start(bf16[128,512]{1,0:T(8,128)(2,1)S(1)} %fusion.5), channel_id=1, source_target_pairs={{0,16},{1,17},{2,18},{3,19},{4,20},{5,21},{6,22},{7,23},{8,24},{9,... | collective-permute-start | bytes 393224 | tf_op jit(solution)/shard_map/ppermute | solution.py:46
  65.8 10.1 %collective-permute-start.14 = (bf16[96,512]{1,0:T(8,128)(2,1)S(1)}, bf16[96,512]{1,0:T(8,128)(2,1)S(1)}, u32[]{:S(2)}, u32[]{:S(2)}) collective-permute-start(bf16[96,512]{1,0:T(8,128)(2,1)S(1)} %fusion.7), channel_id=1, source_target_pairs={{0,16},{1,17},{2,18},{3,19},{4,20},{5,21},{6,22},{7,23},{8,24},{9,... | collective-permute-start | bytes 294920 | tf_op jit(solution)/shard_map/ppermute | solution.py:46
  68.4 17.5 %collective-permute-start.22 = (bf16[96,512]{1,0:T(8,128)(2,1)S(1)}, bf16[96,512]{1,0:T(8,128)(2,1)S(1)}, u32[]{:S(2)}, u32[]{:S(2)}) collective-permute-start(bf16[96,512]{1,0:T(8,128)(2,1)S(1)} %get-tuple-element.134), channel_id=1, source_target_pairs={{0,4},{1,5},{2,6},{3,7},{4,0},{5,1},{6,2},{7,3},{8,12},{9,13},{10,... | collective-permute-start | bytes 294920 | tf_op jit(solution)/shard_map/ppermute | solution.py:444
  69.2 16.7 %collective-permute-start.23 = (bf16[96,512]{1,0:T(8,128)(2,1)S(1)}, bf16[96,512]{1,0:T(8,128)(2,1)S(1)}, u32[]{:S(2)}, u32[]{:S(2)}) collective-permute-start(bf16[96,512]{1,0:T(8,128)(2,1)S(1)} %get-tuple-element.133), channel_id=1, source_target_pairs={{0,2},{1,3},{2,0},{3,1},{4,8},{5,9},{6,10},{7,11},{8,4},{9,5},{10,... | collective-permute-start | bytes 294920 | tf_op jit(solution)/shard_map/ppermute | solution.py:445
  75.9 6.0 %collective-permute-start.19 = (bf16[1,128,512]{2,1,0:T(8,128)(2,1)S(1)}, bf16[1,128,512]{2,1,0:T(8,128)(2,1)S(1)}, u32[]{:S(2)}, u32[]{:S(2)}) collective-permute-start(bf16[1,128,512]{2,1,0:T(8,128)(2,1)S(1)} %bitcast.75), channel_id=1, source_target_pairs={{0,8},{1,9},{2,10},{3,11},{4,12},{5,13},{6,14},{7,15},{8,0},{9,1},... | collective-permute-start | bytes 393224 | tf_op jit(solution)/shard_map/ppermute | solution.py:46
  78.1 5.7 %collective-permute-start.18 = (bf16[1,96,512]{2,1,0:T(8,128)(2,1)S(1)}, bf16[1,96,512]{2,1,0:T(8,128)(2,1)S(1)}, u32[]{:S(2)}, u32[]{:S(2)}) collective-permute-start(bf16[1,96,512]{2,1,0:T(8,128)(2,1)S(1)} %fusion.10), channel_id=1, source_target_pairs={{0,8},{1,9},{2,10},{3,11},{4,12},{5,13},{6,14},{7,15},{8,0},{9,1},... | collective-permute-start | bytes 294920 | tf_op jit(solution)/shard_map/ppermute | solution.py:46
  81.9 6.4 %collective-permute-start.21 = (bf16[2,128,512]{2,1,0:T(8,128)(2,1)S(1)}, bf16[2,128,512]{2,1,0:T(8,128)(2,1)S(1)}, u32[]{:S(2)}, u32[]{:S(2)}) collective-permute-start(bf16[2,128,512]{2,1,0:T(8,128)(2,1)S(1)} %pad_maximum_fusion.4), channel_id=1, source_target_pairs={{0,4},{1,3},{2,6},{3,1},{4,0},{5,7},{6,2},{7,5},{8,12},{9,11},{10,... | collective-permute-start | bytes 786440 | tf_op jit(solution)/shard_map/ppermute | solution.py:46
  83.9 6.6 %collective-permute-start.20 = (bf16[2,96,512]{2,1,0:T(8,128)(2,1)S(1)}, bf16[2,96,512]{2,1,0:T(8,128)(2,1)S(1)}, u32[]{:S(2)}, u32[]{:S(2)}) collective-permute-start(bf16[2,96,512]{2,1,0:T(8,128)(2,1)S(1)} %pad_maximum_fusion.5), channel_id=1, source_target_pairs={{0,4},{1,3},{2,6},{3,1},{4,0},{5,7},{6,2},{7,5},{8,12},{9,11},{10,... | collective-permute-start | bytes 589832 | tf_op jit(solution)/shard_map/ppermute | solution.py:46
  88.5 9.2 %collective-permute-start.25 = (bf16[4,128,512]{2,1,0:T(8,128)(2,1)S(1)}, bf16[4,128,512]{2,1,0:T(8,128)(2,1)S(1)}, u32[]{:S(2)}, u32[]{:S(2)}) collective-permute-start(bf16[4,128,512]{2,1,0:T(8,128)(2,1)S(1)} %pad_maximum_fusion.2), channel_id=1, source_target_pairs={{0,2},{1,5},{2,0},{3,7},{4,6},{5,1},{6,4},{7,3},{8,10},{9,13},{10,... | collective-permute-start | bytes 1572872 | tf_op jit(solution)/shard_map/ppermute | solution.py:46
  90.6 7.4 %copy-start.8 = (bf16[10,96,512]{2,1,0:T(8,128)(2,1)S(1)}, bf16[10,96,512]{2,1,0:T(8,128)(2,1)}, u32[]{:S(2)}) copy-start(bf16[10,96,512]{2,1,0:T(8,128)(2,1)} %get-tuple-element.100) | copy-start | bytes 2949124
  90.6 11.4 %collective-permute-start.24 = (bf16[4,96,512]{2,1,0:T(8,128)(2,1)S(1)}, bf16[4,96,512]{2,1,0:T(8,128)(2,1)S(1)}, u32[]{:S(2)}, u32[]{:S(2)}) collective-permute-start(bf16[4,96,512]{2,1,0:T(8,128)(2,1)S(1)} %pad_maximum_fusion.3), channel_id=1, source_target_pairs={{0,2},{1,5},{2,0},{3,7},{4,6},{5,1},{6,4},{7,3},{8,10},{9,13},{10,... | collective-permute-start | bytes 1179656 | tf_op jit(solution)/shard_map/ppermute | solution.py:46
  97.9 4.5 %collective-permute-start.26 = (bf16[8,128,512]{2,1,0:T(8,128)(2,1)S(1)}, bf16[8,128,512]{2,1,0:T(8,128)(2,1)S(1)}, u32[]{:S(2)}, u32[]{:S(2)}) collective-permute-start(bf16[8,128,512]{2,1,0:T(8,128)(2,1)S(1)} %pad_maximum_fusion), channel_id=1, source_target_pairs={{0,1},{1,0},{2,3},{3,2},{4,5},{5,4},{6,7},{7,6},{8,9},{9,8},{10,11... | collective-permute-start | bytes 3145736 | tf_op jit(solution)/shard_map/ppermute | solution.py:46
  102.1 2.5 %collective-permute-start.27 = (bf16[8,96,512]{2,1,0:T(8,128)(2,1)S(1)}, bf16[8,96,512]{2,1,0:T(8,128)(2,1)}, u32[]{:S(2)}, u32[]{:S(2)}) collective-permute-start(bf16[8,96,512]{2,1,0:T(8,128)(2,1)S(1)} %pad_maximum_fusion.1), channel_id=1, source_target_pairs={{0,1},{1,0},{2,3},{3,2},{4,5},{5,4},{6,7},{7,6},{8,9},{9,8},{10,11... | collective-permute-start | bytes 2359304 | tf_op jit(solution)/shard_map/ppermute | solution.py:46
  (13 other events, 25.4 us)

commit v3 on v1

--- a/solution.py
+++ b/solution.py
@@ -94,9 +94,8 @@
         far = after(send_along(self.place, own, lambda i: 16), *ties)
         return ((own.astype(jnp.float32) + far.astype(jnp.float32)) * scale).astype(own.dtype)
 
-    def gather_near(self, piece, *ties):
-        piece = piece[None]
-        return joined(self.near, piece, after(send_along(self.place, piece, near_mask), *ties))
+    def gather_near(self, buf, *ties):
+        return joined(self.near, buf, after(send_along(self.place, buf, near_mask), *ties))
 
     def gather_second(self, buf, *ties):
         return joined(self.second, buf, after(send_along(self.place, buf, second_mask), *ties))
@@ -467,23 +466,23 @@
         mlp = ring.step(mlp, mlp_out, first_mask, ring.first, to_west)
         mlp_out = ring.leaving(mlp, ring.second)
         mix = ring.step(mix, mix_out, first_mask, ring.first, mlp_out)
-        mix_out = ring.leaving(mix, ring.second)
+        mix_out = ring.leaving(mix, ring.near)
         mlp = ring.step(mlp, mlp_out, second_mask, ring.second, mix_out)
         mlp_out = ring.leaving(mlp, ring.near)
-        mix = ring.step(mix, mix_out, second_mask, ring.second, mlp_out)
-        mix_out = ring.leaving(mix, ring.near)
+        mix = ring.step(mix, mix_out, near_mask, ring.near, mlp_out)
+        mix_out = ring.leaving(mix, ring.second)
         mlp = ring.step(mlp, mlp_out, near_mask, ring.near, mix_out).astype(low)
-        mix = ring.step(mix, mix_out, near_mask, ring.near, mlp).astype(low)
+        mix = ring.step(mix, mix_out, second_mask, ring.second, mlp).astype(low)
         from_east, from_west, _ = lax.optimization_barrier((from_east, from_west, mix))
         top_rim, bottom_rim = rim_blocks(rims, from_east, from_west)
-        mlp = ring.far_step(mlp, grad_scale, mix)
-        mix = ring.far_step(mix, grad_scale, mlp, top_rim, bottom_rim)
+        mlp = ring.far_step(mlp, grad_scale, mix)[None]
+        mix = ring.far_step(mix, grad_scale, mlp, top_rim, bottom_rim)[None]
         from_north, from_south = beyond(top_rim, bottom_rim)
         mlp = ring.gather_near(mlp)
-        mix = ring.gather_near(mix, mlp)
+        mix = ring.gather_second(mix, mlp)
         from_north, from_south, _ = lax.optimization_barrier((from_north, from_south, mlp))
         mlp = ring.gather_second(mlp, mix, from_north, from_south)
-        mix = ring.gather_second(mix, mlp)
+        mix = ring.gather_near(mix, mlp)
         mlp = ring.gather_first(mlp, mix)
         mlp_other = ring.gather_core(mlp)
         grad_field = whole_field(inner, from_east, from_west, from_north, from_south)

time: 103 us -> 102 us (level)
  transfers between devices with their start and end apart: 28 -> 28, of which waited for: 14 -> 15; matrix products, arithmetic and copies ran while one was open for 6% -> 6% of each run, Pallas kernels for 8% -> 9%
where the time goes in v3:
time: 102 us
  starting transfers between devices  35.3 us (35%)
  waiting for transfers between devices  28.1 us (28%)
  Pallas kernels  24.4 us (24%)
  local copies, waits for them, and re-layouts  7.45 us (7%)
  other arithmetic  5.37 us (5%)
  between operations  1.26 us (1%)
    ppermute x18, starting transfers between devices, send_along(): return lax.ppermute(block, AXES, route(place, mask_of))  24.5 us
    pallas_call x2, Pallas kernels, call(): pl.pallas_call(kernel, out_shape=[jax.ShapeDtypeStruct(shape, kind) for s...  24.4 us
    ppermute x18, waiting for transfers between devices, send_along(): return lax.ppermute(block, AXES, route(place, mask_of))  23.8 us
    unnamed x32, local copies, waits for them, and re-layouts  4.13 us
    ppermute x1, starting transfers between devices, local(): lax.ppermute(jnp.where(place.even, top, bottom), AXES, place.bridges)  3.03 us
    ppermute x1, waiting for transfers between devices, local(): corners_east = lax.ppermute(corners, 'lon', place.west)  2.54 us
  transfers between devices with their start and end apart: 28, of which 15 were waited for; matrix products, arithmetic and copies ran while one was open for 6% of the time, Pallas kernels for 9%

profile of v3, /device:TPU:0, one launch (start us, length us, event | category | flops | bytes accessed | tf_op | source)
XLA Modules:
  0.0 101.9 jit_solution(10648057942977820204)
XLA Ops:
  1.6 3.0 %collective-permute-start = (bf16[96,512]{1,0:T(8,128)(2,1)S(1)}, bf16[96,512]{1,0:T(8,128)(2,1)S(1)}, u32[]{:S(2)}, u32[]{:S(2)}) collective-permute-start(bf16[96,512]{1,0:T(8,128)(2,1)S(1)} %get-tuple-element.110), channel_id=1, source_target_pairs={{0,2},{1,3},{2,0},{3,1},{4,8},{5,9},{6,10},{7,11},{8,4},{9,5},{10,... | collective-permute-start | bytes 294920 | tf_op jit(solution)/shard_map/ppermute | solution.py:338
  4.6 1.5 %collective-permute-start.1 = (bf16[96,512]{1,0:T(8,128)(2,1)S(1)}, bf16[96,512]{1,0:T(8,128)(2,1)S(1)}, u32[]{:S(2)}, u32[]{:S(2)}) collective-permute-start(bf16[96,512]{1,0:T(8,128)(2,1)S(1)} %get-tuple-element.109), channel_id=1, source_target_pairs={{0,4},{1,5},{2,6},{3,7},{4,0},{5,1},{6,2},{7,3},{8,12},{9,13},{10,... | collective-permute-start | bytes 294920 | tf_op jit(solution)/shard_map/ppermute | solution.py:337
  7.2 1.7 %collective-permute-start.3 = (bf16[10,16,512]{2,1,0:T(8,128)(2,1)S(1)}, bf16[10,16,512]{2,1,0:T(8,128)(2,1)S(1)}, u32[]{:S(2)}, u32[]{:S(2)}) collective-permute-start(bf16[10,16,512]{2,1,0:T(8,128)(2,1)S(1)} %get-tuple-element.107), channel_id=1, source_target_pairs={{1,0},{2,1},{3,2},{0,3},{5,4},{6,5},{7,6},{4,7},{9,8},{10,9},{11,1... | collective-permute-start | bytes 491528 | tf_op jit(solution)/shard_map/ppermute | solution.py:340
  9.7 1.2 %collective-permute-start.5 = (bf16[2,16,512]{2,1,0:T(8,128)(2,1)S(1)}, bf16[2,16,512]{2,1,0:T(8,128)(2,1)S(1)}, u32[]{:S(2)}, u32[]{:S(2)}) collective-permute-start(bf16[2,16,512]{2,1,0:T(8,128)(2,1)S(1)} %pad_maximum_fusion.7), channel_id=1, source_target_pairs={{1,0},{2,1},{3,2},{0,3},{5,4},{6,5},{7,6},{4,7},{9,8},{10,9},{11,1... | collective-permute-start | bytes 98312 | tf_op jit(solution)/shard_map/ppermute | solution.py:346
  10.9 2.5 %collective-permute-done.5.corners_east = bf16[2,16,512]{2,1,0:T(8,128)(2,1)S(1)} collective-permute-done((bf16[2,16,512]{2,1,0:T(8,128)(2,1)S(1)}, bf16[2,16,512]{2,1,0:T(8,128)(2,1)S(1)}, u32[]{:S(2)}, u32[]{:S(2)}) %collective-permute-start.5) | collective-permute-done | bytes 32800 | tf_op jit(solution)/shard_map/ppermute | solution.py:346
  15.2 15.7 %shard_map.110 = (bf16[960,512]{1,0:T(8,128)(2,1)}, bf16[960,512]{1,0:T(8,128)(2,1)}, bf16[10,288,384]{2,1,0:T(8,128)(2,1)}, bf16[1024,512]{1,0:T(8,128)(2,1)}, ...) custom-call(s32[1]{0:T(128)} %bitcast.core_ref, s32[10]{0:T(128)} %reach_ref.1, ...), custom_call_target="tpu_custom_call" | custom-call | flops 10192158720 | bytes 13762560 | tf_op jit(solution)/shard_map/pallas_call | solution.py:317
  31.7 2.2 %collective-permute-done.8 = bf16[2,2,2,128,512]{4,3,2,1,0:T(8,128)(2,1)S(1)} collective-permute-done((bf16[2,2,2,128,512]{4,3,2,1,0:T(8,128)(2,1)}, bf16[2,2,2,128,512]{4,3,2,1,0:T(8,128)(2,1)S(1)}, u32[]{:S(2)}, u32[]{:S(2)}) %collective-permute-start.8) | collective-permute-done | bytes 1048608 | tf_op jit(solution)/shard_map/ppermute | solution.py:46
  33.9 1.6 %convert_add_fusion = f32[2,2,2,128,512]{4,3,2,1,0:T(8,128)S(1)} fusion(bf16[2,2,2,128,512]{4,3,2,1,0:T(8,128)(2,1)} %bitcast.72, bf16[2,2,2,128,512]{4,3,2,1,0:T(8,128)(2,1)S(1)} %collective-permute-done.8), kind=kLoop, calls=%fused_computation | loop fusion | flops 1572864 | bytes 4194304 | tf_op jit(solution)/shard_map/add | solution.py:84
  36.9 1.2 %collective-permute-start.7 = (bf16[2,2,96,512]{3,2,1,0:T(8,128)(2,1)S(1)}, bf16[2,2,96,512]{3,2,1,0:T(8,128)(2,1)S(1)}, u32[]{:S(2)}, u32[]{:S(2)}) collective-permute-start(bf16[2,2,96,512]{3,2,1,0:T(8,128)(2,1)S(1)} %fusion.3), channel_id=1, source_target_pairs={{0,2},{1,5},{2,0},{3,7},{4,6},{5,1},{6,4},{7,3},{8,10},{9,13},{10,... | collective-permute-start | bytes 1179656 | tf_op jit(solution)/shard_map/ppermute | solution.py:46
  38.0 8.7 %shard_map.111 = (bf16[10,96,512]{2,1,0:T(8,128)(2,1)}, f32[2,96,512]{2,1,0:T(8,128)}, bf16[12,16,512]{2,1,0:T(8,128)(2,1)}, bf16[12,16,512]{2,1,0:T(8,128)(2,1)}) custom-call(bf16[960,512]{1,0:T(8,128)(2,1)} %get-tuple-element.72.hg_in, bf16[3,512,512]{2,1,0:T(8,128)(2,1)} %mix_in.3, bf16[10,288,384]{2,1,0:T(8,128)(2,1)} %get-tuple-element.73.bands_in), custom_call_target="tpu_custom_call" | custom-call | flops 2642411520 | bytes 11796480 | tf_op jit(solution)/shard_map/pallas_call | solution.py:317
  47.6 2.3 %collective-permute-start.11 = (bf16[2,128,512]{2,1,0:T(8,128)(2,1)S(1)}, bf16[2,128,512]{2,1,0:T(8,128)(2,1)S(1)}, u32[]{:S(2)}, u32[]{:S(2)}) collective-permute-start(bf16[2,128,512]{2,1,0:T(8,128)(2,1)S(1)} %fusion.4), channel_id=1, source_target_pairs={{0,4},{1,3},{2,6},{3,1},{4,0},{5,7},{6,2},{7,5},{8,12},{9,11},{10,... | collective-permute-start | bytes 786440 | tf_op jit(solution)/shard_map/ppermute | solution.py:46
  50.0 1.7 %collective-permute-start.10 = (bf16[2,96,512]{2,1,0:T(8,128)(2,1)S(1)}, bf16[2,96,512]{2,1,0:T(8,128)(2,1)S(1)}, u32[]{:S(2)}, u32[]{:S(2)}) collective-permute-start(bf16[2,96,512]{2,1,0:T(8,128)(2,1)S(1)} %fusion.6), channel_id=1, source_target_pairs={{0,8},{1,9},{2,10},{3,11},{4,12},{5,13},{6,14},{7,15},{8,0},{9,1},... | collective-permute-start | bytes 589832 | tf_op jit(solution)/shard_map/ppermute | solution.py:46
  51.7 2.5 %collective-permute-done.11 = bf16[2,128,512]{2,1,0:T(8,128)(2,1)S(1)} collective-permute-done((bf16[2,128,512]{2,1,0:T(8,128)(2,1)S(1)}, bf16[2,128,512]{2,1,0:T(8,128)(2,1)S(1)}, u32[]{:S(2)}, u32[]{:S(2)}) %collective-permute-start.11) | collective-permute-done | bytes 262176 | tf_op jit(solution)/shard_map/ppermute | solution.py:46
  54.3 2.2 %collective-permute-start.13 = (bf16[128,512]{1,0:T(8,128)(2,1)S(1)}, bf16[128,512]{1,0:T(8,128)(2,1)S(1)}, u32[]{:S(2)}, u32[]{:S(2)}) collective-permute-start(bf16[128,512]{1,0:T(8,128)(2,1)S(1)} %fusion.8), channel_id=1, source_target_pairs={{0,8},{1,9},{2,10},{3,11},{4,12},{5,13},{6,14},{7,15},{8,0},{9,1},... | collective-permute-start | bytes 393224 | tf_op jit(solution)/shard_map/ppermute | solution.py:46
  56.8 1.7 %collective-permute-start.12 = (bf16[96,512]{1,0:T(8,128)(2,1)S(1)}, bf16[96,512]{1,0:T(8,128)(2,1)S(1)}, u32[]{:S(2)}, u32[]{:S(2)}) collective-permute-start(bf16[96,512]{1,0:T(8,128)(2,1)S(1)} %fusion.10), channel_id=1, source_target_pairs={{0,4},{1,3},{2,6},{3,1},{4,0},{5,7},{6,2},{7,5},{8,12},{9,11},{10,... | collective-permute-start | bytes 294920 | tf_op jit(solution)/shard_map/ppermute | solution.py:46
  59.5 3.1 %collective-permute-start.15 = (bf16[128,512]{1,0:T(8,128)(2,1)S(1)}, bf16[128,512]{1,0:T(8,128)(2,1)S(1)}, u32[]{:S(2)}, u32[]{:S(2)}) collective-permute-start(bf16[128,512]{1,0:T(8,128)(2,1)S(1)} %fusion.5), channel_id=1, source_target_pairs={{0,16},{1,17},{2,18},{3,19},{4,20},{5,21},{6,22},{7,23},{8,24},{9,... | collective-permute-start | bytes 393224 | tf_op jit(solution)/shard_map/ppermute | solution.py:46
  62.6 1.7 %collective-permute-start.14 = (bf16[96,512]{1,0:T(8,128)(2,1)S(1)}, bf16[96,512]{1,0:T(8,128)(2,1)S(1)}, u32[]{:S(2)}, u32[]{:S(2)}) collective-permute-start(bf16[96,512]{1,0:T(8,128)(2,1)S(1)} %fusion.7), channel_id=1, source_target_pairs={{0,16},{1,17},{2,18},{3,19},{4,20},{5,21},{6,22},{7,23},{8,24},{9,... | collective-permute-start | bytes 294920 | tf_op jit(solution)/shard_map/ppermute | solution.py:46
  64.4 1.6 %collective-permute-start.22 = (bf16[96,512]{1,0:T(8,128)(2,1)S(1)}, bf16[96,512]{1,0:T(8,128)(2,1)S(1)}, u32[]{:S(2)}, u32[]{:S(2)}) collective-permute-start(bf16[96,512]{1,0:T(8,128)(2,1)S(1)} %get-tuple-element.126), channel_id=1, source_target_pairs={{0,4},{1,5},{2,6},{3,7},{4,0},{5,1},{6,2},{7,3},{8,12},{9,13},{10,... | collective-permute-start | bytes 294920 | tf_op jit(solution)/shard_map/ppermute | solution.py:434
  66.0 1.1 %collective-permute-start.23 = (bf16[96,512]{1,0:T(8,128)(2,1)S(1)}, bf16[96,512]{1,0:T(8,128)(2,1)S(1)}, u32[]{:S(2)}, u32[]{:S(2)}) collective-permute-start(bf16[96,512]{1,0:T(8,128)(2,1)S(1)} %get-tuple-element.125), channel_id=1, source_target_pairs={{0,2},{1,3},{2,0},{3,1},{4,8},{5,9},{6,10},{7,11},{8,4},{9,5},{10,... | collective-permute-start | bytes 294920 | tf_op jit(solution)/shard_map/ppermute | solution.py:435
  67.2 3.7 %collective-permute-done.15 = bf16[128,512]{1,0:T(8,128)(2,1)S(1)} collective-permute-done((bf16[128,512]{1,0:T(8,128)(2,1)S(1)}, bf16[128,512]{1,0:T(8,128)(2,1)S(1)}, u32[]{:S(2)}, u32[]{:S(2)}) %collective-permute-start.15) | collective-permute-done | bytes 131104 | tf_op jit(solution)/shard_map/ppermute | solution.py:46
  70.9 2.0 %collective-permute-start.19 = (bf16[1,128,512]{2,1,0:T(8,128)(2,1)S(1)}, bf16[1,128,512]{2,1,0:T(8,128)(2,1)S(1)}, u32[]{:S(2)}, u32[]{:S(2)}) collective-permute-start(bf16[1,128,512]{2,1,0:T(8,128)(2,1)S(1)} %fusion.9), channel_id=1, source_target_pairs={{0,8},{1,9},{2,10},{3,11},{4,12},{5,13},{6,14},{7,15},{8,0},{9,1},... | collective-permute-start | bytes 393224 | tf_op jit(solution)/shard_map/ppermute | solution.py:46
  73.0 2.1 %collective-permute-start.18 = (bf16[1,96,512]{2,1,0:T(8,128)(2,1)S(1)}, bf16[1,96,512]{2,1,0:T(8,128)(2,1)S(1)}, u32[]{:S(2)}, u32[]{:S(2)}) collective-permute-start(bf16[1,96,512]{2,1,0:T(8,128)(2,1)S(1)} %fusion.11), channel_id=1, source_target_pairs={{0,4},{1,3},{2,6},{3,1},{4,0},{5,7},{6,2},{7,5},{8,12},{9,11},{10,... | collective-permute-start | bytes 294920 | tf_op jit(solution)/shard_map/ppermute | solution.py:46
  75.1 1.5 %collective-permute-done.19 = bf16[1,128,512]{2,1,0:T(8,128)(2,1)S(1)} collective-permute-done((bf16[1,128,512]{2,1,0:T(8,128)(2,1)S(1)}, bf16[1,128,512]{2,1,0:T(8,128)(2,1)S(1)}, u32[]{:S(2)}, u32[]{:S(2)}) %collective-permute-start.19) | collective-permute-done | bytes 131104 | tf_op jit(solution)/shard_map/ppermute | solution.py:46
  76.7 2.3 %collective-permute-start.21 = (bf16[2,128,512]{2,1,0:T(8,128)(2,1)S(1)}, bf16[2,128,512]{2,1,0:T(8,128)(2,1)S(1)}, u32[]{:S(2)}, u32[]{:S(2)}) collective-permute-start(bf16[2,128,512]{2,1,0:T(8,128)(2,1)S(1)} %pad_maximum_fusion.4), channel_id=1, source_target_pairs={{0,4},{1,3},{2,6},{3,1},{4,0},{5,7},{6,2},{7,5},{8,12},{9,11},{10,... | collective-permute-start | bytes 786440 | tf_op jit(solution)/shard_map/ppermute | solution.py:46
  79.8 3.6 %collective-permute-done.21 = bf16[2,128,512]{2,1,0:T(8,128)(2,1)S(1)} collective-permute-done((bf16[2,128,512]{2,1,0:T(8,128)(2,1)S(1)}, bf16[2,128,512]{2,1,0:T(8,128)(2,1)S(1)}, u32[]{:S(2)}, u32[]{:S(2)}) %collective-permute-start.21) | collective-permute-done | bytes 262176 | tf_op jit(solution)/shard_map/ppermute | solution.py:46
  84.1 1.2 %collective-permute-done.20 = bf16[2,96,512]{2,1,0:T(8,128)(2,1)S(1)} collective-permute-done((bf16[2,96,512]{2,1,0:T(8,128)(2,1)S(1)}, bf16[2,96,512]{2,1,0:T(8,128)(2,1)S(1)}, u32[]{:S(2)}, u32[]{:S(2)}) %collective-permute-start.20) | collective-permute-done | bytes 196640 | tf_op jit(solution)/shard_map/ppermute | solution.py:46
  85.4 1.2 %collective-permute-start.24 = (bf16[4,96,512]{2,1,0:T(8,128)(2,1)S(1)}, bf16[4,96,512]{2,1,0:T(8,128)(2,1)S(1)}, u32[]{:S(2)}, u32[]{:S(2)}) collective-permute-start(bf16[4,96,512]{2,1,0:T(8,128)(2,1)S(1)} %pad_maximum_fusion.3), channel_id=1, source_target_pairs={{0,2},{1,5},{2,0},{3,7},{4,6},{5,1},{6,4},{7,3},{8,10},{9,13},{10,... | collective-permute-start | bytes 1179656 | tf_op jit(solution)/shard_map/ppermute | solution.py:46
  86.7 6.0 %collective-permute-done.25 = bf16[4,128,512]{2,1,0:T(8,128)(2,1)S(1)} collective-permute-done((bf16[4,128,512]{2,1,0:T(8,128)(2,1)S(1)}, bf16[4,128,512]{2,1,0:T(8,128)(2,1)S(1)}, u32[]{:S(2)}, u32[]{:S(2)}) %collective-permute-start.25) | collective-permute-done | bytes 524320 | tf_op jit(solution)/shard_map/ppermute | solution.py:46
  92.9 1.3 %fusion.1 = bf16[10,96,512]{2,1,0:T(8,128)(2,1)} fusion(f32[10,16,512]{2,1,0:T(8,128)S(1)} %slice_convert_fusion, f32[10,16,512]{2,1,0:T(8,128)S(1)} %slice_convert_fusion.1, f32[1,96,512]{2,1,0:T(8,128)S(1)} %get-tuple-element.116, f32[1,96,512]{2,1,0:T(8,128)S(1)} %get-tuple-element.115, bf16[10,96,512]{2,1,0:T(8,128)(2,1)S(1)} %copy-done.7, ...), kind=kLoop, calls=%fused_computation.3 | loop fusion | flops 3932160 | bytes 3015080 | tf_op jit(solution)/shard_map/convert_element_type | solution.py:452
  95.6 1.3 %collective-permute-done.24 = bf16[4,96,512]{2,1,0:T(8,128)(2,1)S(1)} collective-permute-done((bf16[4,96,512]{2,1,0:T(8,128)(2,1)S(1)}, bf16[4,96,512]{2,1,0:T(8,128)(2,1)S(1)}, u32[]{:S(2)}, u32[]{:S(2)}) %collective-permute-start.24) | collective-permute-done | bytes 393248 | tf_op jit(solution)/shard_map/ppermute | solution.py:46
  99.5 1.2 %constant_dynamic-update-slice_fusion = bf16[3,512,512]{2,1,0:T(8,128)(2,1)S(1)} fusion(bf16[3,512,512]{2,1,0:T(8,128)(2,1)S(1)} %constant_dynamic-update-slice_fusion.3, bf16[3,256,512]{2,1,0:T(8,128)(2,1)} %bitcast.36, s32[]{:T(128)S(6)} %select_n.258), kind=kLoop, calls=%fused_computation.67 | loop fusion | bytes 1572868 | tf_op jit(solution)/shard_map/dynamic_update_slice | solution.py:117
  100.8 1.1 %copy-done = bf16[3,512,512]{2,1,0:T(8,128)(2,1)} copy-done((bf16[3,512,512]{2,1,0:T(8,128)(2,1)}, bf16[3,512,512]{2,1,0:T(8,128)(2,1)S(1)}, u32[]{:S(2)}) %copy-start) | copy-done | bytes 1572888
  (118 shorter events, 14.9 us)
Async XLA Ops:
  1.6 7.4 %collective-permute-start = (bf16[96,512]{1,0:T(8,128)(2,1)S(1)}, bf16[96,512]{1,0:T(8,128)(2,1)S(1)}, u32[]{:S(2)}, u32[]{:S(2)}) collective-permute-start(bf16[96,512]{1,0:T(8,128)(2,1)S(1)} %get-tuple-element.110), channel_id=1, source_target_pairs={{0,2},{1,3},{2,0},{3,1},{4,8},{5,9},{6,10},{7,11},{8,4},{9,5},{10,... | collective-permute-start | bytes 294920 | tf_op jit(solution)/shard_map/ppermute | solution.py:338
  4.6 5.0 %collective-permute-start.1 = (bf16[96,512]{1,0:T(8,128)(2,1)S(1)}, bf16[96,512]{1,0:T(8,128)(2,1)S(1)}, u32[]{:S(2)}, u32[]{:S(2)}) collective-permute-start(bf16[96,512]{1,0:T(8,128)(2,1)S(1)} %get-tuple-element.109), channel_id=1, source_target_pairs={{0,4},{1,5},{2,6},{3,7},{4,0},{5,1},{6,2},{7,3},{8,12},{9,13},{10,... | collective-permute-start | bytes 294920 | tf_op jit(solution)/shard_map/ppermute | solution.py:337
  7.2 7.3 %collective-permute-start.2 = (bf16[10,16,512]{2,1,0:T(8,128)(2,1)S(1)}, bf16[10,16,512]{2,1,0:T(8,128)(2,1)S(1)}, u32[]{:S(2)}, u32[]{:S(2)}) collective-permute-start(bf16[10,16,512]{2,1,0:T(8,128)(2,1)S(1)} %get-tuple-element.108), channel_id=1, source_target_pairs={{0,1},{1,2},{2,3},{3,0},{4,5},{5,6},{6,7},{7,4},{8,9},{9,10},{10,1... | collective-permute-start | bytes 491528 | tf_op jit(solution)/shard_map/ppermute | solution.py:339
  7.2 7.3 %collective-permute-start.3 = (bf16[10,16,512]{2,1,0:T(8,128)(2,1)S(1)}, bf16[10,16,512]{2,1,0:T(8,128)(2,1)S(1)}, u32[]{:S(2)}, u32[]{:S(2)}) collective-permute-start(bf16[10,16,512]{2,1,0:T(8,128)(2,1)S(1)} %get-tuple-element.107), channel_id=1, source_target_pairs={{1,0},{2,1},{3,2},{0,3},{5,4},{6,5},{7,6},{4,7},{9,8},{10,9},{11,1... | collective-permute-start | bytes 491528 | tf_op jit(solution)/shard_map/ppermute | solution.py:340
  9.7 4.8 %copy-start.10 = (bf16[96,512]{1,0:T(8,128)(2,1)}, bf16[96,512]{1,0:T(8,128)(2,1)S(1)}, u32[]{:S(2)}) copy-start(bf16[96,512]{1,0:T(8,128)(2,1)S(1)} %get-tuple-element.131.south) | copy-start | bytes 294916
  9.7 4.8 %copy-start.11 = (bf16[96,512]{1,0:T(8,128)(2,1)}, bf16[96,512]{1,0:T(8,128)(2,1)S(1)}, u32[]{:S(2)}) copy-start(bf16[96,512]{1,0:T(8,128)(2,1)S(1)} %get-tuple-element.132.north) | copy-start | bytes 294916
  9.7 3.7 %collective-permute-start.5 = (bf16[2,16,512]{2,1,0:T(8,128)(2,1)S(1)}, bf16[2,16,512]{2,1,0:T(8,128)(2,1)S(1)}, u32[]{:S(2)}, u32[]{:S(2)}) collective-permute-start(bf16[2,16,512]{2,1,0:T(8,128)(2,1)S(1)} %pad_maximum_fusion.7), channel_id=1, source_target_pairs={{1,0},{2,1},{3,2},{0,3},{5,4},{6,5},{7,6},{4,7},{9,8},{10,9},{11,1... | collective-permute-start | bytes 98312 | tf_op jit(solution)/shard_map/ppermute | solution.py:346
  10.9 3.6 %collective-permute-start.4 = (bf16[2,16,512]{2,1,0:T(8,128)(2,1)S(1)}, bf16[2,16,512]{2,1,0:T(8,128)(2,1)S(1)}, u32[]{:S(2)}, u32[]{:S(2)}) collective-permute-start(bf16[2,16,512]{2,1,0:T(8,128)(2,1)S(1)} %pad_maximum_fusion.6), channel_id=1, source_target_pairs={{0,1},{1,2},{2,3},{3,0},{4,5},{5,6},{6,7},{7,4},{8,9},{9,10},{10,1... | collective-permute-start | bytes 98312 | tf_op jit(solution)/shard_map/ppermute | solution.py:344
  31.0 2.9 %collective-permute-start.8 = (bf16[2,2,2,128,512]{4,3,2,1,0:T(8,128)(2,1)}, bf16[2,2,2,128,512]{4,3,2,1,0:T(8,128)(2,1)S(1)}, u32[]{:S(2)}, u32[]{:S(2)}) collective-permute-start(bf16[2,2,2,128,512]{4,3,2,1,0:T(8,128)(2,1)} %bitcast.74), channel_id=1, source_target_pairs={{0,1},{1,0},{2,3},{3,2},{4,5},{5,4},{6,7},{7,6},{8,9},{9,8},{10,11... | collective-permute-start | bytes 3145736 | tf_op jit(solution)/shard_map/ppermute | solution.py:46
  31.1 5.5 %collective-permute-start.6 = (bf16[2,2,2,96,512]{4,3,2,1,0:T(8,128)(2,1)}, bf16[2,2,2,96,512]{4,3,2,1,0:T(8,128)(2,1)S(1)}, u32[]{:S(2)}, u32[]{:S(2)}) collective-permute-start(bf16[2,2,2,96,512]{4,3,2,1,0:T(8,128)(2,1)} %bitcast.76), channel_id=1, source_target_pairs={{0,1},{1,0},{2,3},{3,2},{4,5},{5,4},{6,7},{7,6},{8,9},{9,8},{10,11... | collective-permute-start | bytes 2359304 | tf_op jit(solution)/shard_map/ppermute | solution.py:46
  35.6 11.7 %collective-permute-start.9 = (bf16[2,2,128,512]{3,2,1,0:T(8,128)(2,1)S(1)}, bf16[2,2,128,512]{3,2,1,0:T(8,128)(2,1)S(1)}, u32[]{:S(2)}, u32[]{:S(2)}) collective-permute-start(bf16[2,2,128,512]{3,2,1,0:T(8,128)(2,1)S(1)} %fusion.2), channel_id=1, source_target_pairs={{0,2},{1,5},{2,0},{3,7},{4,6},{5,1},{6,4},{7,3},{8,10},{9,13},{10,... | collective-permute-start | bytes 1572872 | tf_op jit(solution)/shard_map/ppermute | solution.py:46
  36.9 13.0 %collective-permute-start.7 = (bf16[2,2,96,512]{3,2,1,0:T(8,128)(2,1)S(1)}, bf16[2,2,96,512]{3,2,1,0:T(8,128)(2,1)S(1)}, u32[]{:S(2)}, u32[]{:S(2)}) collective-permute-start(bf16[2,2,96,512]{3,2,1,0:T(8,128)(2,1)S(1)} %fusion.3), channel_id=1, source_target_pairs={{0,2},{1,5},{2,0},{3,7},{4,6},{5,1},{6,4},{7,3},{8,10},{9,13},{10,... | collective-permute-start | bytes 1179656 | tf_op jit(solution)/shard_map/ppermute | solution.py:46
  46.7 17.5 %collective-permute-start.16 = (bf16[12,16,512]{2,1,0:T(8,128)(2,1)}, bf16[12,16,512]{2,1,0:T(8,128)(2,1)S(1)}, u32[]{:S(2)}, u32[]{:S(2)}) collective-permute-start(bf16[12,16,512]{2,1,0:T(8,128)(2,1)} %get-tuple-element.74), channel_id=1, source_target_pairs={{1,0},{2,1},{3,2},{0,3},{5,4},{6,5},{7,6},{4,7},{9,8},{10,9},{11,1... | collective-permute-start | bytes 589832 | tf_op jit(solution)/shard_map/ppermute | solution.py:464
  47.3 17.0 %collective-permute-start.17 = (bf16[12,16,512]{2,1,0:T(8,128)(2,1)}, bf16[12,16,512]{2,1,0:T(8,128)(2,1)S(1)}, u32[]{:S(2)}, u32[]{:S(2)}) collective-permute-start(bf16[12,16,512]{2,1,0:T(8,128)(2,1)} %get-tuple-element.83), channel_id=1, source_target_pairs={{0,1},{1,2},{2,3},{3,0},{4,5},{5,6},{6,7},{7,4},{8,9},{9,10},{10,1... | collective-permute-start | bytes 589832 | tf_op jit(solution)/shard_map/ppermute | solution.py:465
  47.6 6.7 %collective-permute-start.11 = (bf16[2,128,512]{2,1,0:T(8,128)(2,1)S(1)}, bf16[2,128,512]{2,1,0:T(8,128)(2,1)S(1)}, u32[]{:S(2)}, u32[]{:S(2)}) collective-permute-start(bf16[2,128,512]{2,1,0:T(8,128)(2,1)S(1)} %fusion.4), channel_id=1, source_target_pairs={{0,4},{1,3},{2,6},{3,1},{4,0},{5,7},{6,2},{7,5},{8,12},{9,11},{10,... | collective-permute-start | bytes 786440 | tf_op jit(solution)/shard_map/ppermute | solution.py:46
  50.0 14.3 %copy-start.9 = (f32[2,96,512]{2,1,0:T(8,128)S(1)}, f32[2,96,512]{2,1,0:T(8,128)}, u32[]{:S(2)}) copy-start(f32[2,96,512]{2,1,0:T(8,128)} %get-tuple-element.82) | copy-start | bytes 1179652
  50.0 6.6 %collective-permute-start.10 = (bf16[2,96,512]{2,1,0:T(8,128)(2,1)S(1)}, bf16[2,96,512]{2,1,0:T(8,128)(2,1)S(1)}, u32[]{:S(2)}, u32[]{:S(2)}) collective-permute-start(bf16[2,96,512]{2,1,0:T(8,128)(2,1)S(1)} %fusion.6), channel_id=1, source_target_pairs={{0,8},{1,9},{2,10},{3,11},{4,12},{5,13},{6,14},{7,15},{8,0},{9,1},... | collective-permute-start | bytes 589832 | tf_op jit(solution)/shard_map/ppermute | solution.py:46
  54.3 5.1 %collective-permute-start.13 = (bf16[128,512]{1,0:T(8,128)(2,1)S(1)}, bf16[128,512]{1,0:T(8,128)(2,1)S(1)}, u32[]{:S(2)}, u32[]{:S(2)}) collective-permute-start(bf16[128,512]{1,0:T(8,128)(2,1)S(1)} %fusion.8), channel_id=1, source_target_pairs={{0,8},{1,9},{2,10},{3,11},{4,12},{5,13},{6,14},{7,15},{8,0},{9,1},... | collective-permute-start | bytes 393224 | tf_op jit(solution)/shard_map/ppermute | solution.py:46
  56.8 5.8 %collective-permute-start.12 = (bf16[96,512]{1,0:T(8,128)(2,1)S(1)}, bf16[96,512]{1,0:T(8,128)(2,1)S(1)}, u32[]{:S(2)}, u32[]{:S(2)}) collective-permute-start(bf16[96,512]{1,0:T(8,128)(2,1)S(1)} %fusion.10), channel_id=1, source_target_pairs={{0,4},{1,3},{2,6},{3,1},{4,0},{5,7},{6,2},{7,5},{8,12},{9,11},{10,... | collective-permute-start | bytes 294920 | tf_op jit(solution)/shard_map/ppermute | solution.py:46
  59.5 11.4 %collective-permute-start.15 = (bf16[128,512]{1,0:T(8,128)(2,1)S(1)}, bf16[128,512]{1,0:T(8,128)(2,1)S(1)}, u32[]{:S(2)}, u32[]{:S(2)}) collective-permute-start(bf16[128,512]{1,0:T(8,128)(2,1)S(1)} %fusion.5), channel_id=1, source_target_pairs={{0,16},{1,17},{2,18},{3,19},{4,20},{5,21},{6,22},{7,23},{8,24},{9,... | collective-permute-start | bytes 393224 | tf_op jit(solution)/shard_map/ppermute | solution.py:46
  62.6 10.4 %collective-permute-start.14 = (bf16[96,512]{1,0:T(8,128)(2,1)S(1)}, bf16[96,512]{1,0:T(8,128)(2,1)S(1)}, u32[]{:S(2)}, u32[]{:S(2)}) collective-permute-start(bf16[96,512]{1,0:T(8,128)(2,1)S(1)} %fusion.7), channel_id=1, source_target_pairs={{0,16},{1,17},{2,18},{3,19},{4,20},{5,21},{6,22},{7,23},{8,24},{9,... | collective-permute-start | bytes 294920 | tf_op jit(solution)/shard_map/ppermute | solution.py:46
  64.4 14.5 %collective-permute-start.22 = (bf16[96,512]{1,0:T(8,128)(2,1)S(1)}, bf16[96,512]{1,0:T(8,128)(2,1)S(1)}, u32[]{:S(2)}, u32[]{:S(2)}) collective-permute-start(bf16[96,512]{1,0:T(8,128)(2,1)S(1)} %get-tuple-element.126), channel_id=1, source_target_pairs={{0,4},{1,5},{2,6},{3,7},{4,0},{5,1},{6,2},{7,3},{8,12},{9,13},{10,... | collective-permute-start | bytes 294920 | tf_op jit(solution)/shard_map/ppermute | solution.py:434
  66.0 13.0 %collective-permute-start.23 = (bf16[96,512]{1,0:T(8,128)(2,1)S(1)}, bf16[96,512]{1,0:T(8,128)(2,1)S(1)}, u32[]{:S(2)}, u32[]{:S(2)}) collective-permute-start(bf16[96,512]{1,0:T(8,128)(2,1)S(1)} %get-tuple-element.125), channel_id=1, source_target_pairs={{0,2},{1,3},{2,0},{3,1},{4,8},{5,9},{6,10},{7,11},{8,4},{9,5},{10,... | collective-permute-start | bytes 294920 | tf_op jit(solution)/shard_map/ppermute | solution.py:435
  70.9 5.7 %collective-permute-start.19 = (bf16[1,128,512]{2,1,0:T(8,128)(2,1)S(1)}, bf16[1,128,512]{2,1,0:T(8,128)(2,1)S(1)}, u32[]{:S(2)}, u32[]{:S(2)}) collective-permute-start(bf16[1,128,512]{2,1,0:T(8,128)(2,1)S(1)} %fusion.9), channel_id=1, source_target_pairs={{0,8},{1,9},{2,10},{3,11},{4,12},{5,13},{6,14},{7,15},{8,0},{9,1},... | collective-permute-start | bytes 393224 | tf_op jit(solution)/shard_map/ppermute | solution.py:46
  73.0 6.0 %collective-permute-start.18 = (bf16[1,96,512]{2,1,0:T(8,128)(2,1)S(1)}, bf16[1,96,512]{2,1,0:T(8,128)(2,1)S(1)}, u32[]{:S(2)}, u32[]{:S(2)}) collective-permute-start(bf16[1,96,512]{2,1,0:T(8,128)(2,1)S(1)} %fusion.11), channel_id=1, source_target_pairs={{0,4},{1,3},{2,6},{3,1},{4,0},{5,7},{6,2},{7,5},{8,12},{9,11},{10,... | collective-permute-start | bytes 294920 | tf_op jit(solution)/shard_map/ppermute | solution.py:46
  76.7 6.6 %collective-permute-start.21 = (bf16[2,128,512]{2,1,0:T(8,128)(2,1)S(1)}, bf16[2,128,512]{2,1,0:T(8,128)(2,1)S(1)}, u32[]{:S(2)}, u32[]{:S(2)}) collective-permute-start(bf16[2,128,512]{2,1,0:T(8,128)(2,1)S(1)} %pad_maximum_fusion.4), channel_id=1, source_target_pairs={{0,4},{1,3},{2,6},{3,1},{4,0},{5,7},{6,2},{7,5},{8,12},{9,11},{10,... | collective-permute-start | bytes 786440 | tf_op jit(solution)/shard_map/ppermute | solution.py:46
  79.1 6.3 %collective-permute-start.20 = (bf16[2,96,512]{2,1,0:T(8,128)(2,1)S(1)}, bf16[2,96,512]{2,1,0:T(8,128)(2,1)S(1)}, u32[]{:S(2)}, u32[]{:S(2)}) collective-permute-start(bf16[2,96,512]{2,1,0:T(8,128)(2,1)S(1)} %pad_maximum_fusion.5), channel_id=1, source_target_pairs={{0,8},{1,9},{2,10},{3,11},{4,12},{5,13},{6,14},{7,15},{8,0},{9,1},... | collective-permute-start | bytes 589832 | tf_op jit(solution)/shard_map/ppermute | solution.py:46
  83.4 9.2 %collective-permute-start.25 = (bf16[4,128,512]{2,1,0:T(8,128)(2,1)S(1)}, bf16[4,128,512]{2,1,0:T(8,128)(2,1)S(1)}, u32[]{:S(2)}, u32[]{:S(2)}) collective-permute-start(bf16[4,128,512]{2,1,0:T(8,128)(2,1)S(1)} %pad_maximum_fusion.2), channel_id=1, source_target_pairs={{0,2},{1,5},{2,0},{3,7},{4,6},{5,1},{6,4},{7,3},{8,10},{9,13},{10,... | collective-permute-start | bytes 1572872 | tf_op jit(solution)/shard_map/ppermute | solution.py:46
  85.4 7.5 %copy-start.7 = (bf16[10,96,512]{2,1,0:T(8,128)(2,1)S(1)}, bf16[10,96,512]{2,1,0:T(8,128)(2,1)}, u32[]{:S(2)}) copy-start(bf16[10,96,512]{2,1,0:T(8,128)(2,1)} %get-tuple-element.92) | copy-start | bytes 2949124
  85.4 11.4 %collective-permute-start.24 = (bf16[4,96,512]{2,1,0:T(8,128)(2,1)S(1)}, bf16[4,96,512]{2,1,0:T(8,128)(2,1)S(1)}, u32[]{:S(2)}, u32[]{:S(2)}) collective-permute-start(bf16[4,96,512]{2,1,0:T(8,128)(2,1)S(1)} %pad_maximum_fusion.3), channel_id=1, source_target_pairs={{0,2},{1,5},{2,0},{3,7},{4,6},{5,1},{6,4},{7,3},{8,10},{9,13},{10,... | collective-permute-start | bytes 1179656 | tf_op jit(solution)/shard_map/ppermute | solution.py:46
  92.9 4.5 %collective-permute-start.26 = (bf16[8,128,512]{2,1,0:T(8,128)(2,1)S(1)}, bf16[8,128,512]{2,1,0:T(8,128)(2,1)S(1)}, u32[]{:S(2)}, u32[]{:S(2)}) collective-permute-start(bf16[8,128,512]{2,1,0:T(8,128)(2,1)S(1)} %pad_maximum_fusion), channel_id=1, source_target_pairs={{0,1},{1,0},{2,3},{3,2},{4,5},{5,4},{6,7},{7,6},{8,9},{9,8},{10,11... | collective-permute-start | bytes 3145736 | tf_op jit(solution)/shard_map/ppermute | solution.py:46
  97.0 2.5 %collective-permute-start.27 = (bf16[8,96,512]{2,1,0:T(8,128)(2,1)S(1)}, bf16[8,96,512]{2,1,0:T(8,128)(2,1)}, u32[]{:S(2)}, u32[]{:S(2)}) collective-permute-start(bf16[8,96,512]{2,1,0:T(8,128)(2,1)S(1)} %pad_maximum_fusion.1), channel_id=1, source_target_pairs={{0,1},{1,0},{2,3},{3,2},{4,5},{5,4},{6,7},{7,6},{8,9},{9,8},{10,11... | collective-permute-start | bytes 2359304 | tf_op jit(solution)/shard_map/ppermute | solution.py:46
  (12 other events, 16.0 us)

commit v4 on v3

--- a/solution.py
+++ b/solution.py
@@ -146,12 +146,26 @@
         copy.wait()
 
 
+def act_grad_kernel(cot_in, down_in, out, cot, down, ag, sems):
+    points = cot.shape[0]
+    parts = [pl.ds(i * (points // 3), points // 3) for i in range(3)]
+    weights = started([(down_in, down)], sems)
+    loads = started([(cot_in.at[at], cot.at[at]) for at in parts], sems, 1)
+    finish(weights)
+    stores = []
+    for i, at in enumerate(parts):
+        finish(loads[i : i + 1])
+        ag[at, :] = dot(cot[at, :], down[...], OVER_LANES).astype(ag.dtype)
+        stores += started([(ag.at[at], out.at[at])], sems, 4 + i)
+    finish(stores)
+
+
 def main_kernel(
     core_ref, reach_ref, field, north, south, west, east, corners_west, corners_east, taps_in,
-    mix_in, up_in, down_in, cot_in,
+    mix_in, up_in, down_in, cot_in, ag_in,
     block_out, hg_out, bands_out, mlp_send_out, mlp_keep_out, mix_send_out, mix_keep_out,
     ext, taps, lines, bands, mix, up, down, cot, feats, hidden, act, pre_grad, hg, block, turned, pre_a,
-    pre_b, ag_a, ag_b, mlp_send, mlp_keep, mix_send, mix_keep, sems
+    pre_b, ag, mlp_send, mlp_keep, mix_send, mix_keep, sems
 ):
     core = core_ref[0]
     rows, cols, channels = field.shape
@@ -177,7 +191,8 @@
         sems,
     )
     late = 10
-    weights = started([(mix_in, mix), (up_in, up), (down_in, down), (cot_in, cot)], sems, late)
+    weights = started([(mix_in, mix), (up_in, up), (ag_in, ag), (cot_in, cot)], sems, late)
+    weights += started([(down_in, down)], sems, late + 13)
     finish(tap_load)
 
     count, width = taps.shape[3], lines.shape[3]
@@ -213,22 +228,19 @@
         hidden[at, :] = total.astype(hidden.dtype)
     finish(weights[1:])
     size = pre_a.shape[0]
-    slots = ((pre_a, ag_a), (pre_b, ag_b))
+    slots = (pre_a, pre_b)
 
     def products(i):
         at = pl.ds(i * size, size)
-        pre, ag = slots[i % 2]
-        pre[...] = dot(hidden[at, :], up[...])
-        ag[...] = dot(cot[at, :], down[...], OVER_LANES)
+        slots[i % 2][...] = dot(hidden[at, :], up[...])
 
     def activation(i):
         at = pl.ds(i * size, size)
-        pre, ag = slots[i % 2]
-        value = pre[...]
+        value = slots[i % 2][...]
         phi = 0.5 * (1.0 + lax.erf(value * inv_root_two))
         act[at, :] = (value * phi).astype(act.dtype)
         slope = phi + value * jnp.exp(-0.5 * value * value) * inv_root_tau
-        pre_grad[at, :] = (ag[...] * slope).astype(pre_grad.dtype)
+        pre_grad[at, :] = (ag[at, :].astype(jnp.float32) * slope).astype(pre_grad.dtype)
 
     products(0)
     for i in range(points // size):
@@ -361,13 +373,28 @@
     core = place.flat % 2
     core_op = core[None].astype(jnp.int32)
     sized = (points // 5, hidden_units)
+    (act_grad,) = call(
+        act_grad_kernel,
+        (cot, down_weight),
+        [anywhere] * 2,
+        [(wide, low)],
+        [anywhere],
+        [
+            pltpu.VMEM(big, low),
+            pltpu.VMEM(down_weight.shape, low),
+            pltpu.VMEM(wide, low),
+            pltpu.SemaphoreType.DMA((7,)),
+        ],
+        gemm,
+        3 * points * hidden_units * 2,
+    )
     block_out, hidden_grad, bands, mlp_send, mlp_keep, mix_send, mix_keep = call(
         main_kernel,
         (
             core_op, row_reach, field_in, north, south, west, east, corners_west, corners_east,
-            kernel_taps, mix_weight, up_weight, down_weight, cot,
+            kernel_taps, mix_weight, up_weight, down_weight, cot, act_grad,
         ),
-        [smem] * 2 + [anywhere] * 12,
+        [smem] * 2 + [anywhere] * 13,
         [(big, low), (big, low), (band_shape, low), (mlp_half, low), (mlp_half, low), (mix_half, low), (mix_half, low)],
         [anywhere] * 7,
         [
@@ -388,13 +415,12 @@
             pltpu.VMEM((channels, points), low),
             pltpu.VMEM(sized, full),
             pltpu.VMEM(sized, full),
-            pltpu.VMEM(sized, full),
-            pltpu.VMEM(sized, full),
+            pltpu.VMEM(wide, low),
             pltpu.VMEM(mlp_half, low),
             pltpu.VMEM(mlp_half, low),
             pltpu.VMEM(mix_half, low),
             pltpu.VMEM(mix_half, low),
-            pltpu.SemaphoreType.DMA((23,)),
+            pltpu.SemaphoreType.DMA((24,)),
         ],
         band_gemm + 2 * mix_gemm + 6 * gemm,
         7 * points * hidden_units * 2,
@@ -461,14 +487,15 @@
         mix = ring.to_core(mix_keep.reshape(block_shape), mix_send.reshape(block_shape))
         mix_out = ring.leaving(mix, ring.first)
         inner, rims, to_west, to_east = adjoint_of(hidden_grad, mlp_out, mix_out)
-        from_east = lax.ppermute(to_west, "lon", place.west)
-        from_west = lax.ppermute(to_east, "lon", place.east)
         mlp = ring.step(mlp, mlp_out, first_mask, ring.first, to_west)
         mlp_out = ring.leaving(mlp, ring.second)
         mix = ring.step(mix, mix_out, first_mask, ring.first, mlp_out)
         mix_out = ring.leaving(mix, ring.near)
         mlp = ring.step(mlp, mlp_out, second_mask, ring.second, mix_out)
         mlp_out = ring.leaving(mlp, ring.near)
+        to_west, to_east, _ = lax.optimization_barrier((to_west, to_east, mlp_out))
+        from_east = lax.ppermute(to_west, "lon", place.west)
+        from_west = lax.ppermute(to_east, "lon", place.east)
         mix = ring.step(mix, mix_out, near_mask, ring.near, mlp_out)
         mix_out = ring.leaving(mix, ring.second)
         mlp = ring.step(mlp, mlp_out, near_mask, ring.near, mix_out).astype(low)

time: 102 us -> 104 us (1.020)
  starting transfers between devices: 35.3 us -> 30.6 us
  waiting for transfers between devices: 28.1 us -> 31.4 us
  Pallas kernels: 24.4 us -> 27.5 us
    ppermute x18, waiting for transfers between devices: 23.8 us -> 29.2 us  [send_along(): return lax.ppermute(block, AXES, route(place, mask_of))]
    ppermute x18, starting transfers between devices: 24.5 us -> 20.9 us  [send_along(): return lax.ppermute(block, AXES, route(place, mask_of))]
    pallas_call x2 -> x3, Pallas kernels: 24.4 us -> 27.5 us  [call(): pl.pallas_call(kernel, out_shape=[jax.ShapeDtypeStruct(shape, kind) for s...]
    ppermute x1, waiting for transfers between devices: 2.54 us -> 0.01 us  [local(): corners_east = lax.ppermute(corners, 'lon', place.west)]
    ppermute x1, waiting for transfers between devices: 0.01 us -> 1.43 us  [local(): from_west = lax.ppermute(to_east, 'lon', place.east)]
    ppermute x1, starting transfers between devices: 1.57 us -> 0.45 us  [beyond(): near = lax.ppermute(near, AXES, place.pairs)]
    unnamed x32 -> x36, local copies, waits for them, and re-layouts: 4.13 us -> 4.15 us
  transfers between devices with their start and end apart: 28 -> 28, of which waited for: 15 -> 13; matrix products, arithmetic and copies ran while one was open for 6% -> 6% of each run, Pallas kernels for 9% -> 12%
where the time goes in v4:
time: 104 us
  waiting for transfers between devices  31.4 us (30%)
  starting transfers between devices  30.6 us (29%)
  Pallas kernels  27.5 us (26%)
  local copies, waits for them, and re-layouts  7.66 us (7%)
  other arithmetic  5.37 us (5%)
  between operations  1.36 us (1%)
    ppermute x18, waiting for transfers between devices, send_along(): return lax.ppermute(block, AXES, route(place, mask_of))  29.2 us
    pallas_call x3, Pallas kernels, call(): pl.pallas_call(kernel, out_shape=[jax.ShapeDtypeStruct(shape, kind) for s...  27.5 us
    ppermute x18, starting transfers between devices, send_along(): return lax.ppermute(block, AXES, route(place, mask_of))  20.9 us
    unnamed x36, local copies, waits for them, and re-layouts  4.15 us
    ppermute x1, starting transfers between devices, local(): lax.ppermute(jnp.where(place.even, top, bottom), AXES, place.bridges)  3.03 us
  transfers between devices with their start and end apart: 28, of which 13 were waited for; matrix products, arithmetic and copies ran while one was open for 6% of the time, Pallas kernels for 12%

profile of v4, /device:TPU:0, one launch (start us, length us, event | category | flops | bytes accessed | tf_op | source)
XLA Modules:
  0.0 103.8 jit_solution(436966502908223857)
XLA Ops:
  1.6 3.0 %collective-permute-start = (bf16[96,512]{1,0:T(8,128)(2,1)S(1)}, bf16[96,512]{1,0:T(8,128)(2,1)S(1)}, u32[]{:S(2)}, u32[]{:S(2)}) collective-permute-start(bf16[96,512]{1,0:T(8,128)(2,1)S(1)} %get-tuple-element.114), channel_id=1, source_target_pairs={{0,2},{1,3},{2,0},{3,1},{4,8},{5,9},{6,10},{7,11},{8,4},{9,5},{10,... | collective-permute-start | bytes 294920 | tf_op jit(solution)/shard_map/ppermute | solution.py:350
  4.6 1.5 %collective-permute-start.1 = (bf16[96,512]{1,0:T(8,128)(2,1)S(1)}, bf16[96,512]{1,0:T(8,128)(2,1)S(1)}, u32[]{:S(2)}, u32[]{:S(2)}) collective-permute-start(bf16[96,512]{1,0:T(8,128)(2,1)S(1)} %get-tuple-element.113), channel_id=1, source_target_pairs={{0,4},{1,5},{2,6},{3,7},{4,0},{5,1},{6,2},{7,3},{8,12},{9,13},{10,... | collective-permute-start | bytes 294920 | tf_op jit(solution)/shard_map/ppermute | solution.py:349
  6.2 1.0 fusion.14
  7.2 1.7 %collective-permute-start.3 = (bf16[10,16,512]{2,1,0:T(8,128)(2,1)S(1)}, bf16[10,16,512]{2,1,0:T(8,128)(2,1)S(1)}, u32[]{:S(2)}, u32[]{:S(2)}) collective-permute-start(bf16[10,16,512]{2,1,0:T(8,128)(2,1)S(1)} %get-tuple-element.111), channel_id=1, source_target_pairs={{1,0},{2,1},{3,2},{0,3},{5,4},{6,5},{7,6},{4,7},{9,8},{10,9},{11,1... | collective-permute-start | bytes 491528 | tf_op jit(solution)/shard_map/ppermute | solution.py:352
  9.7 1.2 %collective-permute-start.5 = (bf16[2,16,512]{2,1,0:T(8,128)(2,1)S(1)}, bf16[2,16,512]{2,1,0:T(8,128)(2,1)S(1)}, u32[]{:S(2)}, u32[]{:S(2)}) collective-permute-start(bf16[2,16,512]{2,1,0:T(8,128)(2,1)S(1)} %pad_maximum_fusion.7), channel_id=1, source_target_pairs={{1,0},{2,1},{3,2},{0,3},{5,4},{6,5},{7,6},{4,7},{9,8},{10,9},{11,1... | collective-permute-start | bytes 98312 | tf_op jit(solution)/shard_map/ppermute | solution.py:358
  10.9 3.8 %shard_map.110.ag_in = bf16[960,1024]{1,0:T(8,128)(2,1)} custom-call(bf16[960,512]{1,0:T(8,128)(2,1)} %bitcast.73, bf16[1024,512]{1,0:T(8,128)(2,1)} %down_in.3), custom_call_target="tpu_custom_call" | custom-call | flops 1006632960 | bytes 5898240 | tf_op jit(solution)/shard_map/pallas_call | solution.py:329
  15.6 15.1 %shard_map.111 = (bf16[960,512]{1,0:T(8,128)(2,1)}, bf16[960,512]{1,0:T(8,128)(2,1)}, bf16[10,288,384]{2,1,0:T(8,128)(2,1)}, bf16[1024,512]{1,0:T(8,128)(2,1)}, ...) custom-call(s32[1]{0:T(128)} %bitcast.core_ref, s32[10]{0:T(128)} %reach_ref.1, ...), custom_call_target="tpu_custom_call" | custom-call | flops 10192158720 | bytes 13762560 | tf_op jit(solution)/shard_map/pallas_call | solution.py:329
  31.6 2.3 %collective-permute-done.8 = bf16[2,2,2,128,512]{4,3,2,1,0:T(8,128)(2,1)S(1)} collective-permute-done((bf16[2,2,2,128,512]{4,3,2,1,0:T(8,128)(2,1)}, bf16[2,2,2,128,512]{4,3,2,1,0:T(8,128)(2,1)S(1)}, u32[]{:S(2)}, u32[]{:S(2)}) %collective-permute-start.8) | collective-permute-done | bytes 1048608 | tf_op jit(solution)/shard_map/ppermute | solution.py:46
  33.8 1.6 %convert_add_fusion = f32[2,2,2,128,512]{4,3,2,1,0:T(8,128)S(1)} fusion(bf16[2,2,2,128,512]{4,3,2,1,0:T(8,128)(2,1)} %bitcast.72, bf16[2,2,2,128,512]{4,3,2,1,0:T(8,128)(2,1)S(1)} %collective-permute-done.8), kind=kLoop, calls=%fused_computation | loop fusion | flops 1572864 | bytes 4194304 | tf_op jit(solution)/shard_map/add | solution.py:84
  35.7 1.6 %collective-permute-start.9 = (bf16[2,2,128,512]{3,2,1,0:T(8,128)(2,1)S(1)}, bf16[2,2,128,512]{3,2,1,0:T(8,128)(2,1)S(1)}, u32[]{:S(2)}, u32[]{:S(2)}) collective-permute-start(bf16[2,2,128,512]{3,2,1,0:T(8,128)(2,1)S(1)} %fusion.2), channel_id=1, source_target_pairs={{0,2},{1,5},{2,0},{3,7},{4,6},{5,1},{6,4},{7,3},{8,10},{9,13},{10,... | collective-permute-start | bytes 1572872 | tf_op jit(solution)/shard_map/ppermute | solution.py:46
  38.1 8.5 %shard_map.112 = (bf16[10,96,512]{2,1,0:T(8,128)(2,1)}, f32[2,96,512]{2,1,0:T(8,128)}, bf16[12,16,512]{2,1,0:T(8,128)(2,1)}, bf16[12,16,512]{2,1,0:T(8,128)(2,1)}) custom-call(bf16[960,512]{1,0:T(8,128)(2,1)} %get-tuple-element.74.hg_in, bf16[3,512,512]{2,1,0:T(8,128)(2,1)} %mix_in.3, bf16[10,288,384]{2,1,0:T(8,128)(2,1)} %get-tuple-element.75.bands_in), custom_call_target="tpu_custom_call" | custom-call | flops 2642411520 | bytes 11796480 | tf_op jit(solution)/shard_map/pallas_call | solution.py:329
  46.9 2.6 %collective-permute-start.11 = (bf16[2,128,512]{2,1,0:T(8,128)(2,1)S(1)}, bf16[2,128,512]{2,1,0:T(8,128)(2,1)S(1)}, u32[]{:S(2)}, u32[]{:S(2)}) collective-permute-start(bf16[2,128,512]{2,1,0:T(8,128)(2,1)S(1)} %fusion.4), channel_id=1, source_target_pairs={{0,4},{1,3},{2,6},{3,1},{4,0},{5,7},{6,2},{7,5},{8,12},{9,11},{10,... | collective-permute-start | bytes 786440 | tf_op jit(solution)/shard_map/ppermute | solution.py:46
  49.7 2.3 %collective-permute-start.10 = (bf16[2,96,512]{2,1,0:T(8,128)(2,1)S(1)}, bf16[2,96,512]{2,1,0:T(8,128)(2,1)S(1)}, u32[]{:S(2)}, u32[]{:S(2)}) collective-permute-start(bf16[2,96,512]{2,1,0:T(8,128)(2,1)S(1)} %fusion.6), channel_id=1, source_target_pairs={{0,8},{1,9},{2,10},{3,11},{4,12},{5,13},{6,14},{7,15},{8,0},{9,1},... | collective-permute-start | bytes 589832 | tf_op jit(solution)/shard_map/ppermute | solution.py:46
  52.0 1.8 %collective-permute-done.11 = bf16[2,128,512]{2,1,0:T(8,128)(2,1)S(1)} collective-permute-done((bf16[2,128,512]{2,1,0:T(8,128)(2,1)S(1)}, bf16[2,128,512]{2,1,0:T(8,128)(2,1)S(1)}, u32[]{:S(2)}, u32[]{:S(2)}) %collective-permute-start.11) | collective-permute-done | bytes 262176 | tf_op jit(solution)/shard_map/ppermute | solution.py:46
  53.9 2.2 %collective-permute-start.13 = (bf16[128,512]{1,0:T(8,128)(2,1)S(1)}, bf16[128,512]{1,0:T(8,128)(2,1)S(1)}, u32[]{:S(2)}, u32[]{:S(2)}) collective-permute-start(bf16[128,512]{1,0:T(8,128)(2,1)S(1)} %fusion.8), channel_id=1, source_target_pairs={{0,8},{1,9},{2,10},{3,11},{4,12},{5,13},{6,14},{7,15},{8,0},{9,1},... | collective-permute-start | bytes 393224 | tf_op jit(solution)/shard_map/ppermute | solution.py:46
  56.1 1.0 collective-permute-done.10
  57.2 1.7 %collective-permute-start.12 = (bf16[96,512]{1,0:T(8,128)(2,1)S(1)}, bf16[96,512]{1,0:T(8,128)(2,1)S(1)}, u32[]{:S(2)}, u32[]{:S(2)}) collective-permute-start(bf16[96,512]{1,0:T(8,128)(2,1)S(1)} %fusion.10), channel_id=1, source_target_pairs={{0,4},{1,3},{2,6},{3,1},{4,0},{5,7},{6,2},{7,5},{8,12},{9,11},{10,... | collective-permute-start | bytes 294920 | tf_op jit(solution)/shard_map/ppermute | solution.py:46
  59.5 2.7 %collective-permute-start.15 = (bf16[128,512]{1,0:T(8,128)(2,1)S(1)}, bf16[128,512]{1,0:T(8,128)(2,1)S(1)}, u32[]{:S(2)}, u32[]{:S(2)}) collective-permute-start(bf16[128,512]{1,0:T(8,128)(2,1)S(1)} %fusion.5), channel_id=1, source_target_pairs={{0,16},{1,17},{2,18},{3,19},{4,20},{5,21},{6,22},{7,23},{8,24},{9,... | collective-permute-start | bytes 393224 | tf_op jit(solution)/shard_map/ppermute | solution.py:46
  62.3 2.5 %collective-permute-start.14 = (bf16[96,512]{1,0:T(8,128)(2,1)S(1)}, bf16[96,512]{1,0:T(8,128)(2,1)S(1)}, u32[]{:S(2)}, u32[]{:S(2)}) collective-permute-start(bf16[96,512]{1,0:T(8,128)(2,1)S(1)} %fusion.7), channel_id=1, source_target_pairs={{0,16},{1,17},{2,18},{3,19},{4,20},{5,21},{6,22},{7,23},{8,24},{9,... | collective-permute-start | bytes 294920 | tf_op jit(solution)/shard_map/ppermute | solution.py:46
  64.8 1.4 %collective-permute-done.17 = bf16[12,16,512]{2,1,0:T(8,128)(2,1)S(1)} collective-permute-done((bf16[12,16,512]{2,1,0:T(8,128)(2,1)S(1)}, bf16[12,16,512]{2,1,0:T(8,128)(2,1)S(1)}, u32[]{:S(2)}, u32[]{:S(2)}) %collective-permute-start.17) | collective-permute-done | bytes 196640 | tf_op jit(solution)/shard_map/ppermute | solution.py:498
  66.8 1.2 %collective-permute-start.23 = (bf16[96,512]{1,0:T(8,128)(2,1)S(1)}, bf16[96,512]{1,0:T(8,128)(2,1)S(1)}, u32[]{:S(2)}, u32[]{:S(2)}) collective-permute-start(bf16[96,512]{1,0:T(8,128)(2,1)S(1)} %get-tuple-element.129), channel_id=1, source_target_pairs={{0,2},{1,3},{2,0},{3,1},{4,8},{5,9},{6,10},{7,11},{8,4},{9,5},{10,... | collective-permute-start | bytes 294920 | tf_op jit(solution)/shard_map/ppermute | solution.py:461
  68.1 3.6 %collective-permute-done.15 = bf16[128,512]{1,0:T(8,128)(2,1)S(1)} collective-permute-done((bf16[128,512]{1,0:T(8,128)(2,1)S(1)}, bf16[128,512]{1,0:T(8,128)(2,1)S(1)}, u32[]{:S(2)}, u32[]{:S(2)}) %collective-permute-start.15) | collective-permute-done | bytes 131104 | tf_op jit(solution)/shard_map/ppermute | solution.py:46
  72.5 1.2 %collective-permute-done.14 = bf16[96,512]{1,0:T(8,128)(2,1)S(1)} collective-permute-done((bf16[96,512]{1,0:T(8,128)(2,1)S(1)}, bf16[96,512]{1,0:T(8,128)(2,1)S(1)}, u32[]{:S(2)}, u32[]{:S(2)}) %collective-permute-start.14) | collective-permute-done | bytes 98336 | tf_op jit(solution)/shard_map/ppermute | solution.py:46
  74.7 4.1 %collective-permute-done.19 = bf16[1,128,512]{2,1,0:T(8,128)(2,1)S(1)} collective-permute-done((bf16[1,128,512]{2,1,0:T(8,128)(2,1)S(1)}, bf16[1,128,512]{2,1,0:T(8,128)(2,1)S(1)}, u32[]{:S(2)}, u32[]{:S(2)}) %collective-permute-start.19) | collective-permute-done | bytes 131104 | tf_op jit(solution)/shard_map/ppermute | solution.py:46
  79.2 6.0 %collective-permute-done.21 = bf16[2,128,512]{2,1,0:T(8,128)(2,1)S(1)} collective-permute-done((bf16[2,128,512]{2,1,0:T(8,128)(2,1)S(1)}, bf16[2,128,512]{2,1,0:T(8,128)(2,1)S(1)}, u32[]{:S(2)}, u32[]{:S(2)}) %collective-permute-start.21) | collective-permute-done | bytes 262176 | tf_op jit(solution)/shard_map/ppermute | solution.py:46
  86.0 1.8 %collective-permute-start.24 = (bf16[4,96,512]{2,1,0:T(8,128)(2,1)S(1)}, bf16[4,96,512]{2,1,0:T(8,128)(2,1)S(1)}, u32[]{:S(2)}, u32[]{:S(2)}) collective-permute-start(bf16[4,96,512]{2,1,0:T(8,128)(2,1)S(1)} %pad_maximum_fusion.3), channel_id=1, source_target_pairs={{0,2},{1,5},{2,0},{3,7},{4,6},{5,1},{6,4},{7,3},{8,10},{9,13},{10,... | collective-permute-start | bytes 1179656 | tf_op jit(solution)/shard_map/ppermute | solution.py:46
  87.8 6.9 %collective-permute-done.25 = bf16[4,128,512]{2,1,0:T(8,128)(2,1)S(1)} collective-permute-done((bf16[4,128,512]{2,1,0:T(8,128)(2,1)S(1)}, bf16[4,128,512]{2,1,0:T(8,128)(2,1)S(1)}, u32[]{:S(2)}, u32[]{:S(2)}) %collective-permute-start.25) | collective-permute-done | bytes 524320 | tf_op jit(solution)/shard_map/ppermute | solution.py:46
  94.9 1.3 %fusion.1 = bf16[10,96,512]{2,1,0:T(8,128)(2,1)} fusion(f32[10,16,512]{2,1,0:T(8,128)S(1)} %slice_convert_fusion, f32[10,16,512]{2,1,0:T(8,128)S(1)} %slice_convert_fusion.1, f32[1,96,512]{2,1,0:T(8,128)S(1)} %get-tuple-element.120, f32[1,96,512]{2,1,0:T(8,128)S(1)} %get-tuple-element.119, bf16[10,96,512]{2,1,0:T(8,128)(2,1)S(1)} %copy-done.7, ...), kind=kLoop, calls=%fused_computation.3 | loop fusion | flops 3932160 | bytes 3015080 | tf_op jit(solution)/shard_map/convert_element_type | solution.py:478
  97.5 1.3 %collective-permute-done.24 = bf16[4,96,512]{2,1,0:T(8,128)(2,1)S(1)} collective-permute-done((bf16[4,96,512]{2,1,0:T(8,128)(2,1)S(1)}, bf16[4,96,512]{2,1,0:T(8,128)(2,1)S(1)}, u32[]{:S(2)}, u32[]{:S(2)}) %collective-permute-start.24) | collective-permute-done | bytes 393248 | tf_op jit(solution)/shard_map/ppermute | solution.py:46
  99.4 1.0 %copy-done.5 = bf16[512,1024]{1,0:T(8,128)(2,1)S(1)} copy-done((bf16[512,1024]{1,0:T(8,128)(2,1)S(1)}, bf16[512,1024]{1,0:T(8,128)(2,1)}, u32[]{:S(2)}) %copy-start.5) | copy-done | bytes 1048600
  101.5 1.2 %constant_dynamic-update-slice_fusion = bf16[3,512,512]{2,1,0:T(8,128)(2,1)S(1)} fusion(bf16[3,512,512]{2,1,0:T(8,128)(2,1)S(1)} %constant_dynamic-update-slice_fusion.3, bf16[3,256,512]{2,1,0:T(8,128)(2,1)} %bitcast.36, s32[]{:T(128)S(6)} %select_n.258), kind=kLoop, calls=%fused_computation.67 | loop fusion | bytes 1572868 | tf_op jit(solution)/shard_map/dynamic_update_slice | solution.py:117
  102.7 1.1 %copy-done = bf16[3,512,512]{2,1,0:T(8,128)(2,1)} copy-done((bf16[3,512,512]{2,1,0:T(8,128)(2,1)}, bf16[3,512,512]{2,1,0:T(8,128)(2,1)S(1)}, u32[]{:S(2)}) %copy-start) | copy-done | bytes 1572888
  (123 shorter events, 12.0 us)
Async XLA Ops:
  1.6 7.4 %collective-permute-start = (bf16[96,512]{1,0:T(8,128)(2,1)S(1)}, bf16[96,512]{1,0:T(8,128)(2,1)S(1)}, u32[]{:S(2)}, u32[]{:S(2)}) collective-permute-start(bf16[96,512]{1,0:T(8,128)(2,1)S(1)} %get-tuple-element.114), channel_id=1, source_target_pairs={{0,2},{1,3},{2,0},{3,1},{4,8},{5,9},{6,10},{7,11},{8,4},{9,5},{10,... | collective-permute-start | bytes 294920 | tf_op jit(solution)/shard_map/ppermute | solution.py:350
  4.6 5.0 %collective-permute-start.1 = (bf16[96,512]{1,0:T(8,128)(2,1)S(1)}, bf16[96,512]{1,0:T(8,128)(2,1)S(1)}, u32[]{:S(2)}, u32[]{:S(2)}) collective-permute-start(bf16[96,512]{1,0:T(8,128)(2,1)S(1)} %get-tuple-element.113), channel_id=1, source_target_pairs={{0,4},{1,5},{2,6},{3,7},{4,0},{5,1},{6,2},{7,3},{8,12},{9,13},{10,... | collective-permute-start | bytes 294920 | tf_op jit(solution)/shard_map/ppermute | solution.py:349
  7.2 7.7 %collective-permute-start.2 = (bf16[10,16,512]{2,1,0:T(8,128)(2,1)S(1)}, bf16[10,16,512]{2,1,0:T(8,128)(2,1)S(1)}, u32[]{:S(2)}, u32[]{:S(2)}) collective-permute-start(bf16[10,16,512]{2,1,0:T(8,128)(2,1)S(1)} %get-tuple-element.112), channel_id=1, source_target_pairs={{0,1},{1,2},{2,3},{3,0},{4,5},{5,6},{6,7},{7,4},{8,9},{9,10},{10,1... | collective-permute-start | bytes 491528 | tf_op jit(solution)/shard_map/ppermute | solution.py:351
  7.2 7.6 %collective-permute-start.3 = (bf16[10,16,512]{2,1,0:T(8,128)(2,1)S(1)}, bf16[10,16,512]{2,1,0:T(8,128)(2,1)S(1)}, u32[]{:S(2)}, u32[]{:S(2)}) collective-permute-start(bf16[10,16,512]{2,1,0:T(8,128)(2,1)S(1)} %get-tuple-element.111), channel_id=1, source_target_pairs={{1,0},{2,1},{3,2},{0,3},{5,4},{6,5},{7,6},{4,7},{9,8},{10,9},{11,1... | collective-permute-start | bytes 491528 | tf_op jit(solution)/shard_map/ppermute | solution.py:352
  9.7 5.1 %collective-permute-start.5 = (bf16[2,16,512]{2,1,0:T(8,128)(2,1)S(1)}, bf16[2,16,512]{2,1,0:T(8,128)(2,1)S(1)}, u32[]{:S(2)}, u32[]{:S(2)}) collective-permute-start(bf16[2,16,512]{2,1,0:T(8,128)(2,1)S(1)} %pad_maximum_fusion.7), channel_id=1, source_target_pairs={{1,0},{2,1},{3,2},{0,3},{5,4},{6,5},{7,6},{4,7},{9,8},{10,9},{11,1... | collective-permute-start | bytes 98312 | tf_op jit(solution)/shard_map/ppermute | solution.py:358
  10.9 3.9 %collective-permute-start.4 = (bf16[2,16,512]{2,1,0:T(8,128)(2,1)S(1)}, bf16[2,16,512]{2,1,0:T(8,128)(2,1)S(1)}, u32[]{:S(2)}, u32[]{:S(2)}) collective-permute-start(bf16[2,16,512]{2,1,0:T(8,128)(2,1)S(1)} %pad_maximum_fusion.6), channel_id=1, source_target_pairs={{0,1},{1,2},{2,3},{3,0},{4,5},{5,6},{6,7},{7,4},{8,9},{9,10},{10,1... | collective-permute-start | bytes 98312 | tf_op jit(solution)/shard_map/ppermute | solution.py:356
  30.7 3.1 %collective-permute-start.8 = (bf16[2,2,2,128,512]{4,3,2,1,0:T(8,128)(2,1)}, bf16[2,2,2,128,512]{4,3,2,1,0:T(8,128)(2,1)S(1)}, u32[]{:S(2)}, u32[]{:S(2)}) collective-permute-start(bf16[2,2,2,128,512]{4,3,2,1,0:T(8,128)(2,1)} %bitcast.76), channel_id=1, source_target_pairs={{0,1},{1,0},{2,3},{3,2},{4,5},{5,4},{6,7},{7,6},{8,9},{9,8},{10,11... | collective-permute-start | bytes 3145736 | tf_op jit(solution)/shard_map/ppermute | solution.py:46
  31.3 5.9 %collective-permute-start.6 = (bf16[2,2,2,96,512]{4,3,2,1,0:T(8,128)(2,1)}, bf16[2,2,2,96,512]{4,3,2,1,0:T(8,128)(2,1)S(1)}, u32[]{:S(2)}, u32[]{:S(2)}) collective-permute-start(bf16[2,2,2,96,512]{4,3,2,1,0:T(8,128)(2,1)} %bitcast.77), channel_id=1, source_target_pairs={{0,1},{1,0},{2,3},{3,2},{4,5},{5,4},{6,7},{7,6},{8,9},{9,8},{10,11... | collective-permute-start | bytes 2359304 | tf_op jit(solution)/shard_map/ppermute | solution.py:46
  35.7 11.0 %collective-permute-start.9 = (bf16[2,2,128,512]{3,2,1,0:T(8,128)(2,1)S(1)}, bf16[2,2,128,512]{3,2,1,0:T(8,128)(2,1)S(1)}, u32[]{:S(2)}, u32[]{:S(2)}) collective-permute-start(bf16[2,2,128,512]{3,2,1,0:T(8,128)(2,1)S(1)} %fusion.2), channel_id=1, source_target_pairs={{0,2},{1,5},{2,0},{3,7},{4,6},{5,1},{6,4},{7,3},{8,10},{9,13},{10,... | collective-permute-start | bytes 1572872 | tf_op jit(solution)/shard_map/ppermute | solution.py:46
  37.6 11.9 %collective-permute-start.7 = (bf16[2,2,96,512]{3,2,1,0:T(8,128)(2,1)S(1)}, bf16[2,2,96,512]{3,2,1,0:T(8,128)(2,1)S(1)}, u32[]{:S(2)}, u32[]{:S(2)}) collective-permute-start(bf16[2,2,96,512]{3,2,1,0:T(8,128)(2,1)S(1)} %fusion.3), channel_id=1, source_target_pairs={{0,2},{1,5},{2,0},{3,7},{4,6},{5,1},{6,4},{7,3},{8,10},{9,13},{10,... | collective-permute-start | bytes 1179656 | tf_op jit(solution)/shard_map/ppermute | solution.py:46
  46.9 6.9 %collective-permute-start.11 = (bf16[2,128,512]{2,1,0:T(8,128)(2,1)S(1)}, bf16[2,128,512]{2,1,0:T(8,128)(2,1)S(1)}, u32[]{:S(2)}, u32[]{:S(2)}) collective-permute-start(bf16[2,128,512]{2,1,0:T(8,128)(2,1)S(1)} %fusion.4), channel_id=1, source_target_pairs={{0,4},{1,3},{2,6},{3,1},{4,0},{5,7},{6,2},{7,5},{8,12},{9,11},{10,... | collective-permute-start | bytes 786440 | tf_op jit(solution)/shard_map/ppermute | solution.py:46
  49.6 9.4 %copy-start.13 = (bf16[12,16,512]{2,1,0:T(8,128)(2,1)S(1)}, bf16[12,16,512]{2,1,0:T(8,128)(2,1)}, u32[]{:S(2)}) copy-start(bf16[12,16,512]{2,1,0:T(8,128)(2,1)} %get-tuple-element.86) | copy-start | bytes 589828
  49.6 9.3 %copy-start.12 = (bf16[12,16,512]{2,1,0:T(8,128)(2,1)S(1)}, bf16[12,16,512]{2,1,0:T(8,128)(2,1)}, u32[]{:S(2)}) copy-start(bf16[12,16,512]{2,1,0:T(8,128)(2,1)} %get-tuple-element.87) | copy-start | bytes 589828
  49.7 16.6 %copy-start.9 = (f32[2,96,512]{2,1,0:T(8,128)S(1)}, f32[2,96,512]{2,1,0:T(8,128)}, u32[]{:S(2)}) copy-start(f32[2,96,512]{2,1,0:T(8,128)} %get-tuple-element.84) | copy-start | bytes 1179652
  49.7 7.5 %collective-permute-start.10 = (bf16[2,96,512]{2,1,0:T(8,128)(2,1)S(1)}, bf16[2,96,512]{2,1,0:T(8,128)(2,1)S(1)}, u32[]{:S(2)}, u32[]{:S(2)}) collective-permute-start(bf16[2,96,512]{2,1,0:T(8,128)(2,1)S(1)} %fusion.6), channel_id=1, source_target_pairs={{0,8},{1,9},{2,10},{3,11},{4,12},{5,13},{6,14},{7,15},{8,0},{9,1},... | collective-permute-start | bytes 589832 | tf_op jit(solution)/shard_map/ppermute | solution.py:46
  53.9 5.5 %collective-permute-start.13 = (bf16[128,512]{1,0:T(8,128)(2,1)S(1)}, bf16[128,512]{1,0:T(8,128)(2,1)S(1)}, u32[]{:S(2)}, u32[]{:S(2)}) collective-permute-start(bf16[128,512]{1,0:T(8,128)(2,1)S(1)} %fusion.8), channel_id=1, source_target_pairs={{0,8},{1,9},{2,10},{3,11},{4,12},{5,13},{6,14},{7,15},{8,0},{9,1},... | collective-permute-start | bytes 393224 | tf_op jit(solution)/shard_map/ppermute | solution.py:46
  57.2 5.0 %collective-permute-start.12 = (bf16[96,512]{1,0:T(8,128)(2,1)S(1)}, bf16[96,512]{1,0:T(8,128)(2,1)S(1)}, u32[]{:S(2)}, u32[]{:S(2)}) collective-permute-start(bf16[96,512]{1,0:T(8,128)(2,1)S(1)} %fusion.10), channel_id=1, source_target_pairs={{0,4},{1,3},{2,6},{3,1},{4,0},{5,7},{6,2},{7,5},{8,12},{9,11},{10,... | collective-permute-start | bytes 294920 | tf_op jit(solution)/shard_map/ppermute | solution.py:46
  58.9 5.8 %collective-permute-start.16 = (bf16[12,16,512]{2,1,0:T(8,128)(2,1)S(1)}, bf16[12,16,512]{2,1,0:T(8,128)(2,1)S(1)}, u32[]{:S(2)}, u32[]{:S(2)}) collective-permute-start(bf16[12,16,512]{2,1,0:T(8,128)(2,1)S(1)} %copy-done.13), channel_id=1, source_target_pairs={{1,0},{2,1},{3,2},{0,3},{5,4},{6,5},{7,6},{4,7},{9,8},{10,9},{11,1... | collective-permute-start | bytes 589832 | tf_op jit(solution)/shard_map/ppermute | solution.py:497
  59.0 7.2 %collective-permute-start.17 = (bf16[12,16,512]{2,1,0:T(8,128)(2,1)S(1)}, bf16[12,16,512]{2,1,0:T(8,128)(2,1)S(1)}, u32[]{:S(2)}, u32[]{:S(2)}) collective-permute-start(bf16[12,16,512]{2,1,0:T(8,128)(2,1)S(1)} %copy-done.12), channel_id=1, source_target_pairs={{0,1},{1,2},{2,3},{3,0},{4,5},{5,6},{6,7},{7,4},{8,9},{9,10},{10,1... | collective-permute-start | bytes 589832 | tf_op jit(solution)/shard_map/ppermute | solution.py:498
  59.5 12.1 %collective-permute-start.15 = (bf16[128,512]{1,0:T(8,128)(2,1)S(1)}, bf16[128,512]{1,0:T(8,128)(2,1)S(1)}, u32[]{:S(2)}, u32[]{:S(2)}) collective-permute-start(bf16[128,512]{1,0:T(8,128)(2,1)S(1)} %fusion.5), channel_id=1, source_target_pairs={{0,16},{1,17},{2,18},{3,19},{4,20},{5,21},{6,22},{7,23},{8,24},{9,... | collective-permute-start | bytes 393224 | tf_op jit(solution)/shard_map/ppermute | solution.py:46
  62.3 11.5 %collective-permute-start.14 = (bf16[96,512]{1,0:T(8,128)(2,1)S(1)}, bf16[96,512]{1,0:T(8,128)(2,1)S(1)}, u32[]{:S(2)}, u32[]{:S(2)}) collective-permute-start(bf16[96,512]{1,0:T(8,128)(2,1)S(1)} %fusion.7), channel_id=1, source_target_pairs={{0,16},{1,17},{2,18},{3,19},{4,20},{5,21},{6,22},{7,23},{8,24},{9,... | collective-permute-start | bytes 294920 | tf_op jit(solution)/shard_map/ppermute | solution.py:46
  66.4 12.6 %collective-permute-start.22 = (bf16[96,512]{1,0:T(8,128)(2,1)S(1)}, bf16[96,512]{1,0:T(8,128)(2,1)S(1)}, u32[]{:S(2)}, u32[]{:S(2)}) collective-permute-start(bf16[96,512]{1,0:T(8,128)(2,1)S(1)} %get-tuple-element.130), channel_id=1, source_target_pairs={{0,4},{1,5},{2,6},{3,7},{4,0},{5,1},{6,2},{7,3},{8,12},{9,13},{10,... | collective-permute-start | bytes 294920 | tf_op jit(solution)/shard_map/ppermute | solution.py:460
  66.8 12.1 %collective-permute-start.23 = (bf16[96,512]{1,0:T(8,128)(2,1)S(1)}, bf16[96,512]{1,0:T(8,128)(2,1)S(1)}, u32[]{:S(2)}, u32[]{:S(2)}) collective-permute-start(bf16[96,512]{1,0:T(8,128)(2,1)S(1)} %get-tuple-element.129), channel_id=1, source_target_pairs={{0,2},{1,3},{2,0},{3,1},{4,8},{5,9},{6,10},{7,11},{8,4},{9,5},{10,... | collective-permute-start | bytes 294920 | tf_op jit(solution)/shard_map/ppermute | solution.py:461
  71.7 7.1 %collective-permute-start.19 = (bf16[1,128,512]{2,1,0:T(8,128)(2,1)S(1)}, bf16[1,128,512]{2,1,0:T(8,128)(2,1)S(1)}, u32[]{:S(2)}, u32[]{:S(2)}) collective-permute-start(bf16[1,128,512]{2,1,0:T(8,128)(2,1)S(1)} %fusion.9), channel_id=1, source_target_pairs={{0,8},{1,9},{2,10},{3,11},{4,12},{5,13},{6,14},{7,15},{8,0},{9,1},... | collective-permute-start | bytes 393224 | tf_op jit(solution)/shard_map/ppermute | solution.py:46
  73.8 5.2 %collective-permute-start.18 = (bf16[1,96,512]{2,1,0:T(8,128)(2,1)S(1)}, bf16[1,96,512]{2,1,0:T(8,128)(2,1)S(1)}, u32[]{:S(2)}, u32[]{:S(2)}) collective-permute-start(bf16[1,96,512]{2,1,0:T(8,128)(2,1)S(1)} %fusion.11), channel_id=1, source_target_pairs={{0,4},{1,3},{2,6},{3,1},{4,0},{5,7},{6,2},{7,5},{8,12},{9,11},{10,... | collective-permute-start | bytes 294920 | tf_op jit(solution)/shard_map/ppermute | solution.py:46
  78.8 6.4 %collective-permute-start.21 = (bf16[2,128,512]{2,1,0:T(8,128)(2,1)S(1)}, bf16[2,128,512]{2,1,0:T(8,128)(2,1)S(1)}, u32[]{:S(2)}, u32[]{:S(2)}) collective-permute-start(bf16[2,128,512]{2,1,0:T(8,128)(2,1)S(1)} %pad_maximum_fusion.4), channel_id=1, source_target_pairs={{0,4},{1,3},{2,6},{3,1},{4,0},{5,7},{6,2},{7,5},{8,12},{9,11},{10,... | collective-permute-start | bytes 786440 | tf_op jit(solution)/shard_map/ppermute | solution.py:46
  79.0 6.9 %collective-permute-start.20 = (bf16[2,96,512]{2,1,0:T(8,128)(2,1)S(1)}, bf16[2,96,512]{2,1,0:T(8,128)(2,1)S(1)}, u32[]{:S(2)}, u32[]{:S(2)}) collective-permute-start(bf16[2,96,512]{2,1,0:T(8,128)(2,1)S(1)} %pad_maximum_fusion.5), channel_id=1, source_target_pairs={{0,8},{1,9},{2,10},{3,11},{4,12},{5,13},{6,14},{7,15},{8,0},{9,1},... | collective-permute-start | bytes 589832 | tf_op jit(solution)/shard_map/ppermute | solution.py:46
  85.4 9.2 %collective-permute-start.25 = (bf16[4,128,512]{2,1,0:T(8,128)(2,1)S(1)}, bf16[4,128,512]{2,1,0:T(8,128)(2,1)S(1)}, u32[]{:S(2)}, u32[]{:S(2)}) collective-permute-start(bf16[4,128,512]{2,1,0:T(8,128)(2,1)S(1)} %pad_maximum_fusion.2), channel_id=1, source_target_pairs={{0,2},{1,5},{2,0},{3,7},{4,6},{5,1},{6,4},{7,3},{8,10},{9,13},{10,... | collective-permute-start | bytes 1572872 | tf_op jit(solution)/shard_map/ppermute | solution.py:46
  86.0 8.9 %copy-start.7 = (bf16[10,96,512]{2,1,0:T(8,128)(2,1)S(1)}, bf16[10,96,512]{2,1,0:T(8,128)(2,1)}, u32[]{:S(2)}) copy-start(bf16[10,96,512]{2,1,0:T(8,128)(2,1)} %get-tuple-element.96) | copy-start | bytes 2949124
  86.0 12.8 %collective-permute-start.24 = (bf16[4,96,512]{2,1,0:T(8,128)(2,1)S(1)}, bf16[4,96,512]{2,1,0:T(8,128)(2,1)S(1)}, u32[]{:S(2)}, u32[]{:S(2)}) collective-permute-start(bf16[4,96,512]{2,1,0:T(8,128)(2,1)S(1)} %pad_maximum_fusion.3), channel_id=1, source_target_pairs={{0,2},{1,5},{2,0},{3,7},{4,6},{5,1},{6,4},{7,3},{8,10},{9,13},{10,... | collective-permute-start | bytes 1179656 | tf_op jit(solution)/shard_map/ppermute | solution.py:46
  94.8 4.5 %collective-permute-start.26 = (bf16[8,128,512]{2,1,0:T(8,128)(2,1)S(1)}, bf16[8,128,512]{2,1,0:T(8,128)(2,1)S(1)}, u32[]{:S(2)}, u32[]{:S(2)}) collective-permute-start(bf16[8,128,512]{2,1,0:T(8,128)(2,1)S(1)} %pad_maximum_fusion), channel_id=1, source_target_pairs={{0,1},{1,0},{2,3},{3,2},{4,5},{5,4},{6,7},{7,6},{8,9},{9,8},{10,11... | collective-permute-start | bytes 3145736 | tf_op jit(solution)/shard_map/ppermute | solution.py:46
  99.0 2.5 %collective-permute-start.27 = (bf16[8,96,512]{2,1,0:T(8,128)(2,1)S(1)}, bf16[8,96,512]{2,1,0:T(8,128)(2,1)}, u32[]{:S(2)}, u32[]{:S(2)}) collective-permute-start(bf16[8,96,512]{2,1,0:T(8,128)(2,1)S(1)} %pad_maximum_fusion.1), channel_id=1, source_target_pairs={{0,1},{1,0},{2,3},{3,2},{4,5},{5,4},{6,7},{7,6},{8,9},{9,8},{10,11... | collective-permute-start | bytes 2359304 | tf_op jit(solution)/shard_map/ppermute | solution.py:46
  (14 other events, 26.4 us)

commit v5 on v3

--- a/solution.py
+++ b/solution.py
@@ -156,7 +156,7 @@
     core = core_ref[0]
     rows, cols, channels = field.shape
     reach = west.shape[1]
-    basis = mix.shape[0]
+    basis = mix_in.shape[0]
     points = rows * cols
     half_units, half_channels = up.shape[1] // 2, channels // 2
     body, inner = pl.ds(1, rows), pl.ds(reach, cols)
@@ -177,7 +177,10 @@
         sems,
     )
     late = 10
-    weights = started([(mix_in, mix), (up_in, up), (down_in, down), (cot_in, cot)], sems, late)
+    mix_loads = started(
+        [(mix_in.at[k], mix.at[pl.ds(k * channels, channels)]) for k in range(basis)], sems, late + 13
+    )
+    weights = started([(up_in, up), (down_in, down), (cot_in, cot)], sems, late)
     finish(tap_load)
 
     count, width = taps.shape[3], lines.shape[3]
@@ -201,17 +204,15 @@
         out = dot(bands[r], window).astype(feats.dtype)
         at = pl.ds(r * cols, cols)
         for k in range(basis):
-            feats[k, at, :] = out[k * cols : (k + 1) * cols]
+            feats[at, k * channels : (k + 1) * channels] = out[k * cols : (k + 1) * cols]
         hidden[at, :] = ext[r + 1, inner, :]
-    finish(weights[:1])
+    finish(mix_loads)
 
     for i in range(3):
         at = pl.ds(i * (points // 3), points // 3)
-        total = hidden[at, :].astype(jnp.float32)
-        for k in range(basis):
-            total = total + dot(feats[k, at, :], mix[k])
+        total = hidden[at, :].astype(jnp.float32) + dot(feats[at, :], mix[...])
         hidden[at, :] = total.astype(hidden.dtype)
-    finish(weights[1:])
+    finish(weights)
     size = pre_a.shape[0]
     slots = ((pre_a, ag_a), (pre_b, ag_b))
 
@@ -254,9 +255,10 @@
     stores += started([(hg, hg_out)], sems, late + 6)
 
     def mix_sums(half, out):
-        at = pl.ds(pl.multiple_of(half * half_channels, half_channels), half_channels)
         for k in range(basis):
-            out[k] = dot(feats[k, :, at], hg[...], OVER_ROWS).astype(out.dtype)
+            start = k * channels + half * half_channels
+            at = pl.ds(pl.multiple_of(start, half_channels), half_channels)
+            out[k] = dot(feats[:, at], hg[...], OVER_ROWS).astype(out.dtype)
 
     mix_sums(1 - core, mix_send)
     stores += started([(mix_send, mix_send_out)], sems, late + 7)
@@ -280,12 +282,12 @@
     loads = started([(hg_in, hg)], sems)
     loads += started([(mix_in.at[k], mix.at[k]) for k in range(basis)], sems, 1)
     late = 1 + basis
-    band_loads = started([(bands_in.at[r], bands.at[r]) for r in range(rows)], sems, late)
     pulled[...] = jnp.zeros(pulled.shape, pulled.dtype)
     group = 5 if rows % 5 == 0 else 1
-    finish(loads[:1])
+    finish(loads[:2])
+    band_loads = started([(bands_in.at[r], bands.at[r]) for r in range(rows)], sems, late)
     for k in range(basis):
-        finish(loads[1 + k : 2 + k])
+        finish(loads[1 + k : 2 + k] if k else [])
         for r in range(0, rows, group):
             part = dot(hg[r * cols : (r + group) * cols, :], mix[k], OVER_LANES)
             grads[r : r + group, k * cols : (k + 1) * cols] = part.astype(grads.dtype).reshape(
@@ -357,7 +359,7 @@
     half_units, half_channels = hidden_units // 2, channels // 2
     mlp_half = (half_units + channels, channels)
     mix_half = (basis_count, half_channels, channels)
-    big, wide, many = (points, channels), (points, hidden_units), (basis_count, points, channels)
+    big, wide = (points, channels), (points, hidden_units)
     core = place.flat % 2
     core_op = core[None].astype(jnp.int32)
     sized = (points // 5, hidden_units)
@@ -375,11 +377,11 @@
             pltpu.VMEM(kernel_taps.shape, low),
             pltpu.VMEM((lat_rows, basis_count, 3, width), full),
             pltpu.VMEM(band_shape, low),
-            pltpu.VMEM(mix_weight.shape, low),
+            pltpu.VMEM((basis_count * channels, channels), low),
             pltpu.VMEM(up_weight.shape, low),
             pltpu.VMEM(down_weight.shape, low),
             pltpu.VMEM(big, low),
-            pltpu.VMEM(many, low),
+            pltpu.VMEM((points, basis_count * channels), low),
             pltpu.VMEM(big, low),
             pltpu.VMEM(wide, low),
             pltpu.VMEM(wide, low),
@@ -394,7 +396,7 @@
             pltpu.VMEM(mlp_half, low),
             pltpu.VMEM(mix_half, low),
             pltpu.VMEM(mix_half, low),
-            pltpu.SemaphoreType.DMA((23,)),
+            pltpu.SemaphoreType.DMA((23 + basis_count,)),
         ],
         band_gemm + 2 * mix_gemm + 6 * gemm,
         7 * points * hidden_units * 2,

time: 102 us -> 102 us (level)
  no operation moved by 1% of the time
where the time goes in v5:
time: 102 us
  starting transfers between devices  35.3 us (35%)
  waiting for transfers between devices  28.1 us (28%)
  Pallas kernels  24.5 us (24%)
  local copies, waits for them, and re-layouts  7.45 us (7%)
  other arithmetic  5.37 us (5%)
  between operations  1.26 us (1%)
    ppermute x18, starting transfers between devices, send_along(): return lax.ppermute(block, AXES, route(place, mask_of))  24.5 us
    pallas_call x2, Pallas kernels, call(): pl.pallas_call(kernel, out_shape=[jax.ShapeDtypeStruct(shape, kind) for s...  24.5 us
    ppermute x18, waiting for transfers between devices, send_along(): return lax.ppermute(block, AXES, route(place, mask_of))  23.8 us
    unnamed x32, local copies, waits for them, and re-layouts  4.13 us
    ppermute x1, starting transfers between devices, local(): lax.ppermute(jnp.where(place.even, top, bottom), AXES, place.bridges)  3.03 us
    ppermute x1, waiting for transfers between devices, local(): corners_east = lax.ppermute(corners, 'lon', place.west)  2.54 us
  transfers between devices with their start and end apart: 28, of which 15 were waited for; matrix products, arithmetic and copies ran while one was open for 6% of the time, Pallas kernels for 9%

profile of v5, /device:TPU:0, one launch (start us, length us, event | category | flops | bytes accessed | tf_op | source)
XLA Modules:
  0.0 101.9 jit_solution(3993786917029543134)
XLA Ops:
  1.6 3.0 %collective-permute-start = (bf16[96,512]{1,0:T(8,128)(2,1)S(1)}, bf16[96,512]{1,0:T(8,128)(2,1)S(1)}, u32[]{:S(2)}, u32[]{:S(2)}) collective-permute-start(bf16[96,512]{1,0:T(8,128)(2,1)S(1)} %get-tuple-element.110), channel_id=1, source_target_pairs={{0,2},{1,3},{2,0},{3,1},{4,8},{5,9},{6,10},{7,11},{8,4},{9,5},{10,... | collective-permute-start | bytes 294920 | tf_op jit(solution)/shard_map/ppermute | solution.py:340
  4.6 1.5 %collective-permute-start.1 = (bf16[96,512]{1,0:T(8,128)(2,1)S(1)}, bf16[96,512]{1,0:T(8,128)(2,1)S(1)}, u32[]{:S(2)}, u32[]{:S(2)}) collective-permute-start(bf16[96,512]{1,0:T(8,128)(2,1)S(1)} %get-tuple-element.109), channel_id=1, source_target_pairs={{0,4},{1,5},{2,6},{3,7},{4,0},{5,1},{6,2},{7,3},{8,12},{9,13},{10,... | collective-permute-start | bytes 294920 | tf_op jit(solution)/shard_map/ppermute | solution.py:339
  7.2 1.7 %collective-permute-start.3 = (bf16[10,16,512]{2,1,0:T(8,128)(2,1)S(1)}, bf16[10,16,512]{2,1,0:T(8,128)(2,1)S(1)}, u32[]{:S(2)}, u32[]{:S(2)}) collective-permute-start(bf16[10,16,512]{2,1,0:T(8,128)(2,1)S(1)} %get-tuple-element.107), channel_id=1, source_target_pairs={{1,0},{2,1},{3,2},{0,3},{5,4},{6,5},{7,6},{4,7},{9,8},{10,9},{11,1... | collective-permute-start | bytes 491528 | tf_op jit(solution)/shard_map/ppermute | solution.py:342
  9.7 1.2 %collective-permute-start.5 = (bf16[2,16,512]{2,1,0:T(8,128)(2,1)S(1)}, bf16[2,16,512]{2,1,0:T(8,128)(2,1)S(1)}, u32[]{:S(2)}, u32[]{:S(2)}) collective-permute-start(bf16[2,16,512]{2,1,0:T(8,128)(2,1)S(1)} %pad_maximum_fusion.7), channel_id=1, source_target_pairs={{1,0},{2,1},{3,2},{0,3},{5,4},{6,5},{7,6},{4,7},{9,8},{10,9},{11,1... | collective-permute-start | bytes 98312 | tf_op jit(solution)/shard_map/ppermute | solution.py:348
  10.9 2.5 %collective-permute-done.5.corners_east = bf16[2,16,512]{2,1,0:T(8,128)(2,1)S(1)} collective-permute-done((bf16[2,16,512]{2,1,0:T(8,128)(2,1)S(1)}, bf16[2,16,512]{2,1,0:T(8,128)(2,1)S(1)}, u32[]{:S(2)}, u32[]{:S(2)}) %collective-permute-start.5) | collective-permute-done | bytes 32800 | tf_op jit(solution)/shard_map/ppermute | solution.py:348
  15.2 15.8 %shard_map.110 = (bf16[960,512]{1,0:T(8,128)(2,1)}, bf16[960,512]{1,0:T(8,128)(2,1)}, bf16[10,288,384]{2,1,0:T(8,128)(2,1)}, bf16[1024,512]{1,0:T(8,128)(2,1)}, ...) custom-call(s32[1]{0:T(128)} %bitcast.core_ref, s32[10]{0:T(128)} %reach_ref.1, ...), custom_call_target="tpu_custom_call" | custom-call | flops 10192158720 | bytes 13762560 | tf_op jit(solution)/shard_map/pallas_call | solution.py:319
  31.7 2.2 %collective-permute-done.8 = bf16[2,2,2,128,512]{4,3,2,1,0:T(8,128)(2,1)S(1)} collective-permute-done((bf16[2,2,2,128,512]{4,3,2,1,0:T(8,128)(2,1)}, bf16[2,2,2,128,512]{4,3,2,1,0:T(8,128)(2,1)S(1)}, u32[]{:S(2)}, u32[]{:S(2)}) %collective-permute-start.8) | collective-permute-done | bytes 1048608 | tf_op jit(solution)/shard_map/ppermute | solution.py:46
  33.9 1.6 %convert_add_fusion = f32[2,2,2,128,512]{4,3,2,1,0:T(8,128)S(1)} fusion(bf16[2,2,2,128,512]{4,3,2,1,0:T(8,128)(2,1)} %bitcast.72, bf16[2,2,2,128,512]{4,3,2,1,0:T(8,128)(2,1)S(1)} %collective-permute-done.8), kind=kLoop, calls=%fused_computation | loop fusion | flops 1572864 | bytes 4194304 | tf_op jit(solution)/shard_map/add | solution.py:84
  36.9 1.2 %collective-permute-start.7 = (bf16[2,2,96,512]{3,2,1,0:T(8,128)(2,1)S(1)}, bf16[2,2,96,512]{3,2,1,0:T(8,128)(2,1)S(1)}, u32[]{:S(2)}, u32[]{:S(2)}) collective-permute-start(bf16[2,2,96,512]{3,2,1,0:T(8,128)(2,1)S(1)} %fusion.3), channel_id=1, source_target_pairs={{0,2},{1,5},{2,0},{3,7},{4,6},{5,1},{6,4},{7,3},{8,10},{9,13},{10,... | collective-permute-start | bytes 1179656 | tf_op jit(solution)/shard_map/ppermute | solution.py:46
  38.0 8.7 %shard_map.111 = (bf16[10,96,512]{2,1,0:T(8,128)(2,1)}, f32[2,96,512]{2,1,0:T(8,128)}, bf16[12,16,512]{2,1,0:T(8,128)(2,1)}, bf16[12,16,512]{2,1,0:T(8,128)(2,1)}) custom-call(bf16[960,512]{1,0:T(8,128)(2,1)} %get-tuple-element.72.hg_in, bf16[3,512,512]{2,1,0:T(8,128)(2,1)} %mix_in.3, bf16[10,288,384]{2,1,0:T(8,128)(2,1)} %get-tuple-element.73.bands_in), custom_call_target="tpu_custom_call" | custom-call | flops 2642411520 | bytes 11796480 | tf_op jit(solution)/shard_map/pallas_call | solution.py:319
  47.6 2.3 %collective-permute-start.11 = (bf16[2,128,512]{2,1,0:T(8,128)(2,1)S(1)}, bf16[2,128,512]{2,1,0:T(8,128)(2,1)S(1)}, u32[]{:S(2)}, u32[]{:S(2)}) collective-permute-start(bf16[2,128,512]{2,1,0:T(8,128)(2,1)S(1)} %fusion.4), channel_id=1, source_target_pairs={{0,4},{1,3},{2,6},{3,1},{4,0},{5,7},{6,2},{7,5},{8,12},{9,11},{10,... | collective-permute-start | bytes 786440 | tf_op jit(solution)/shard_map/ppermute | solution.py:46
  50.1 1.7 %collective-permute-start.10 = (bf16[2,96,512]{2,1,0:T(8,128)(2,1)S(1)}, bf16[2,96,512]{2,1,0:T(8,128)(2,1)S(1)}, u32[]{:S(2)}, u32[]{:S(2)}) collective-permute-start(bf16[2,96,512]{2,1,0:T(8,128)(2,1)S(1)} %fusion.6), channel_id=1, source_target_pairs={{0,8},{1,9},{2,10},{3,11},{4,12},{5,13},{6,14},{7,15},{8,0},{9,1},... | collective-permute-start | bytes 589832 | tf_op jit(solution)/shard_map/ppermute | solution.py:46
  51.7 2.5 %collective-permute-done.11 = bf16[2,128,512]{2,1,0:T(8,128)(2,1)S(1)} collective-permute-done((bf16[2,128,512]{2,1,0:T(8,128)(2,1)S(1)}, bf16[2,128,512]{2,1,0:T(8,128)(2,1)S(1)}, u32[]{:S(2)}, u32[]{:S(2)}) %collective-permute-start.11) | collective-permute-done | bytes 262176 | tf_op jit(solution)/shard_map/ppermute | solution.py:46
  54.4 2.2 %collective-permute-start.13 = (bf16[128,512]{1,0:T(8,128)(2,1)S(1)}, bf16[128,512]{1,0:T(8,128)(2,1)S(1)}, u32[]{:S(2)}, u32[]{:S(2)}) collective-permute-start(bf16[128,512]{1,0:T(8,128)(2,1)S(1)} %fusion.8), channel_id=1, source_target_pairs={{0,8},{1,9},{2,10},{3,11},{4,12},{5,13},{6,14},{7,15},{8,0},{9,1},... | collective-permute-start | bytes 393224 | tf_op jit(solution)/shard_map/ppermute | solution.py:46
  56.8 1.7 %collective-permute-start.12 = (bf16[96,512]{1,0:T(8,128)(2,1)S(1)}, bf16[96,512]{1,0:T(8,128)(2,1)S(1)}, u32[]{:S(2)}, u32[]{:S(2)}) collective-permute-start(bf16[96,512]{1,0:T(8,128)(2,1)S(1)} %fusion.10), channel_id=1, source_target_pairs={{0,4},{1,3},{2,6},{3,1},{4,0},{5,7},{6,2},{7,5},{8,12},{9,11},{10,... | collective-permute-start | bytes 294920 | tf_op jit(solution)/shard_map/ppermute | solution.py:46
  59.5 3.1 %collective-permute-start.15 = (bf16[128,512]{1,0:T(8,128)(2,1)S(1)}, bf16[128,512]{1,0:T(8,128)(2,1)S(1)}, u32[]{:S(2)}, u32[]{:S(2)}) collective-permute-start(bf16[128,512]{1,0:T(8,128)(2,1)S(1)} %fusion.5), channel_id=1, source_target_pairs={{0,16},{1,17},{2,18},{3,19},{4,20},{5,21},{6,22},{7,23},{8,24},{9,... | collective-permute-start | bytes 393224 | tf_op jit(solution)/shard_map/ppermute | solution.py:46
  62.6 1.7 %collective-permute-start.14 = (bf16[96,512]{1,0:T(8,128)(2,1)S(1)}, bf16[96,512]{1,0:T(8,128)(2,1)S(1)}, u32[]{:S(2)}, u32[]{:S(2)}) collective-permute-start(bf16[96,512]{1,0:T(8,128)(2,1)S(1)} %fusion.7), channel_id=1, source_target_pairs={{0,16},{1,17},{2,18},{3,19},{4,20},{5,21},{6,22},{7,23},{8,24},{9,... | collective-permute-start | bytes 294920 | tf_op jit(solution)/shard_map/ppermute | solution.py:46
  64.5 1.6 %collective-permute-start.22 = (bf16[96,512]{1,0:T(8,128)(2,1)S(1)}, bf16[96,512]{1,0:T(8,128)(2,1)S(1)}, u32[]{:S(2)}, u32[]{:S(2)}) collective-permute-start(bf16[96,512]{1,0:T(8,128)(2,1)S(1)} %get-tuple-element.126), channel_id=1, source_target_pairs={{0,4},{1,5},{2,6},{3,7},{4,0},{5,1},{6,2},{7,3},{8,12},{9,13},{10,... | collective-permute-start | bytes 294920 | tf_op jit(solution)/shard_map/ppermute | solution.py:436
  66.1 1.1 %collective-permute-start.23 = (bf16[96,512]{1,0:T(8,128)(2,1)S(1)}, bf16[96,512]{1,0:T(8,128)(2,1)S(1)}, u32[]{:S(2)}, u32[]{:S(2)}) collective-permute-start(bf16[96,512]{1,0:T(8,128)(2,1)S(1)} %get-tuple-element.125), channel_id=1, source_target_pairs={{0,2},{1,3},{2,0},{3,1},{4,8},{5,9},{6,10},{7,11},{8,4},{9,5},{10,... | collective-permute-start | bytes 294920 | tf_op jit(solution)/shard_map/ppermute | solution.py:437
  67.2 3.7 %collective-permute-done.15 = bf16[128,512]{1,0:T(8,128)(2,1)S(1)} collective-permute-done((bf16[128,512]{1,0:T(8,128)(2,1)S(1)}, bf16[128,512]{1,0:T(8,128)(2,1)S(1)}, u32[]{:S(2)}, u32[]{:S(2)}) %collective-permute-start.15) | collective-permute-done | bytes 131104 | tf_op jit(solution)/shard_map/ppermute | solution.py:46
  71.0 2.0 %collective-permute-start.19 = (bf16[1,128,512]{2,1,0:T(8,128)(2,1)S(1)}, bf16[1,128,512]{2,1,0:T(8,128)(2,1)S(1)}, u32[]{:S(2)}, u32[]{:S(2)}) collective-permute-start(bf16[1,128,512]{2,1,0:T(8,128)(2,1)S(1)} %fusion.9), channel_id=1, source_target_pairs={{0,8},{1,9},{2,10},{3,11},{4,12},{5,13},{6,14},{7,15},{8,0},{9,1},... | collective-permute-start | bytes 393224 | tf_op jit(solution)/shard_map/ppermute | solution.py:46
  73.1 2.1 %collective-permute-start.18 = (bf16[1,96,512]{2,1,0:T(8,128)(2,1)S(1)}, bf16[1,96,512]{2,1,0:T(8,128)(2,1)S(1)}, u32[]{:S(2)}, u32[]{:S(2)}) collective-permute-start(bf16[1,96,512]{2,1,0:T(8,128)(2,1)S(1)} %fusion.11), channel_id=1, source_target_pairs={{0,4},{1,3},{2,6},{3,1},{4,0},{5,7},{6,2},{7,5},{8,12},{9,11},{10,... | collective-permute-start | bytes 294920 | tf_op jit(solution)/shard_map/ppermute | solution.py:46
  75.2 1.5 %collective-permute-done.19 = bf16[1,128,512]{2,1,0:T(8,128)(2,1)S(1)} collective-permute-done((bf16[1,128,512]{2,1,0:T(8,128)(2,1)S(1)}, bf16[1,128,512]{2,1,0:T(8,128)(2,1)S(1)}, u32[]{:S(2)}, u32[]{:S(2)}) %collective-permute-start.19) | collective-permute-done | bytes 131104 | tf_op jit(solution)/shard_map/ppermute | solution.py:46
  76.7 2.3 %collective-permute-start.21 = (bf16[2,128,512]{2,1,0:T(8,128)(2,1)S(1)}, bf16[2,128,512]{2,1,0:T(8,128)(2,1)S(1)}, u32[]{:S(2)}, u32[]{:S(2)}) collective-permute-start(bf16[2,128,512]{2,1,0:T(8,128)(2,1)S(1)} %pad_maximum_fusion.4), channel_id=1, source_target_pairs={{0,4},{1,3},{2,6},{3,1},{4,0},{5,7},{6,2},{7,5},{8,12},{9,11},{10,... | collective-permute-start | bytes 786440 | tf_op jit(solution)/shard_map/ppermute | solution.py:46
  79.8 3.6 %collective-permute-done.21 = bf16[2,128,512]{2,1,0:T(8,128)(2,1)S(1)} collective-permute-done((bf16[2,128,512]{2,1,0:T(8,128)(2,1)S(1)}, bf16[2,128,512]{2,1,0:T(8,128)(2,1)S(1)}, u32[]{:S(2)}, u32[]{:S(2)}) %collective-permute-start.21) | collective-permute-done | bytes 262176 | tf_op jit(solution)/shard_map/ppermute | solution.py:46
  84.2 1.2 %collective-permute-done.20 = bf16[2,96,512]{2,1,0:T(8,128)(2,1)S(1)} collective-permute-done((bf16[2,96,512]{2,1,0:T(8,128)(2,1)S(1)}, bf16[2,96,512]{2,1,0:T(8,128)(2,1)S(1)}, u32[]{:S(2)}, u32[]{:S(2)}) %collective-permute-start.20) | collective-permute-done | bytes 196640 | tf_op jit(solution)/shard_map/ppermute | solution.py:46
  85.5 1.2 %collective-permute-start.24 = (bf16[4,96,512]{2,1,0:T(8,128)(2,1)S(1)}, bf16[4,96,512]{2,1,0:T(8,128)(2,1)S(1)}, u32[]{:S(2)}, u32[]{:S(2)}) collective-permute-start(bf16[4,96,512]{2,1,0:T(8,128)(2,1)S(1)} %pad_maximum_fusion.3), channel_id=1, source_target_pairs={{0,2},{1,5},{2,0},{3,7},{4,6},{5,1},{6,4},{7,3},{8,10},{9,13},{10,... | collective-permute-start | bytes 1179656 | tf_op jit(solution)/shard_map/ppermute | solution.py:46
  86.7 6.0 %collective-permute-done.25 = bf16[4,128,512]{2,1,0:T(8,128)(2,1)S(1)} collective-permute-done((bf16[4,128,512]{2,1,0:T(8,128)(2,1)S(1)}, bf16[4,128,512]{2,1,0:T(8,128)(2,1)S(1)}, u32[]{:S(2)}, u32[]{:S(2)}) %collective-permute-start.25) | collective-permute-done | bytes 524320 | tf_op jit(solution)/shard_map/ppermute | solution.py:46
  93.0 1.3 %fusion.1 = bf16[10,96,512]{2,1,0:T(8,128)(2,1)} fusion(f32[10,16,512]{2,1,0:T(8,128)S(1)} %slice_convert_fusion, f32[10,16,512]{2,1,0:T(8,128)S(1)} %slice_convert_fusion.1, f32[1,96,512]{2,1,0:T(8,128)S(1)} %get-tuple-element.116, f32[1,96,512]{2,1,0:T(8,128)S(1)} %get-tuple-element.115, bf16[10,96,512]{2,1,0:T(8,128)(2,1)S(1)} %copy-done.7, ...), kind=kLoop, calls=%fused_computation.3 | loop fusion | flops 3932160 | bytes 3015080 | tf_op jit(solution)/shard_map/convert_element_type | solution.py:454
  95.6 1.3 %collective-permute-done.24 = bf16[4,96,512]{2,1,0:T(8,128)(2,1)S(1)} collective-permute-done((bf16[4,96,512]{2,1,0:T(8,128)(2,1)S(1)}, bf16[4,96,512]{2,1,0:T(8,128)(2,1)S(1)}, u32[]{:S(2)}, u32[]{:S(2)}) %collective-permute-start.24) | collective-permute-done | bytes 393248 | tf_op jit(solution)/shard_map/ppermute | solution.py:46
  99.6 1.2 %constant_dynamic-update-slice_fusion = bf16[3,512,512]{2,1,0:T(8,128)(2,1)S(1)} fusion(bf16[3,512,512]{2,1,0:T(8,128)(2,1)S(1)} %constant_dynamic-update-slice_fusion.3, bf16[3,256,512]{2,1,0:T(8,128)(2,1)} %bitcast.36, s32[]{:T(128)S(6)} %select_n.258), kind=kLoop, calls=%fused_computation.67 | loop fusion | bytes 1572868 | tf_op jit(solution)/shard_map/dynamic_update_slice | solution.py:117
  100.8 1.1 %copy-done = bf16[3,512,512]{2,1,0:T(8,128)(2,1)} copy-done((bf16[3,512,512]{2,1,0:T(8,128)(2,1)}, bf16[3,512,512]{2,1,0:T(8,128)(2,1)S(1)}, u32[]{:S(2)}) %copy-start) | copy-done | bytes 1572888
  (118 shorter events, 14.9 us)
Async XLA Ops:
  1.6 7.4 %collective-permute-start = (bf16[96,512]{1,0:T(8,128)(2,1)S(1)}, bf16[96,512]{1,0:T(8,128)(2,1)S(1)}, u32[]{:S(2)}, u32[]{:S(2)}) collective-permute-start(bf16[96,512]{1,0:T(8,128)(2,1)S(1)} %get-tuple-element.110), channel_id=1, source_target_pairs={{0,2},{1,3},{2,0},{3,1},{4,8},{5,9},{6,10},{7,11},{8,4},{9,5},{10,... | collective-permute-start | bytes 294920 | tf_op jit(solution)/shard_map/ppermute | solution.py:340
  4.6 5.0 %collective-permute-start.1 = (bf16[96,512]{1,0:T(8,128)(2,1)S(1)}, bf16[96,512]{1,0:T(8,128)(2,1)S(1)}, u32[]{:S(2)}, u32[]{:S(2)}) collective-permute-start(bf16[96,512]{1,0:T(8,128)(2,1)S(1)} %get-tuple-element.109), channel_id=1, source_target_pairs={{0,4},{1,5},{2,6},{3,7},{4,0},{5,1},{6,2},{7,3},{8,12},{9,13},{10,... | collective-permute-start | bytes 294920 | tf_op jit(solution)/shard_map/ppermute | solution.py:339
  7.2 7.3 %collective-permute-start.2 = (bf16[10,16,512]{2,1,0:T(8,128)(2,1)S(1)}, bf16[10,16,512]{2,1,0:T(8,128)(2,1)S(1)}, u32[]{:S(2)}, u32[]{:S(2)}) collective-permute-start(bf16[10,16,512]{2,1,0:T(8,128)(2,1)S(1)} %get-tuple-element.108), channel_id=1, source_target_pairs={{0,1},{1,2},{2,3},{3,0},{4,5},{5,6},{6,7},{7,4},{8,9},{9,10},{10,1... | collective-permute-start | bytes 491528 | tf_op jit(solution)/shard_map/ppermute | solution.py:341
  7.2 7.3 %collective-permute-start.3 = (bf16[10,16,512]{2,1,0:T(8,128)(2,1)S(1)}, bf16[10,16,512]{2,1,0:T(8,128)(2,1)S(1)}, u32[]{:S(2)}, u32[]{:S(2)}) collective-permute-start(bf16[10,16,512]{2,1,0:T(8,128)(2,1)S(1)} %get-tuple-element.107), channel_id=1, source_target_pairs={{1,0},{2,1},{3,2},{0,3},{5,4},{6,5},{7,6},{4,7},{9,8},{10,9},{11,1... | collective-permute-start | bytes 491528 | tf_op jit(solution)/shard_map/ppermute | solution.py:342
  9.7 4.8 %copy-start.10 = (bf16[96,512]{1,0:T(8,128)(2,1)}, bf16[96,512]{1,0:T(8,128)(2,1)S(1)}, u32[]{:S(2)}) copy-start(bf16[96,512]{1,0:T(8,128)(2,1)S(1)} %get-tuple-element.131.south) | copy-start | bytes 294916
  9.7 4.8 %copy-start.11 = (bf16[96,512]{1,0:T(8,128)(2,1)}, bf16[96,512]{1,0:T(8,128)(2,1)S(1)}, u32[]{:S(2)}) copy-start(bf16[96,512]{1,0:T(8,128)(2,1)S(1)} %get-tuple-element.132.north) | copy-start | bytes 294916
  9.7 3.7 %collective-permute-start.5 = (bf16[2,16,512]{2,1,0:T(8,128)(2,1)S(1)}, bf16[2,16,512]{2,1,0:T(8,128)(2,1)S(1)}, u32[]{:S(2)}, u32[]{:S(2)}) collective-permute-start(bf16[2,16,512]{2,1,0:T(8,128)(2,1)S(1)} %pad_maximum_fusion.7), channel_id=1, source_target_pairs={{1,0},{2,1},{3,2},{0,3},{5,4},{6,5},{7,6},{4,7},{9,8},{10,9},{11,1... | collective-permute-start | bytes 98312 | tf_op jit(solution)/shard_map/ppermute | solution.py:348
  10.9 3.6 %collective-permute-start.4 = (bf16[2,16,512]{2,1,0:T(8,128)(2,1)S(1)}, bf16[2,16,512]{2,1,0:T(8,128)(2,1)S(1)}, u32[]{:S(2)}, u32[]{:S(2)}) collective-permute-start(bf16[2,16,512]{2,1,0:T(8,128)(2,1)S(1)} %pad_maximum_fusion.6), channel_id=1, source_target_pairs={{0,1},{1,2},{2,3},{3,0},{4,5},{5,6},{6,7},{7,4},{8,9},{9,10},{10,1... | collective-permute-start | bytes 98312 | tf_op jit(solution)/shard_map/ppermute | solution.py:346
  31.0 2.9 %collective-permute-start.8 = (bf16[2,2,2,128,512]{4,3,2,1,0:T(8,128)(2,1)}, bf16[2,2,2,128,512]{4,3,2,1,0:T(8,128)(2,1)S(1)}, u32[]{:S(2)}, u32[]{:S(2)}) collective-permute-start(bf16[2,2,2,128,512]{4,3,2,1,0:T(8,128)(2,1)} %bitcast.74), channel_id=1, source_target_pairs={{0,1},{1,0},{2,3},{3,2},{4,5},{5,4},{6,7},{7,6},{8,9},{9,8},{10,11... | collective-permute-start | bytes 3145736 | tf_op jit(solution)/shard_map/ppermute | solution.py:46
  31.1 5.5 %collective-permute-start.6 = (bf16[2,2,2,96,512]{4,3,2,1,0:T(8,128)(2,1)}, bf16[2,2,2,96,512]{4,3,2,1,0:T(8,128)(2,1)S(1)}, u32[]{:S(2)}, u32[]{:S(2)}) collective-permute-start(bf16[2,2,2,96,512]{4,3,2,1,0:T(8,128)(2,1)} %bitcast.76), channel_id=1, source_target_pairs={{0,1},{1,0},{2,3},{3,2},{4,5},{5,4},{6,7},{7,6},{8,9},{9,8},{10,11... | collective-permute-start | bytes 2359304 | tf_op jit(solution)/shard_map/ppermute | solution.py:46
  35.6 11.7 %collective-permute-start.9 = (bf16[2,2,128,512]{3,2,1,0:T(8,128)(2,1)S(1)}, bf16[2,2,128,512]{3,2,1,0:T(8,128)(2,1)S(1)}, u32[]{:S(2)}, u32[]{:S(2)}) collective-permute-start(bf16[2,2,128,512]{3,2,1,0:T(8,128)(2,1)S(1)} %fusion.2), channel_id=1, source_target_pairs={{0,2},{1,5},{2,0},{3,7},{4,6},{5,1},{6,4},{7,3},{8,10},{9,13},{10,... | collective-permute-start | bytes 1572872 | tf_op jit(solution)/shard_map/ppermute | solution.py:46
  36.9 13.0 %collective-permute-start.7 = (bf16[2,2,96,512]{3,2,1,0:T(8,128)(2,1)S(1)}, bf16[2,2,96,512]{3,2,1,0:T(8,128)(2,1)S(1)}, u32[]{:S(2)}, u32[]{:S(2)}) collective-permute-start(bf16[2,2,96,512]{3,2,1,0:T(8,128)(2,1)S(1)} %fusion.3), channel_id=1, source_target_pairs={{0,2},{1,5},{2,0},{3,7},{4,6},{5,1},{6,4},{7,3},{8,10},{9,13},{10,... | collective-permute-start | bytes 1179656 | tf_op jit(solution)/shard_map/ppermute | solution.py:46
  46.8 17.6 %collective-permute-start.16 = (bf16[12,16,512]{2,1,0:T(8,128)(2,1)}, bf16[12,16,512]{2,1,0:T(8,128)(2,1)S(1)}, u32[]{:S(2)}, u32[]{:S(2)}) collective-permute-start(bf16[12,16,512]{2,1,0:T(8,128)(2,1)} %get-tuple-element.74), channel_id=1, source_target_pairs={{1,0},{2,1},{3,2},{0,3},{5,4},{6,5},{7,6},{4,7},{9,8},{10,9},{11,1... | collective-permute-start | bytes 589832 | tf_op jit(solution)/shard_map/ppermute | solution.py:466
  47.3 17.0 %collective-permute-start.17 = (bf16[12,16,512]{2,1,0:T(8,128)(2,1)}, bf16[12,16,512]{2,1,0:T(8,128)(2,1)S(1)}, u32[]{:S(2)}, u32[]{:S(2)}) collective-permute-start(bf16[12,16,512]{2,1,0:T(8,128)(2,1)} %get-tuple-element.83), channel_id=1, source_target_pairs={{0,1},{1,2},{2,3},{3,0},{4,5},{5,6},{6,7},{7,4},{8,9},{9,10},{10,1... | collective-permute-start | bytes 589832 | tf_op jit(solution)/shard_map/ppermute | solution.py:467
  47.6 6.7 %collective-permute-start.11 = (bf16[2,128,512]{2,1,0:T(8,128)(2,1)S(1)}, bf16[2,128,512]{2,1,0:T(8,128)(2,1)S(1)}, u32[]{:S(2)}, u32[]{:S(2)}) collective-permute-start(bf16[2,128,512]{2,1,0:T(8,128)(2,1)S(1)} %fusion.4), channel_id=1, source_target_pairs={{0,4},{1,3},{2,6},{3,1},{4,0},{5,7},{6,2},{7,5},{8,12},{9,11},{10,... | collective-permute-start | bytes 786440 | tf_op jit(solution)/shard_map/ppermute | solution.py:46
  50.1 14.3 %copy-start.9 = (f32[2,96,512]{2,1,0:T(8,128)S(1)}, f32[2,96,512]{2,1,0:T(8,128)}, u32[]{:S(2)}) copy-start(f32[2,96,512]{2,1,0:T(8,128)} %get-tuple-element.82) | copy-start | bytes 1179652
  50.1 6.6 %collective-permute-start.10 = (bf16[2,96,512]{2,1,0:T(8,128)(2,1)S(1)}, bf16[2,96,512]{2,1,0:T(8,128)(2,1)S(1)}, u32[]{:S(2)}, u32[]{:S(2)}) collective-permute-start(bf16[2,96,512]{2,1,0:T(8,128)(2,1)S(1)} %fusion.6), channel_id=1, source_target_pairs={{0,8},{1,9},{2,10},{3,11},{4,12},{5,13},{6,14},{7,15},{8,0},{9,1},... | collective-permute-start | bytes 589832 | tf_op jit(solution)/shard_map/ppermute | solution.py:46
  54.4 5.1 %collective-permute-start.13 = (bf16[128,512]{1,0:T(8,128)(2,1)S(1)}, bf16[128,512]{1,0:T(8,128)(2,1)S(1)}, u32[]{:S(2)}, u32[]{:S(2)}) collective-permute-start(bf16[128,512]{1,0:T(8,128)(2,1)S(1)} %fusion.8), channel_id=1, source_target_pairs={{0,8},{1,9},{2,10},{3,11},{4,12},{5,13},{6,14},{7,15},{8,0},{9,1},... | collective-permute-start | bytes 393224 | tf_op jit(solution)/shard_map/ppermute | solution.py:46
  56.8 5.8 %collective-permute-start.12 = (bf16[96,512]{1,0:T(8,128)(2,1)S(1)}, bf16[96,512]{1,0:T(8,128)(2,1)S(1)}, u32[]{:S(2)}, u32[]{:S(2)}) collective-permute-start(bf16[96,512]{1,0:T(8,128)(2,1)S(1)} %fusion.10), channel_id=1, source_target_pairs={{0,4},{1,3},{2,6},{3,1},{4,0},{5,7},{6,2},{7,5},{8,12},{9,11},{10,... | collective-permute-start | bytes 294920 | tf_op jit(solution)/shard_map/ppermute | solution.py:46
  59.5 11.4 %collective-permute-start.15 = (bf16[128,512]{1,0:T(8,128)(2,1)S(1)}, bf16[128,512]{1,0:T(8,128)(2,1)S(1)}, u32[]{:S(2)}, u32[]{:S(2)}) collective-permute-start(bf16[128,512]{1,0:T(8,128)(2,1)S(1)} %fusion.5), channel_id=1, source_target_pairs={{0,16},{1,17},{2,18},{3,19},{4,20},{5,21},{6,22},{7,23},{8,24},{9,... | collective-permute-start | bytes 393224 | tf_op jit(solution)/shard_map/ppermute | solution.py:46
  62.6 10.4 %collective-permute-start.14 = (bf16[96,512]{1,0:T(8,128)(2,1)S(1)}, bf16[96,512]{1,0:T(8,128)(2,1)S(1)}, u32[]{:S(2)}, u32[]{:S(2)}) collective-permute-start(bf16[96,512]{1,0:T(8,128)(2,1)S(1)} %fusion.7), channel_id=1, source_target_pairs={{0,16},{1,17},{2,18},{3,19},{4,20},{5,21},{6,22},{7,23},{8,24},{9,... | collective-permute-start | bytes 294920 | tf_op jit(solution)/shard_map/ppermute | solution.py:46
  64.5 14.5 %collective-permute-start.22 = (bf16[96,512]{1,0:T(8,128)(2,1)S(1)}, bf16[96,512]{1,0:T(8,128)(2,1)S(1)}, u32[]{:S(2)}, u32[]{:S(2)}) collective-permute-start(bf16[96,512]{1,0:T(8,128)(2,1)S(1)} %get-tuple-element.126), channel_id=1, source_target_pairs={{0,4},{1,5},{2,6},{3,7},{4,0},{5,1},{6,2},{7,3},{8,12},{9,13},{10,... | collective-permute-start | bytes 294920 | tf_op jit(solution)/shard_map/ppermute | solution.py:436
  66.1 13.0 %collective-permute-start.23 = (bf16[96,512]{1,0:T(8,128)(2,1)S(1)}, bf16[96,512]{1,0:T(8,128)(2,1)S(1)}, u32[]{:S(2)}, u32[]{:S(2)}) collective-permute-start(bf16[96,512]{1,0:T(8,128)(2,1)S(1)} %get-tuple-element.125), channel_id=1, source_target_pairs={{0,2},{1,3},{2,0},{3,1},{4,8},{5,9},{6,10},{7,11},{8,4},{9,5},{10,... | collective-permute-start | bytes 294920 | tf_op jit(solution)/shard_map/ppermute | solution.py:437
  71.0 5.7 %collective-permute-start.19 = (bf16[1,128,512]{2,1,0:T(8,128)(2,1)S(1)}, bf16[1,128,512]{2,1,0:T(8,128)(2,1)S(1)}, u32[]{:S(2)}, u32[]{:S(2)}) collective-permute-start(bf16[1,128,512]{2,1,0:T(8,128)(2,1)S(1)} %fusion.9), channel_id=1, source_target_pairs={{0,8},{1,9},{2,10},{3,11},{4,12},{5,13},{6,14},{7,15},{8,0},{9,1},... | collective-permute-start | bytes 393224 | tf_op jit(solution)/shard_map/ppermute | solution.py:46
  73.1 6.0 %collective-permute-start.18 = (bf16[1,96,512]{2,1,0:T(8,128)(2,1)S(1)}, bf16[1,96,512]{2,1,0:T(8,128)(2,1)S(1)}, u32[]{:S(2)}, u32[]{:S(2)}) collective-permute-start(bf16[1,96,512]{2,1,0:T(8,128)(2,1)S(1)} %fusion.11), channel_id=1, source_target_pairs={{0,4},{1,3},{2,6},{3,1},{4,0},{5,7},{6,2},{7,5},{8,12},{9,11},{10,... | collective-permute-start | bytes 294920 | tf_op jit(solution)/shard_map/ppermute | solution.py:46
  76.7 6.6 %collective-permute-start.21 = (bf16[2,128,512]{2,1,0:T(8,128)(2,1)S(1)}, bf16[2,128,512]{2,1,0:T(8,128)(2,1)S(1)}, u32[]{:S(2)}, u32[]{:S(2)}) collective-permute-start(bf16[2,128,512]{2,1,0:T(8,128)(2,1)S(1)} %pad_maximum_fusion.4), channel_id=1, source_target_pairs={{0,4},{1,3},{2,6},{3,1},{4,0},{5,7},{6,2},{7,5},{8,12},{9,11},{10,... | collective-permute-start | bytes 786440 | tf_op jit(solution)/shard_map/ppermute | solution.py:46
  79.1 6.3 %collective-permute-start.20 = (bf16[2,96,512]{2,1,0:T(8,128)(2,1)S(1)}, bf16[2,96,512]{2,1,0:T(8,128)(2,1)S(1)}, u32[]{:S(2)}, u32[]{:S(2)}) collective-permute-start(bf16[2,96,512]{2,1,0:T(8,128)(2,1)S(1)} %pad_maximum_fusion.5), channel_id=1, source_target_pairs={{0,8},{1,9},{2,10},{3,11},{4,12},{5,13},{6,14},{7,15},{8,0},{9,1},... | collective-permute-start | bytes 589832 | tf_op jit(solution)/shard_map/ppermute | solution.py:46
  83.5 9.2 %collective-permute-start.25 = (bf16[4,128,512]{2,1,0:T(8,128)(2,1)S(1)}, bf16[4,128,512]{2,1,0:T(8,128)(2,1)S(1)}, u32[]{:S(2)}, u32[]{:S(2)}) collective-permute-start(bf16[4,128,512]{2,1,0:T(8,128)(2,1)S(1)} %pad_maximum_fusion.2), channel_id=1, source_target_pairs={{0,2},{1,5},{2,0},{3,7},{4,6},{5,1},{6,4},{7,3},{8,10},{9,13},{10,... | collective-permute-start | bytes 1572872 | tf_op jit(solution)/shard_map/ppermute | solution.py:46
  85.5 7.5 %copy-start.7 = (bf16[10,96,512]{2,1,0:T(8,128)(2,1)S(1)}, bf16[10,96,512]{2,1,0:T(8,128)(2,1)}, u32[]{:S(2)}) copy-start(bf16[10,96,512]{2,1,0:T(8,128)(2,1)} %get-tuple-element.92) | copy-start | bytes 2949124
  85.5 11.4 %collective-permute-start.24 = (bf16[4,96,512]{2,1,0:T(8,128)(2,1)S(1)}, bf16[4,96,512]{2,1,0:T(8,128)(2,1)S(1)}, u32[]{:S(2)}, u32[]{:S(2)}) collective-permute-start(bf16[4,96,512]{2,1,0:T(8,128)(2,1)S(1)} %pad_maximum_fusion.3), channel_id=1, source_target_pairs={{0,2},{1,5},{2,0},{3,7},{4,6},{5,1},{6,4},{7,3},{8,10},{9,13},{10,... | collective-permute-start | bytes 1179656 | tf_op jit(solution)/shard_map/ppermute | solution.py:46
  92.9 4.5 %collective-permute-start.26 = (bf16[8,128,512]{2,1,0:T(8,128)(2,1)S(1)}, bf16[8,128,512]{2,1,0:T(8,128)(2,1)S(1)}, u32[]{:S(2)}, u32[]{:S(2)}) collective-permute-start(bf16[8,128,512]{2,1,0:T(8,128)(2,1)S(1)} %pad_maximum_fusion), channel_id=1, source_target_pairs={{0,1},{1,0},{2,3},{3,2},{4,5},{5,4},{6,7},{7,6},{8,9},{9,8},{10,11... | collective-permute-start | bytes 3145736 | tf_op jit(solution)/shard_map/ppermute | solution.py:46
  97.1 2.5 %collective-permute-start.27 = (bf16[8,96,512]{2,1,0:T(8,128)(2,1)S(1)}, bf16[8,96,512]{2,1,0:T(8,128)(2,1)}, u32[]{:S(2)}, u32[]{:S(2)}) collective-permute-start(bf16[8,96,512]{2,1,0:T(8,128)(2,1)S(1)} %pad_maximum_fusion.1), channel_id=1, source_target_pairs={{0,1},{1,0},{2,3},{3,2},{4,5},{5,4},{6,7},{7,6},{8,9},{9,8},{10,11... | collective-permute-start | bytes 2359304 | tf_op jit(solution)/shard_map/ppermute | solution.py:46
  (12 other events, 16.0 us)
